TPU v7x, 128 devices: a whole 4x4x4 slice. The times are simulated.
128 devices in a mesh: corpus: 32 (over z, x, core), query: 4 (over y).
Axes of the slice: x: 4, y: 4, z: 4, core: 2. Of those that a mesh axis runs over, the one named last changes fastest.
Arguments:
- queries: bfloat16 [16384, 4096], P(('corpus', 'query')), may hold values from -6 to 6
- corpus: bfloat16 [65536, 4096], P(('corpus', 'query')), may hold values from -6 to 6
- shortlist: int32 [1024, 8], P(('corpus', 'query')), may hold values from 0 to 511, as said below
Outputs:
- coarse: float32 [512, 16384], P(('corpus', 'query'))
- rescored: bfloat16 [16384, 1024], P(('corpus', 'query'))
Inputs may be any that keep to these rules, and one draw needn't show every extreme that they name: `shortlist`: the 8 blocks of one group differ. Block b lies with the rows of device b // 4; the 8 groups of one device name at most 1 block of any one device, and in every draw one device has exactly 1 of its blocks named by the groups of every device.
All inputs are finite; a program needn't handle non-finite values.
Results may differ from a plain program's by a relative error of at most 0.001.
Values may be sent and summed in bfloat16 or wider, within the bound.
No kernel may reach another device: no remote copies, remote signals or barrier semaphores. Data moves between devices by JAX's collectives and lax.ppermute only.
A program may use at most 128 MiB of HBM per device.

v0:
```python
import jax
import jax.numpy as jnp
from jax import lax
from jax.sharding import PartitionSpec as P

D = 4096
PREFIX = 256
BLOCK = 128
GROUP = 16
SHORT = 8
MOST = 1


def body(queries, corpus, shortlist):
    local_blocks = corpus.shape[0] // BLOCK
    head_scale = PREFIX ** (-0.5)
    full_scale = D ** (-0.5)
    corpus_heads = corpus[:, :PREFIX]
    piece = lax.all_gather(queries[:, :PREFIX], ("corpus", "query"), axis=0, tiled=True)
    scores = (
        jnp.einsum("qd,pd->qp", piece, corpus_heads, preferred_element_type=jnp.float32)
        * head_scale
    )
    best = jnp.max(scores.reshape(piece.shape[0], local_blocks, BLOCK), axis=2)
    coarse = best.T
    n_corpus = lax.axis_size("corpus")
    n_query = lax.axis_size("query")
    n_all = n_corpus * n_query
    wanted = shortlist.reshape(-1)
    count = wanted.shape[0]
    holder = wanted // local_blocks
    local = wanted % local_blocks
    order_ids = jnp.arange(count, dtype=jnp.int32)
    earlier = (holder[:, None] == holder[None, :]) & (order_ids[:, None] > order_ids[None, :])
    rank = jnp.sum(earlier.astype(jnp.int32), axis=1)
    slot = holder * MOST + rank
    members = queries.reshape(-1, GROUP, D)[order_ids // SHORT]
    payload = jnp.zeros((n_all * MOST, GROUP, D), jnp.bfloat16).at[slot].set(members)
    tag_rows = jnp.zeros((n_all * MOST,), jnp.int32).at[slot].set(local)
    payload = payload.reshape(n_all, MOST, GROUP, D)
    tag_rows = tag_rows.reshape(n_all, MOST)
    asked = lax.all_to_all(payload, ("corpus", "query"), split_axis=0, concat_axis=0, tiled=True)
    lead = asked.shape[:-2]
    flat_rows = asked.reshape(-1, D)
    scores = (
        jnp.einsum("rd,pd->rp", flat_rows, corpus, preferred_element_type=jnp.float32) * full_scale
    )
    scores = scores.reshape(lead + (GROUP, local_blocks, BLOCK))
    pick = lax.all_to_all(tag_rows, ("corpus", "query"), split_axis=0, concat_axis=0, tiled=True)[
        ..., None
    ] == jnp.arange(local_blocks, dtype=jnp.int32)
    chosen = jnp.sum(jnp.where(pick[..., None, :, None], scores, 0.0), axis=-2)
    answers = chosen.astype(jnp.bfloat16)
    returned = lax.all_to_all(answers, ("corpus", "query"), split_axis=0, concat_axis=0, tiled=True)
    returned = returned.reshape(n_all * MOST, GROUP, BLOCK)[slot]
    returned = returned.reshape(-1, SHORT, GROUP, BLOCK).transpose(0, 2, 1, 3)
    rescored = returned.reshape(-1, SHORT * BLOCK)
    return (coarse, rescored)


def solution(mesh):
    return jax.shard_map(
        body,
        mesh=mesh,
        in_specs=(
            P(("corpus", "query"), None),
            P(("corpus", "query"), None),
            P(("corpus", "query"), None),
        ),
        out_specs=(P(("corpus", "query"), None), P(("corpus", "query"), None)),
        check_vma=False,
    )
```

profile of v0, /device:TPU:1, one launch (start us, length us, event | category | flops | bytes accessed | tf_op | source)
XLA Modules:
  0.0 336.9 jit_solution(10940141057854764172)
XLA Ops:
  7.2 0.8 reshape.254
  7.9 0.8 reshape.253
  8.7 0.2 convert_reduce_fusion
  8.9 0.8 scatter_custom_fusion
  9.7 0.7 copy.10
  10.4 11.5 %all-to-all-start = ((s32[128,1,1]{2,1,0:T(1,128)}), s32[128,1,1]{2,1,0:T(1,128)S(1)}, u32[]{:S(2)}, u32[]{:S(2)}) async-start(s32[128,1,1]{2,1,0:T(1,128)} %copy.10), calls=%async_computation | async-start | bytes 131072 | tf_op jit(solution)/shard_map/all_to_all | solution.py:49
  22.0 6.8 %gather_fusion = bf16[64,16,4096]{2,1,0:T(8,128)(2,1)} fusion(bf16[8,16,4096]{2,1,0:T(8,128)(2,1)} %bitcast.31, s32[1024]{0:T(1024)S(1)} %pad_clamp_fusion.1), kind=kCustom, calls=%fused_computation | custom fusion | bytes 16777472 | tf_op jit(solution)/shard_map/gather | solution.py:37
  28.7 6.0 %broadcast_in_dim.14 = bf16[128,16,4096]{2,1,0:T(8,128)(2,1)} broadcast(bf16[]{:T(256)} %constant.52.clone.1), dimensions={} | broadcast | bytes 16777218 | tf_op jit(solution)/shard_map/broadcast_in_dim | solution.py:38
  34.7 22.1 %scatter_fusion = bf16[128,16,4096]{2,1,0:T(8,128)(2,1)} fusion(bf16[128,16,4096]{2,1,0:T(8,128)(2,1)} %broadcast_in_dim.14, s32[64]{0:T(128)S(1)} %fusion.3, bf16[64,16,4096]{2,1,0:T(8,128)(2,1)} %gather_fusion), kind=kCustom, calls=%fused_computation.3 | custom fusion | bytes 25166080 | tf_op jit(solution)/shard_map/scatter | solution.py:38
  56.8 0.0 all-to-all-done
  56.8 10.2 %all-to-all-start.1 = ((bf16[128,1,16,4096]{3,2,1,0:T(8,128)(2,1)}), bf16[128,1,16,4096]{3,2,1,0:T(8,128)(2,1)}, u32[]{:S(2)}, u32[]{:S(2)}) async-start(bf16[128,1,16,4096]{3,2,1,0:T(8,128)(2,1)} %bitcast.30), calls=%async_computation.1 | async-start | bytes 33554432 | tf_op jit(solution)/shard_map/all_to_all | solution.py:42
  67.1 0.2 all-gather.2.cloned.1.call-start
  67.3 1.5 slice.6
  68.8 0.0 all-gather.2.cloned.1.call-update
  68.8 2.4 reduce.1
  71.2 0.1 iota_compare_fusion
  71.3 207.2 %all-to-all-done.1 = bf16[128,1,16,4096]{3,2,1,0:T(8,128)(2,1)} async-done(((bf16[128,1,16,4096]{3,2,1,0:T(8,128)(2,1)}), bf16[128,1,16,4096]{3,2,1,0:T(8,128)(2,1)}, u32[]{:S(2)}, u32[]{:S(2)}) %all-to-all-start.1) | async-done | bytes 16777248 | tf_op jit(solution)/shard_map/all_to_all | solution.py:42
  278.4 15.3 %convolution_multiply_fusion.1 = f32[2048,512]{1,0:T(8,128)} fusion(bf16[2048,4096]{1,0:T(8,128)(2,1)} %bitcast.8, bf16[512,4096]{1,0:T(8,128)(2,1)} %param.4), kind=kOutput, calls=%fused_computation.7 | convolution fusion | flops 8590983168 | bytes 25165824 | tf_op jit(solution)/shard_map/rd,pd->rp/dot_general | solution.py:46
  293.7 5.2 %reshape.258 = f32[128,1,16,4,128]{4,3,2,0,1:T(4,128)} reshape(f32[2048,512]{1,0:T(8,128)} %convolution_multiply_fusion.1) | data formatting | bytes 8388608 | tf_op jit(solution)/shard_map/reshape | solution.py:48
  299.0 6.4 %select_reduce_fusion = bf16[128,16,128]{2,1,0:T(8,128)(2,1)} fusion(f32[128,1,16,4,128]{4,3,2,0,1:T(4,128)} %reshape.258, pred[128,4]{1,0:T(8,128)(4,1)S(1)} %iota_compare_fusion), kind=kLoop, calls=%fused_computation.6 | loop fusion | flops 1835008 | bytes 4719104 | tf_op jit(solution)/shard_map/reduce_sum | solution.py:52
  305.3 9.5 %all-to-all-start.2 = ((bf16[128,1,16,128]{3,2,1,0:T(8,128)(2,1)}), bf16[128,1,16,128]{3,2,1,0:T(8,128)(2,1)S(1)}, u32[]{:S(2)}, u32[]{:S(2)}) async-start(bf16[128,1,16,128]{3,2,1,0:T(8,128)(2,1)} %bitcast.25), calls=%async_computation.2 | async-start | bytes 1048576 | tf_op jit(solution)/shard_map/all_to_all | solution.py:54
  314.8 0.0 all-gather.2.cloned.1.call-done
  314.9 8.7 %bitcast_reduce_fusion = f32[16384,4]{0,1:T(4,128)} fusion(bf16[16384,256]{1,0:T(8,128)(2,1)} %all-gather.2.cloned.1.call-done, bf16[512,4096]{1,0:T(8,128)(2,1)} %param.4), kind=kOutput, calls=%fused_computation.4 | convolution fusion | flops 4311678976 | bytes 8912896 | tf_op jit(solution)/shard_map/qd,pd->qp/dot_general | solution.py:21
  323.6 5.0 %all-to-all-done.2 = bf16[128,1,16,128]{3,2,1,0:T(8,128)(2,1)S(1)} async-done(((bf16[128,1,16,128]{3,2,1,0:T(8,128)(2,1)}), bf16[128,1,16,128]{3,2,1,0:T(8,128)(2,1)S(1)}, u32[]{:S(2)}, u32[]{:S(2)}) %all-to-all-start.2) | async-done | bytes 524320 | tf_op jit(solution)/shard_map/all_to_all | solution.py:54
  328.6 0.6 gather_fusion.1
  329.2 0.1 copy.11
  329.3 0.8 copy.14
  (5 shorter events, 0.0 us)
Async XLA Ops:
  10.4 46.4 %all-to-all-start = ((s32[128,1,1]{2,1,0:T(1,128)}), s32[128,1,1]{2,1,0:T(1,128)S(1)}, u32[]{:S(2)}, u32[]{:S(2)}) async-start(s32[128,1,1]{2,1,0:T(1,128)} %copy.10), calls=%async_computation | async-start | bytes 131072 | tf_op jit(solution)/shard_map/all_to_all | solution.py:49
  56.8 221.6 %all-to-all-start.1 = ((bf16[128,1,16,4096]{3,2,1,0:T(8,128)(2,1)}), bf16[128,1,16,4096]{3,2,1,0:T(8,128)(2,1)}, u32[]{:S(2)}, u32[]{:S(2)}) async-start(bf16[128,1,16,4096]{3,2,1,0:T(8,128)(2,1)} %bitcast.30), calls=%async_computation.1 | async-start | bytes 33554432 | tf_op jit(solution)/shard_map/all_to_all | solution.py:42
  67.1 247.8 %all-gather.2.cloned.1.call-start = ((), (), s32[]{:S(2)}) async-start(), calls=%async_computation.3 | async-start | bytes 8454144 | tf_op jit(solution)/shard_map/all_gather | solution.py:19
  305.3 23.2 %all-to-all-start.2 = ((bf16[128,1,16,128]{3,2,1,0:T(8,128)(2,1)}), bf16[128,1,16,128]{3,2,1,0:T(8,128)(2,1)S(1)}, u32[]{:S(2)}, u32[]{:S(2)}) async-start(bf16[128,1,16,128]{3,2,1,0:T(8,128)(2,1)} %bitcast.25), calls=%async_computation.2 | async-start | bytes 1048576 | tf_op jit(solution)/shard_map/all_to_all | solution.py:54
Sparse Core Ops, SparseCore 0:
  71.6 224.1 all-gather.1
where the time goes:
time: 338 us; the launch traced here: 337 us
  waiting for transfers between devices  212 us (63%)
  local copies, waits for them, and re-layouts  46.1 us (14%)
  starting transfers between devices  31.4 us (9%)
  matrix products  24 us (7%)
  between operations  14.1 us (4%)
  other arithmetic  9.02 us (3%)
    all_to_all x1, waiting for transfers between devices, body(): lax.all_to_all(payload, ('corpus', 'query'), split_axis=0, concat_axis=0,...  207 us
    scatter x1, local copies, waits for them, and re-layouts, body(): jnp.zeros((n_all * MOST, GROUP, D), jnp.bfloat16).at[slot].set(members)  22.1 us
    dot_general x1, matrix products, body(): jnp.einsum('rd,pd->rp', flat_rows, corpus, preferred_element_type=jnp.flo...  15.3 us
    all_to_all x1, starting transfers between devices, body(): lax.all_to_all(tag_rows, ('corpus', 'query'), split_axis=0, concat_axis=0...  11.5 us
    all_to_all x1, starting transfers between devices, body(): lax.all_to_all(payload, ('corpus', 'query'), split_axis=0, concat_axis=0,...  10.2 us
    all_to_all x1, starting transfers between devices, body(): lax.all_to_all(answers, ('corpus', 'query'), split_axis=0, concat_axis=0,...  9.48 us
    dot_general x1, matrix products, body(): jnp.einsum('qd,pd->qp', piece, corpus_heads, preferred_element_type=jnp.f...  8.74 us
    gather x1, local copies, waits for them, and re-layouts, body(): members = queries.reshape(-1, GROUP, D)[order_ids // SHORT]  6.76 us
  transfers between devices with their start and end apart: 4, of which 2 were waited for; matrix products, arithmetic and copies ran while one was open for 22% of the time, Pallas kernels for 0%

commit v1 on v0

v1 whole, which is shorter than its diff:
```python
import functools

import jax
import jax.numpy as jnp
from jax import lax
from jax.experimental import pallas as pl
from jax.experimental.pallas import tpu as pltpu
from jax.sharding import PartitionSpec as P

D = 4096
PREFIX = 256
BLOCK = 128
GROUP = 16
SHORT = 8
BATCH = 8


def rescore_kernel(chunks, n_src, n_rel, scale, tab, q_ref, *refs):
    n_blocks = len(chunks) * n_rel
    blocks = refs[:n_blocks]
    prev, out, qbuf, slots, first, sems = refs[n_blocks:]
    blk_dev = 4

    if prev is not None:
        out[...] = prev[...]

    def row_copy(slot, src_row, pos):
        return pltpu.make_async_copy(
            q_ref.at[pl.ds(pl.multiple_of(src_row, GROUP), GROUP)],
            qbuf.at[pl.ds(pl.multiple_of(pos * GROUP, GROUP), GROUP)],
            sems.at[pos],
        )

    count = jnp.int32(0)
    for c, local in enumerate(chunks):
        for r in range(n_rel):
            first[c * n_rel + r] = count

            def scan(i, n):
                slot = i * n_rel + r
                v = tab[slot] - 1
                hit = (v >= 0) & (v % blk_dev == local)

                @pl.when(hit)
                def _():
                    slots[n] = slot
                    row_copy(slot, i * (8 * GROUP) + (v // blk_dev) * GROUP, n).start()

                return n + hit.astype(jnp.int32)

            count = lax.fori_loop(0, n_src, scan, count)
    first[n_blocks] = count

    def wait(n, _):
        row_copy(0, 0, n).wait()
        return 0

    lax.fori_loop(0, count, wait, 0)

    for b in range(n_blocks):
        start, end = first[b], first[b + 1]

        def step(t, _, start=start, end=end, block=blocks[b]):
            at = start + t * BATCH
            rows = qbuf[pl.ds(pl.multiple_of(at * GROUP, GROUP), BATCH * GROUP), :]
            s = lax.dot_general(
                rows, block[...], (((1,), (1,)), ((), ())), preferred_element_type=jnp.float32
            )
            s = (s * scale).astype(out.dtype)
            for m in range(BATCH):

                @pl.when(at + m < end)
                def _():
                    out[slots[at + m]] = s[m * GROUP : (m + 1) * GROUP]

            return 0

        lax.fori_loop(0, (end - start + BATCH - 1) // BATCH, step, 0)


def rescore(chunks, tab, q, blocks, prev, scale):
    n_slots = tab.shape[0]
    n_src = q.shape[0] // BLOCK
    n_rel = n_slots // n_src
    body = functools.partial(rescore_kernel, chunks, n_src, n_rel, scale)
    if prev is None:
        kernel = lambda tab, q, *refs: body(tab, q, *refs[: len(blocks)], None, *refs[len(blocks) :])
    else:
        kernel = body
    vmem = pl.BlockSpec(memory_space=pltpu.VMEM)
    extra = [] if prev is None else [prev]
    return pl.pallas_call(
        kernel,
        out_shape=jax.ShapeDtypeStruct((n_slots, GROUP, BLOCK), jnp.bfloat16),
        in_specs=[pl.BlockSpec(memory_space=pltpu.SMEM), pl.BlockSpec(memory_space=pl.ANY)]
        + [vmem] * (len(blocks) + len(extra)),
        out_specs=vmem,
        scratch_shapes=[
            pltpu.VMEM(((n_slots + BATCH) * GROUP, D), jnp.bfloat16),
            pltpu.SMEM((n_slots,), jnp.int32),
            pltpu.SMEM((len(blocks) + 1,), jnp.int32),
            pltpu.SemaphoreType.DMA((n_slots,)),
        ],
        compiler_params=pltpu.CompilerParams(vmem_limit_bytes=40 * 2**20),
        cost_estimate=pl.CostEstimate(
            flops=2 * 16 * len(chunks) * GROUP * BLOCK * D, bytes_accessed=16 * len(chunks) * GROUP * D * 2, transcendentals=0
        ),
    )(tab, q, *blocks, *extra)


def body(queries, corpus, shortlist):
    head_scale = PREFIX ** (-0.5)
    full_scale = D ** (-0.5)
    n_corpus = lax.axis_size("corpus")
    n_query = lax.axis_size("query")
    blk_dev = corpus.shape[0] // BLOCK
    j = lax.axis_index("query")

    def along(a, d):
        return lax.ppermute(a, "query", [(t, (t + d) % n_query) for t in range(n_query)])

    wanted = shortlist.reshape(-1)
    holder = wanted // blk_dev
    slot = (holder // n_query) * n_query + (holder - j) % n_query
    value = (jnp.arange(wanted.shape[0], dtype=jnp.int32) // SHORT) * blk_dev + wanted % blk_dev + 1
    ids = jnp.arange(n_corpus * n_query, dtype=jnp.int32)
    tags = jnp.max(jnp.where(slot[None, :] == ids[:, None], value[None, :], 0), axis=1)
    tab = lax.all_to_all(
        tags.reshape(n_corpus, n_query), "corpus", split_axis=0, concat_axis=0, tiled=True
    ).reshape(-1)

    q = lax.all_gather(queries, "corpus", axis=0, tiled=True)

    pieces = []
    for l in range(blk_dev):
        own = corpus[l * BLOCK : (l + 1) * BLOCK]
        before = along(own, 1)
        after = along(own, -1)
        across = along(before, 1) if l % 2 == 0 else along(after, -1)
        pieces.append([own, after, across, before])

    heads = q[:, :PREFIX]
    best = []
    for l in range(blk_dev):
        ch = jnp.concatenate([p[:, :PREFIX] for p in pieces[l]], axis=0)
        s = jnp.einsum("qd,pd->qp", heads, ch, preferred_element_type=jnp.float32) * head_scale
        best.append(jnp.max(s.reshape(heads.shape[0], n_query, BLOCK), axis=2).T)
    best = jnp.stack(best, axis=1)
    back = jnp.stack([best[0], along(best[1], 1), along(best[2], 2), along(best[3], -1)])
    back = back.reshape(n_query, blk_dev, n_corpus, BLOCK)
    coarse = jnp.stack(
        [lax.dynamic_index_in_dim(back, (j - t) % n_query, 0, keepdims=False) for t in range(n_query)], axis=2
    ).reshape(blk_dev, -1)

    flat = [b for l in range(blk_dev - 1) for b in pieces[l]]
    answers = rescore(tuple(range(blk_dev - 1)), tab, q, flat, None, full_scale)
    answers = rescore((blk_dev - 1,), tab, q, pieces[blk_dev - 1], answers, full_scale)
    returned = lax.all_to_all(
        answers.reshape(n_corpus, n_query, GROUP, BLOCK), "corpus", split_axis=0, concat_axis=0, tiled=True
    )
    returned = returned.reshape(n_corpus * n_query, GROUP, BLOCK)[slot]
    rescored = returned.reshape(-1, SHORT, GROUP, BLOCK).transpose(0, 2, 1, 3).reshape(-1, SHORT * BLOCK)
    return (coarse, rescored)


def solution(mesh):
    spec = P(("corpus", "query"), None)
    return jax.shard_map(
        body, mesh=mesh, in_specs=(spec, spec, spec), out_specs=(spec, spec), check_vma=False
    )
```

time: 338 us -> 224 us (0.66)
  waiting for transfers between devices: 212 us -> 109 us
  local copies, waits for them, and re-layouts: 46.1 us -> 21.1 us
  Pallas kernels: 0 us -> 23.3 us
  matrix products: 24 us -> 12 us
  starting transfers between devices: 31.4 us -> 42.1 us
  other arithmetic: 9.02 us -> 1.34 us
    all_to_all x3 -> x2, waiting for transfers between devices: 212 us -> 7.01 us  [the longest x1 5.03 us: body(): lax.all_to_all(tags.reshape(n_corpus, n_query), 'corpus', split_axis=0, c...]
    ppermute x0 -> x15, waiting for transfers between devices: none -> 101 us  [along(): lax.ppermute(a, 'query', [(t, (t + d) % n_query) for t in range(n_query)])]
    pallas_call x0 -> x2, Pallas kernels: none -> 23.3 us  [rescore(): pl.pallas_call(kernel, out_shape=jax.ShapeDtypeStruct((n_slots, GROUP, BL...]
    scatter x2 -> x0, local copies, waits for them, and re-layouts: 22.9 us -> none  [the longest x1 22.1 us: body(): jnp.zeros((n_all * MOST, GROUP, D), jnp.bfloat16).at[slot].set(members)]
    ppermute x0 -> x15, starting transfers between devices: none -> 17.6 us  [along(): lax.ppermute(a, 'query', [(t, (t + d) % n_query) for t in range(n_query)])]
    slice x1 -> x16, local copies, waits for them, and re-layouts: 1.48 us -> 16 us  [the longest x15 13.3 us: body(): ch = jnp.concatenate([p[:, :PREFIX] for p in pieces[l]], axis=0)]
    dot_general x2 -> x4, matrix products: 24 us -> 12 us  [body(): jnp.einsum('qd,pd->qp', heads, ch, preferred_element_type=jnp.float32)]
    all_to_all x3 -> x2, starting transfers between devices: 31.2 us -> 24.4 us  [the longest x1 13.3 us: body(): lax.all_to_all(answers.reshape(n_corpus, n_query, GROUP, BLOCK), 'corpus'...]
  transfers between devices with their start and end apart: 4 -> 18, of which waited for: 2 -> 8; matrix products, arithmetic and copies ran while one was open for 22% -> 8% of each run, Pallas kernels for 0% -> 0%
where the time goes in v1:
time: 224 us; the launch traced here: 223 us
  waiting for transfers between devices  109 us (49%)
  starting transfers between devices  42.1 us (19%)
  Pallas kernels  23.3 us (10%)
  local copies, waits for them, and re-layouts  21.1 us (9%)
  between operations  14.5 us (6%)
  matrix products  12 us (5%)
    ppermute x15, waiting for transfers between devices, along(): lax.ppermute(a, 'query', [(t, (t + d) % n_query) for t in range(n_query)])  101 us
    pallas_call x2, Pallas kernels, rescore(): pl.pallas_call(kernel, out_shape=jax.ShapeDtypeStruct((n_slots, GROUP, BL...  23.3 us
    ppermute x15, starting transfers between devices, along(): lax.ppermute(a, 'query', [(t, (t + d) % n_query) for t in range(n_query)])  17.6 us
    slice x15, local copies, waits for them, and re-layouts, body(): ch = jnp.concatenate([p[:, :PREFIX] for p in pieces[l]], axis=0)  13.3 us
    all_to_all x1, starting transfers between devices, body(): lax.all_to_all(answers.reshape(n_corpus, n_query, GROUP, BLOCK), 'corpus'...  13.3 us
    dot_general x4, matrix products, body(): jnp.einsum('qd,pd->qp', heads, ch, preferred_element_type=jnp.float32)  12 us
    all_to_all x1, starting transfers between devices, body(): lax.all_to_all(tags.reshape(n_corpus, n_query), 'corpus', split_axis=0, c...  11.1 us
    all_to_all x1, waiting for transfers between devices, body(): lax.all_to_all(tags.reshape(n_corpus, n_query), 'corpus', split_axis=0, c...  5.03 us
  transfers between devices with their start and end apart: 18, of which 8 were waited for; matrix products, arithmetic and copies ran while one was open for 8% of the time, Pallas kernels for 0%

profile of v1, /device:TPU:1, one launch (start us, length us, event | category | flops | bytes accessed | tf_op | source)
XLA Modules:
  0.0 223.0 jit_solution(6428904190973942984)
XLA Ops:
  7.2 0.0 all-gather.2.cloned.1.call-start
  7.2 0.7 all-gather.2.cloned.1.call-update
  7.9 2.7 %fusion.45 = (bf16[128,4096]{1,0:T(8,128)(2,1)S(1)}, bf16[128,4096]{1,0:T(8,128)(2,1)S(1)}, bf16[128,4096]{1,0:T(8,128)(2,1)S(1)}, bf16[128,4096]{1,0:T(8,128)(2,1)S(1)}) fusion(bf16[512,4096]{1,0:T(8,128)(2,1)} %param.4), kind=kLoop, calls=%fused_computation.100 | loop fusion | bytes 8388608 | tf_op jit(solution)/shard_map/slice | solution.py:136
  10.6 2.2 collective-permute-start.1
  12.8 1.5 collective-permute-start
  14.3 0.0 collective-permute-start.7
  14.3 2.7 %collective-permute-start.6 = (bf16[128,4096]{1,0:T(8,128)(2,1)S(1)}, bf16[128,4096]{1,0:T(8,128)(2,1)S(1)}, u32[]{:S(2)}, u32[]{:S(2)}) collective-permute-start(bf16[128,4096]{1,0:T(8,128)(2,1)S(1)} %get-tuple-element.7.refs_8_), channel_id=1, source_target_pairs={{0,3},{1,0},{2,1},{3,2},{4,7},{5,4},{6,5},{7,6},{8,11},{9,8},{10,9... | collective-permute-start | bytes 3145736 | tf_op jit(solution)/shard_map/ppermute | solution.py:120
  17.0 0.0 collective-permute-start.5
  17.0 20.1 %collective-permute-done.1.refs_3_ = bf16[128,4096]{1,0:T(8,128)(2,1)} collective-permute-done((bf16[128,4096]{1,0:T(8,128)(2,1)S(1)}, bf16[128,4096]{1,0:T(8,128)(2,1)}, u32[]{:S(2)}, u32[]{:S(2)}) %collective-permute-start.1) | collective-permute-done | bytes 1048608 | tf_op jit(solution)/shard_map/ppermute | solution.py:120
  37.1 1.3 collective-permute-start.3
  38.3 0.9 copy-done
  39.3 0.0 collective-permute-done.refs_1_
  39.3 0.5 collective-permute-start.9
  39.8 19.8 %collective-permute-done.7.refs_11_ = bf16[128,4096]{1,0:T(8,128)(2,1)} collective-permute-done((bf16[128,4096]{1,0:T(8,128)(2,1)S(1)}, bf16[128,4096]{1,0:T(8,128)(2,1)}, u32[]{:S(2)}, u32[]{:S(2)}) %collective-permute-start.7) | collective-permute-done | bytes 1048608 | tf_op jit(solution)/shard_map/ppermute | solution.py:120
  59.5 0.0 collective-permute-start.11
  59.5 0.0 collective-permute-done.6.refs_9_
  59.5 1.1 collective-permute-start.2
  60.7 21.3 %collective-permute-done.5.refs_7_ = bf16[128,4096]{1,0:T(8,128)(2,1)S(1)} collective-permute-done((bf16[128,4096]{1,0:T(8,128)(2,1)S(1)}, bf16[128,4096]{1,0:T(8,128)(2,1)S(1)}, u32[]{:S(2)}, u32[]{:S(2)}) %collective-permute-start.5) | collective-permute-done | bytes 1048608 | tf_op jit(solution)/shard_map/ppermute | solution.py:120
  82.0 0.0 collective-permute-start.8
  82.0 0.0 collective-permute-done.3.refs_5_
  82.0 2.7 %collective-permute-start.4 = (bf16[128,4096]{1,0:T(8,128)(2,1)}, bf16[128,4096]{1,0:T(8,128)(2,1)}, u32[]{:S(2)}, u32[]{:S(2)}) collective-permute-start(bf16[128,4096]{1,0:T(8,128)(2,1)} %collective-permute-done.3.refs_5_), channel_id=1, source_target_pairs={{0,3},{1,0},{2,1},{3,2},{4,7},{5,4},{6,5},{7,6},{8,11},{9,8},{10,9... | collective-permute-start | bytes 3145736 | tf_op jit(solution)/shard_map/ppermute | solution.py:120
  84.7 19.3 %collective-permute-done.9.refs_1_ = bf16[128,4096]{1,0:T(8,128)(2,1)} collective-permute-done((bf16[128,4096]{1,0:T(8,128)(2,1)S(1)}, bf16[128,4096]{1,0:T(8,128)(2,1)}, u32[]{:S(2)}, u32[]{:S(2)}) %collective-permute-start.9) | collective-permute-done | bytes 1048608 | tf_op jit(solution)/shard_map/ppermute | solution.py:120
  104.0 3.0 %collective-permute-start.10 = (bf16[128,4096]{1,0:T(8,128)(2,1)}, bf16[128,4096]{1,0:T(8,128)(2,1)}, u32[]{:S(2)}, u32[]{:S(2)}) collective-permute-start(bf16[128,4096]{1,0:T(8,128)(2,1)} %collective-permute-done.9.refs_1_), channel_id=1, source_target_pairs={{0,3},{1,0},{2,1},{3,2},{4,7},{5,4},{6,5},{7,6},{8,11},{9,8},{10,9... | collective-permute-start | bytes 3145736 | tf_op jit(solution)/shard_map/ppermute | solution.py:120
  107.0 0.1 reshape.321
  107.1 0.1 select_reduce_fusion
  107.2 0.7 all_to_all.9
  107.9 11.1 %all-to-all-start = ((s32[32,1,4]{2,1,0:T(1,128)}), s32[32,1,4]{2,1,0:T(1,128)S(1)}, u32[]{:S(2)}, u32[]{:S(2)}) async-start(s32[32,1,4]{2,1,0:T(1,128)} %bitcast.19), calls=%async_computation | async-start | bytes 32768 | tf_op jit(solution)/shard_map/all_to_all | solution.py:128
  119.1 0.1 reshape.325
  119.3 1.7 fusion.44
  121.0 5.0 %all-to-all-done = s32[32,1,4]{2,1,0:T(1,128)S(1)} async-done(((s32[32,1,4]{2,1,0:T(1,128)}), s32[32,1,4]{2,1,0:T(1,128)S(1)}, u32[]{:S(2)}, u32[]{:S(2)}) %all-to-all-start) | async-done | bytes 544 | tf_op jit(solution)/shard_map/all_to_all | solution.py:128
  126.0 0.5 broadcast.361
  126.6 0.7 reduce.3
  127.2 0.1 reshape.322.tab
  127.4 0.8 slice.108
  128.2 0.8 slice.115
  129.0 0.8 slice.110
  129.9 0.8 slice.116
  130.7 1.5 slice.106
  132.2 0.0 collective-permute-done.11.refs_3_
  132.2 0.8 slice.118
  133.1 1.5 slice.107
  134.5 14.9 %collective-permute-done.8.refs_10_ = bf16[128,4096]{1,0:T(8,128)(2,1)} collective-permute-done((bf16[128,4096]{1,0:T(8,128)(2,1)}, bf16[128,4096]{1,0:T(8,128)(2,1)}, u32[]{:S(2)}, u32[]{:S(2)}) %collective-permute-start.8) | collective-permute-done | bytes 1048608 | tf_op jit(solution)/shard_map/ppermute | solution.py:120
  149.4 1.5 slice.114
  150.9 1.5 slice.111
  152.3 0.0 collective-permute-done.10.refs_2_
  152.4 1.5 slice.117
  153.9 3.1 %bitcast_reduce_fusion.3 = f32[4096,4]{0,1:T(4,128)S(1)} fusion(bf16[4096,4096]{1,0:T(8,128)(2,1)} %all-gather.2.cloned.1.call-done.q.q_ref, bf16[128,256]{1,0:T(8,128)(2,1)S(1)} %slice.108, bf16[128,256]{1,0:T(8,128)(2,1)} %slice.107, bf16[128,256]{1,0:T(8,128)(2,1)} %slice.106, bf16[128,256]{1,0:T(8,128)(2,1)} %get-tuple-element.2), kind=kOutput, calls=%fused_computation.4 | convolution fusion | flops 1078968320 | bytes 2424832 | tf_op jit(solution)/shard_map/qd,pd->qp/dot_general | solution.py:146
  157.0 0.0 copy-start.8
  157.1 2.9 %bitcast_reduce_fusion.1 = f32[4096,4]{0,1:T(4,128)S(1)} fusion(bf16[4096,4096]{1,0:T(8,128)(2,1)} %all-gather.2.cloned.1.call-done.q.q_ref, bf16[128,256]{1,0:T(8,128)(2,1)S(1)} %slice.115, bf16[128,256]{1,0:T(8,128)(2,1)S(1)} %copy-done.10, bf16[128,256]{1,0:T(8,128)(2,1)S(1)} %slice-done, bf16[128,256]{1,0:T(8,128)(2,1)S(1)} %copy-done.13), kind=kOutput, calls=%fused_computation.2 | convolution fusion | flops 1078968320 | bytes 2424832 | tf_op jit(solution)/shard_map/qd,pd->qp/dot_general | solution.py:146
  160.1 3.1 %bitcast_reduce_fusion.2 = f32[4096,4]{0,1:T(4,128)S(1)} fusion(bf16[4096,4096]{1,0:T(8,128)(2,1)} %all-gather.2.cloned.1.call-done.q.q_ref, bf16[128,256]{1,0:T(8,128)(2,1)S(1)} %slice-done.1, bf16[128,256]{1,0:T(8,128)(2,1)S(1)} %copy-done.9, bf16[128,256]{1,0:T(8,128)(2,1)S(1)} %slice.110, bf16[128,256]{1,0:T(8,128)(2,1)S(1)} %copy-done.12), kind=kOutput, calls=%fused_computation.3 | convolution fusion | flops 1078968320 | bytes 2424832 | tf_op jit(solution)/shard_map/qd,pd->qp/dot_general | solution.py:146
  163.3 2.9 %bitcast_reduce_fusion = f32[4096,4]{0,1:T(4,128)S(1)} fusion(bf16[4096,4096]{1,0:T(8,128)(2,1)} %all-gather.2.cloned.1.call-done.q.q_ref, bf16[128,256]{1,0:T(8,128)(2,1)S(1)} %slice.118, bf16[128,256]{1,0:T(8,128)(2,1)S(1)} %copy-done.8, bf16[128,256]{1,0:T(8,128)(2,1)S(1)} %slice.116, bf16[128,256]{1,0:T(8,128)(2,1)S(1)} %copy-done.11), kind=kOutput, calls=%fused_computation.1 | convolution fusion | flops 1078968320 | bytes 2424832 | tf_op jit(solution)/shard_map/qd,pd->qp/dot_general | solution.py:146
  166.2 0.2 pad_maximum_fusion
  166.6 15.5 %shard_map.50.refs_4_ = bf16[128,16,128]{2,1,0:T(8,128)(2,1)S(1)} custom-call(s32[128]{0:T(128)S(1)} %reshape.322.tab, bf16[4096,4096]{1,0:T(8,128)(2,1)} %all-gather.2.cloned.1.call-done.q.q_ref, bf16[128,4096]{1,0:T(8,128)(2,1)S(1)} %get-tuple-element.6.refs_0_, bf16[128,4096]{1,0:T(8,128)(2,1)S(1)} %copy-done.3, ...), custom_call_target="tpu_custom_call" | custom-call | flops 805306368 | bytes 6291456 | tf_op jit(solution)/shard_map/pallas_call | solution.py:92
  182.0 7.8 %shard_map.51 = bf16[128,16,128]{2,1,0:T(8,128)(2,1)} custom-call(s32[128]{0:T(128)S(1)} %reshape.322.tab, bf16[4096,4096]{1,0:T(8,128)(2,1)} %all-gather.2.cloned.1.call-done.q.q_ref, bf16[128,4096]{1,0:T(8,128)(2,1)S(1)} %get-tuple-element.9.refs_0_, bf16[128,4096]{1,0:T(8,128)(2,1)} %collective-permute-done.9.refs_1_, ...), custom_call_target="tpu_custom_call" | custom-call | flops 268435456 | bytes 2097152 | tf_op jit(solution)/shard_map/pallas_call | solution.py:92
  189.8 13.3 %all-to-all-start.1 = ((bf16[32,4,16,128]{3,2,1,0:T(8,128)(2,1)}), bf16[32,4,16,128]{3,2,1,0:T(8,128)(2,1)S(1)}, u32[]{:S(2)}, u32[]{:S(2)}) async-start(bf16[32,4,16,128]{3,2,1,0:T(8,128)(2,1)} %bitcast.20), calls=%async_computation.1 | async-start | bytes 1048576 | tf_op jit(solution)/shard_map/all_to_all | solution.py:158
  203.1 2.0 collective-permute-start.14
  205.1 0.7 collective-permute-start.12
  205.8 5.6 %collective-permute-done.12 = f32[4,4096]{1,0:T(4,128)S(1)} collective-permute-done((f32[4,4096]{1,0:T(4,128)S(1)}, f32[4,4096]{1,0:T(4,128)S(1)}, u32[]{:S(2)}, u32[]{:S(2)}) %collective-permute-start.12) | collective-permute-done | bytes 65568 | tf_op jit(solution)/shard_map/ppermute | solution.py:120
  211.6 0.2 pad_maximum_fusion.1
  211.8 0.9 reshape.320
  212.7 2.0 all-to-all-done.1
  214.7 0.6 gather_fusion
  215.3 0.1 copy.9
  215.4 0.8 copy.20
  (51 shorter events, 0.4 us)
Async XLA Ops:
  7.2 99.8 %copy-start.14 = (s32[8,8]{1,0:T(8,128)S(1)}, s32[8,8]{1,0:T(8,128)}, u32[]{:S(2)}) copy-start(s32[8,8]{1,0:T(8,128)} %param.5) | copy-start | bytes 772
  7.2 146.7 %all-gather.2.cloned.1.call-start = ((), (), s32[]{:S(2)}) async-start(), calls=%async_computation.2 | async-start | bytes 34603008 | tf_op jit(solution)/shard_map/all_gather | solution.py:132
  10.6 26.5 %collective-permute-start.1 = (bf16[128,4096]{1,0:T(8,128)(2,1)S(1)}, bf16[128,4096]{1,0:T(8,128)(2,1)}, u32[]{:S(2)}, u32[]{:S(2)}) collective-permute-start(bf16[128,4096]{1,0:T(8,128)(2,1)S(1)} %get-tuple-element.6.refs_0_), channel_id=1, source_target_pairs={{0,1},{1,2},{2,3},{3,0},{4,5},{5,6},{6,7},{7,4},{8,9},{9,10},{10,1... | collective-permute-start | bytes 3145736 | tf_op jit(solution)/shard_map/ppermute | solution.py:120
  12.8 26.5 %collective-permute-start = (bf16[128,4096]{1,0:T(8,128)(2,1)S(1)}, bf16[128,4096]{1,0:T(8,128)(2,1)S(1)}, u32[]{:S(2)}, u32[]{:S(2)}) collective-permute-start(bf16[128,4096]{1,0:T(8,128)(2,1)S(1)} %get-tuple-element.6.refs_0_), channel_id=1, source_target_pairs={{0,3},{1,0},{2,1},{3,2},{4,7},{5,4},{6,5},{7,6},{8,11},{9,8},{10,9... | collective-permute-start | bytes 3145736 | tf_op jit(solution)/shard_map/ppermute | solution.py:120
  14.3 45.2 %collective-permute-start.7 = (bf16[128,4096]{1,0:T(8,128)(2,1)S(1)}, bf16[128,4096]{1,0:T(8,128)(2,1)}, u32[]{:S(2)}, u32[]{:S(2)}) collective-permute-start(bf16[128,4096]{1,0:T(8,128)(2,1)S(1)} %get-tuple-element.7.refs_8_), channel_id=1, source_target_pairs={{0,1},{1,2},{2,3},{3,0},{4,5},{5,6},{6,7},{7,4},{8,9},{9,10},{10,1... | collective-permute-start | bytes 3145736 | tf_op jit(solution)/shard_map/ppermute | solution.py:120
  14.3 45.2 %collective-permute-start.6 = (bf16[128,4096]{1,0:T(8,128)(2,1)S(1)}, bf16[128,4096]{1,0:T(8,128)(2,1)S(1)}, u32[]{:S(2)}, u32[]{:S(2)}) collective-permute-start(bf16[128,4096]{1,0:T(8,128)(2,1)S(1)} %get-tuple-element.7.refs_8_), channel_id=1, source_target_pairs={{0,3},{1,0},{2,1},{3,2},{4,7},{5,4},{6,5},{7,6},{8,11},{9,8},{10,9... | collective-permute-start | bytes 3145736 | tf_op jit(solution)/shard_map/ppermute | solution.py:120
  17.0 65.0 %collective-permute-start.5 = (bf16[128,4096]{1,0:T(8,128)(2,1)S(1)}, bf16[128,4096]{1,0:T(8,128)(2,1)S(1)}, u32[]{:S(2)}, u32[]{:S(2)}) collective-permute-start(bf16[128,4096]{1,0:T(8,128)(2,1)S(1)} %get-tuple-element.8.refs_4_), channel_id=1, source_target_pairs={{0,1},{1,2},{2,3},{3,0},{4,5},{5,6},{6,7},{7,4},{8,9},{9,10},{10,1... | collective-permute-start | bytes 3145736 | tf_op jit(solution)/shard_map/ppermute | solution.py:120
  37.1 44.9 %collective-permute-start.3 = (bf16[128,4096]{1,0:T(8,128)(2,1)S(1)}, bf16[128,4096]{1,0:T(8,128)(2,1)}, u32[]{:S(2)}, u32[]{:S(2)}) collective-permute-start(bf16[128,4096]{1,0:T(8,128)(2,1)S(1)} %get-tuple-element.8.refs_4_), channel_id=1, source_target_pairs={{0,3},{1,0},{2,1},{3,2},{4,7},{5,4},{6,5},{7,6},{8,11},{9,8},{10,9... | collective-permute-start | bytes 3145736 | tf_op jit(solution)/shard_map/ppermute | solution.py:120
  38.3 0.9 copy-start
  39.3 64.7 %copy-start.2 = (bf16[128,4096]{1,0:T(8,128)(2,1)}, bf16[128,4096]{1,0:T(8,128)(2,1)S(1)}, u32[]{:S(2)}) copy-start(bf16[128,4096]{1,0:T(8,128)(2,1)S(1)} %collective-permute-done.refs_1_) | copy-start | bytes 3145732
  39.3 64.7 %collective-permute-start.9 = (bf16[128,4096]{1,0:T(8,128)(2,1)S(1)}, bf16[128,4096]{1,0:T(8,128)(2,1)}, u32[]{:S(2)}, u32[]{:S(2)}) collective-permute-start(bf16[128,4096]{1,0:T(8,128)(2,1)S(1)} %get-tuple-element.9.refs_0_), channel_id=1, source_target_pairs={{0,3},{1,0},{2,1},{3,2},{4,7},{5,4},{6,5},{7,6},{8,11},{9,8},{10,9... | collective-permute-start | bytes 3145736 | tf_op jit(solution)/shard_map/ppermute | solution.py:120
  59.5 72.7 %collective-permute-start.11 = (bf16[128,4096]{1,0:T(8,128)(2,1)S(1)}, bf16[128,4096]{1,0:T(8,128)(2,1)}, u32[]{:S(2)}, u32[]{:S(2)}) collective-permute-start(bf16[128,4096]{1,0:T(8,128)(2,1)S(1)} %get-tuple-element.9.refs_0_), channel_id=1, source_target_pairs={{0,1},{1,2},{2,3},{3,0},{4,5},{5,6},{6,7},{7,4},{8,9},{9,10},{10,1... | collective-permute-start | bytes 3145736 | tf_op jit(solution)/shard_map/ppermute | solution.py:120
  59.5 47.5 %copy-start.4 = (bf16[128,4096]{1,0:T(8,128)(2,1)}, bf16[128,4096]{1,0:T(8,128)(2,1)S(1)}, u32[]{:S(2)}) copy-start(bf16[128,4096]{1,0:T(8,128)(2,1)S(1)} %collective-permute-done.6.refs_9_) | copy-start | bytes 3145732
  59.5 73.5 %collective-permute-start.2 = (bf16[128,4096]{1,0:T(8,128)(2,1)}, bf16[128,4096]{1,0:T(8,128)(2,1)}, u32[]{:S(2)}, u32[]{:S(2)}) collective-permute-start(bf16[128,4096]{1,0:T(8,128)(2,1)} %collective-permute-done.1.refs_3_), channel_id=1, source_target_pairs={{0,1},{1,2},{2,3},{3,0},{4,5},{5,6},{6,7},{7,4},{8,9},{9,10},{10,1... | collective-permute-start | bytes 3145736 | tf_op jit(solution)/shard_map/ppermute | solution.py:120
  82.0 25.0 %copy-start.6 = (bf16[128,4096]{1,0:T(8,128)(2,1)}, bf16[128,4096]{1,0:T(8,128)(2,1)S(1)}, u32[]{:S(2)}) copy-start(bf16[128,4096]{1,0:T(8,128)(2,1)S(1)} %collective-permute-done.5.refs_7_) | copy-start | bytes 3145732
  82.0 67.4 %collective-permute-start.8 = (bf16[128,4096]{1,0:T(8,128)(2,1)}, bf16[128,4096]{1,0:T(8,128)(2,1)}, u32[]{:S(2)}, u32[]{:S(2)}) collective-permute-start(bf16[128,4096]{1,0:T(8,128)(2,1)} %collective-permute-done.7.refs_11_), channel_id=1, source_target_pairs={{0,1},{1,2},{2,3},{3,0},{4,5},{5,6},{6,7},{7,4},{8,9},{9,10},{10,1... | collective-permute-start | bytes 3145736 | tf_op jit(solution)/shard_map/ppermute | solution.py:120
  82.0 68.9 %collective-permute-start.4 = (bf16[128,4096]{1,0:T(8,128)(2,1)}, bf16[128,4096]{1,0:T(8,128)(2,1)}, u32[]{:S(2)}, u32[]{:S(2)}) collective-permute-start(bf16[128,4096]{1,0:T(8,128)(2,1)} %collective-permute-done.3.refs_5_), channel_id=1, source_target_pairs={{0,3},{1,0},{2,1},{3,2},{4,7},{5,4},{6,5},{7,6},{8,11},{9,8},{10,9... | collective-permute-start | bytes 3145736 | tf_op jit(solution)/shard_map/ppermute | solution.py:120
  104.0 48.3 %collective-permute-start.10 = (bf16[128,4096]{1,0:T(8,128)(2,1)}, bf16[128,4096]{1,0:T(8,128)(2,1)}, u32[]{:S(2)}, u32[]{:S(2)}) collective-permute-start(bf16[128,4096]{1,0:T(8,128)(2,1)} %collective-permute-done.9.refs_1_), channel_id=1, source_target_pairs={{0,3},{1,0},{2,1},{3,2},{4,7},{5,4},{6,5},{7,6},{8,11},{9,8},{10,9... | collective-permute-start | bytes 3145736 | tf_op jit(solution)/shard_map/ppermute | solution.py:120
  107.0 50.0 %slice-start = ((bf16[128,4096]{1,0:T(8,128)(2,1)}), bf16[128,256]{1,0:T(8,128)(2,1)S(1)}, s32[]{:S(2)}) async-start(bf16[128,4096]{1,0:T(8,128)(2,1)} %copy-done.4), calls=%async_computation.3 | async-start | bytes 131072 | tf_op jit(solution)/shard_map/slice | solution.py:145
  107.9 18.1 %all-to-all-start = ((s32[32,1,4]{2,1,0:T(1,128)}), s32[32,1,4]{2,1,0:T(1,128)S(1)}, u32[]{:S(2)}, u32[]{:S(2)}) async-start(s32[32,1,4]{2,1,0:T(1,128)} %bitcast.19), calls=%async_computation | async-start | bytes 32768 | tf_op jit(solution)/shard_map/all_to_all | solution.py:128
  153.8 3.2 %copy-start.10 = (bf16[128,256]{1,0:T(8,128)(2,1)S(1)}, bf16[128,256]{1,0:T(8,128)(2,1)}, u32[]{:S(2)}) copy-start(bf16[128,256]{1,0:T(8,128)(2,1)} %slice.114) | copy-start | bytes 196612
  153.8 3.2 %copy-start.13 = (bf16[128,256]{1,0:T(8,128)(2,1)S(1)}, bf16[128,256]{1,0:T(8,128)(2,1)}, u32[]{:S(2)}) copy-start(bf16[128,256]{1,0:T(8,128)(2,1)} %get-tuple-element.3) | copy-start | bytes 196612
  153.8 6.2 %slice-start.1 = ((bf16[128,4096]{1,0:T(8,128)(2,1)}), bf16[128,256]{1,0:T(8,128)(2,1)S(1)}, s32[]{:S(2)}) async-start(bf16[128,4096]{1,0:T(8,128)(2,1)} %copy-done.6), calls=%async_computation.4 | async-start | bytes 131072 | tf_op jit(solution)/shard_map/slice | solution.py:145
  153.8 6.2 %copy-start.9 = (bf16[128,256]{1,0:T(8,128)(2,1)S(1)}, bf16[128,256]{1,0:T(8,128)(2,1)}, u32[]{:S(2)}) copy-start(bf16[128,256]{1,0:T(8,128)(2,1)} %slice.111) | copy-start | bytes 196612
  153.8 6.2 %copy-start.12 = (bf16[128,256]{1,0:T(8,128)(2,1)S(1)}, bf16[128,256]{1,0:T(8,128)(2,1)}, u32[]{:S(2)}) copy-start(bf16[128,256]{1,0:T(8,128)(2,1)} %get-tuple-element.4) | copy-start | bytes 196612
  157.0 6.2 %copy-start.8 = (bf16[128,256]{1,0:T(8,128)(2,1)S(1)}, bf16[128,256]{1,0:T(8,128)(2,1)}, u32[]{:S(2)}) copy-start(bf16[128,256]{1,0:T(8,128)(2,1)} %slice.117) | copy-start | bytes 196612
  157.0 6.2 %copy-start.11 = (bf16[128,256]{1,0:T(8,128)(2,1)S(1)}, bf16[128,256]{1,0:T(8,128)(2,1)}, u32[]{:S(2)}) copy-start(bf16[128,256]{1,0:T(8,128)(2,1)} %get-tuple-element.5) | copy-start | bytes 196612
  160.1 6.4 %copy-start.1 = (bf16[128,4096]{1,0:T(8,128)(2,1)S(1)}, bf16[128,4096]{1,0:T(8,128)(2,1)}, u32[]{:S(2)}) copy-start(bf16[128,4096]{1,0:T(8,128)(2,1)} %copy-done) | copy-start | bytes 3145732
  160.1 6.4 %copy-start.3 = (bf16[128,4096]{1,0:T(8,128)(2,1)S(1)}, bf16[128,4096]{1,0:T(8,128)(2,1)}, u32[]{:S(2)}) copy-start(bf16[128,4096]{1,0:T(8,128)(2,1)} %copy-done.2) | copy-start | bytes 3145732
  160.1 6.4 %copy-start.5 = (bf16[128,4096]{1,0:T(8,128)(2,1)S(1)}, bf16[128,4096]{1,0:T(8,128)(2,1)}, u32[]{:S(2)}) copy-start(bf16[128,4096]{1,0:T(8,128)(2,1)} %copy-done.4) | copy-start | bytes 3145732
  160.1 6.4 %copy-start.7 = (bf16[128,4096]{1,0:T(8,128)(2,1)S(1)}, bf16[128,4096]{1,0:T(8,128)(2,1)}, u32[]{:S(2)}) copy-start(bf16[128,4096]{1,0:T(8,128)(2,1)} %copy-done.6) | copy-start | bytes 3145732
  189.8 24.8 %all-to-all-start.1 = ((bf16[32,4,16,128]{3,2,1,0:T(8,128)(2,1)}), bf16[32,4,16,128]{3,2,1,0:T(8,128)(2,1)S(1)}, u32[]{:S(2)}, u32[]{:S(2)}) async-start(bf16[32,4,16,128]{3,2,1,0:T(8,128)(2,1)} %bitcast.20), calls=%async_computation.1 | async-start | bytes 1048576 | tf_op jit(solution)/shard_map/all_to_all | solution.py:158
  203.1 8.4 %collective-permute-start.14 = (f32[4,4096]{1,0:T(4,128)S(1)}, f32[4,4096]{1,0:T(4,128)S(1)}, u32[]{:S(2)}, u32[]{:S(2)}) collective-permute-start(f32[4,4096]{1,0:T(4,128)S(1)} %get-tuple-element.14), channel_id=1, source_target_pairs={{0,3},{1,0},{2,1},{3,2},{4,7},{5,4},{6,5},{7,6},{8,11},{9,8},{10,9... | collective-permute-start | bytes 196616 | tf_op jit(solution)/shard_map/ppermute | solution.py:120
  205.1 6.3 %collective-permute-start.13 = (f32[4,4096]{1,0:T(4,128)S(1)}, f32[4,4096]{1,0:T(4,128)S(1)}, u32[]{:S(2)}, u32[]{:S(2)}) collective-permute-start(f32[4,4096]{1,0:T(4,128)S(1)} %get-tuple-element.15), channel_id=1, source_target_pairs={{0,2},{1,3},{2,0},{3,1},{4,6},{5,7},{6,4},{7,5},{8,10},{9,11},{10,... | collective-permute-start | bytes 196616 | tf_op jit(solution)/shard_map/ppermute | solution.py:120
  205.1 6.3 %collective-permute-start.12 = (f32[4,4096]{1,0:T(4,128)S(1)}, f32[4,4096]{1,0:T(4,128)S(1)}, u32[]{:S(2)}, u32[]{:S(2)}) collective-permute-start(f32[4,4096]{1,0:T(4,128)S(1)} %get-tuple-element.16), channel_id=1, source_target_pairs={{0,1},{1,2},{2,3},{3,0},{4,5},{5,6},{6,7},{7,4},{8,9},{9,10},{10,1... | collective-permute-start | bytes 196616 | tf_op jit(solution)/shard_map/ppermute | solution.py:120
Sparse Core Ops, SparseCore 0:
  10.3 117.6 all-gather.1

commit v2 on v1

v2 whole, which is shorter than its diff:
```python
import functools

import jax
import jax.numpy as jnp
from jax import lax
from jax.experimental import pallas as pl
from jax.experimental.pallas import tpu as pltpu
from jax.sharding import PartitionSpec as P

D = 4096
PREFIX = 256
BLOCK = 128
GROUP = 16
SHORT = 8
BATCH = 8
TILE = 256

SMEM = pl.BlockSpec(memory_space=pltpu.SMEM)
VMEM = pl.BlockSpec(memory_space=pltpu.VMEM)


def list_kernel(order, blk_dev, n_src, n_rel, tab, rows, slots, first):
    def clear(n, _):
        rows[n] = 0
        slots[n] = 0
        return 0

    lax.fori_loop(0, n_src * n_rel, clear, 0)
    count = jnp.int32(0)
    for b, (local, r) in enumerate(order):
        first[b] = count

        def scan(i, n, local=local, r=r):
            slot = i * n_rel + r
            v = tab[slot] - 1
            hit = (v >= 0) & (v % blk_dev == local)

            @pl.when(hit)
            def _():
                slots[n] = slot
                rows[n] = i * BLOCK + (v // blk_dev) * GROUP

            return n + hit.astype(jnp.int32)

        count = lax.fori_loop(0, n_src, scan, count)
    first[len(order)] = count


def score_kernel(b0, groups, n_prev, full_scale, head_scale, rows, slots, first, q_ref, *refs):
    n_blocks = sum(n for _, n in groups)
    blocks = refs[:n_blocks]
    prev = refs[n_blocks : n_blocks + n_prev]
    out = refs[n_blocks + n_prev]
    best = refs[n_blocks + n_prev + 1 : n_blocks + n_prev + 1 + len(groups)]
    qbuf, hbuf, cbuf, sems, hsem = refs[n_blocks + n_prev + 1 + len(groups) :]

    def row_copy(src_row, pos):
        return pltpu.make_async_copy(
            q_ref.at[pl.ds(pl.multiple_of(src_row, GROUP), GROUP)],
            qbuf.at[pl.ds(pl.multiple_of(pos * GROUP, GROUP), GROUP)],
            sems.at[pos],
        )

    heads = pltpu.make_async_copy(q_ref.at[:, pl.ds(0, PREFIX)], hbuf, hsem)
    heads.start()
    base = first[b0]
    total = first[b0 + n_blocks] - base

    def start(n, _):
        row_copy(rows[base + n], n).start()
        return 0

    lax.fori_loop(0, total, start, 0)

    for b in range(n_blocks):
        cbuf[b * BLOCK : (b + 1) * BLOCK] = blocks[b][:, :PREFIX]
    if n_prev:
        out[...] = prev[0][...]
        for ref, old in zip(best, prev[1:]):
            ref[...] = old[...]
    heads.wait()

    def coarse(t, _):
        h = hbuf[pl.ds(pl.multiple_of(t * TILE, TILE), TILE), :]
        at = 0
        for ref, (l0, n) in zip(best, groups):
            s = lax.dot_general(
                cbuf[at * BLOCK : (at + n) * BLOCK], h, (((1,), (1,)), ((), ())), preferred_element_type=jnp.float32
            )
            top = jnp.max(s.reshape(n, BLOCK, TILE), axis=1) * head_scale
            ref[l0 : l0 + n, pl.ds(pl.multiple_of(t * TILE, TILE), TILE)] = top
            at += n
        return 0

    lax.fori_loop(0, hbuf.shape[0] // TILE, coarse, 0)

    waited = jnp.int32(0)
    for b in range(n_blocks):
        lo, hi = first[b0 + b] - base, first[b0 + b + 1] - base

        def step(t, waited, lo=lo, hi=hi, block=blocks[b]):
            at = lo + t * BATCH
            upto = jnp.minimum(at + BATCH, total)

            def wait(n, _):
                row_copy(0, n).wait()
                return 0

            lax.fori_loop(waited, upto, wait, 0)
            part = qbuf[pl.ds(pl.multiple_of(at * GROUP, GROUP), BATCH * GROUP), :]
            s = lax.dot_general(part, block[...], (((1,), (1,)), ((), ())), preferred_element_type=jnp.float32)
            s = (s * full_scale).astype(out.dtype)
            for m in range(BATCH):

                @pl.when(at + m < hi)
                def _():
                    out[slots[base + at + m]] = s[m * GROUP : (m + 1) * GROUP]

            return jnp.maximum(waited, upto)

        waited = lax.fori_loop(0, (hi - lo + BATCH - 1) // BATCH, step, waited)


def score(b0, groups, lists, q, blocks, prev, blk_dev, n_slots):
    n_q = q.shape[0]
    n_blocks = len(blocks)
    kernel = functools.partial(score_kernel, b0, groups, len(prev), D ** (-0.5), PREFIX ** (-0.5))
    return pl.pallas_call(
        kernel,
        out_shape=[jax.ShapeDtypeStruct((n_slots, GROUP, BLOCK), jnp.bfloat16)]
        + [jax.ShapeDtypeStruct((blk_dev, n_q), jnp.float32)] * len(groups),
        in_specs=[SMEM] * 3 + [pl.BlockSpec(memory_space=pl.ANY)] + [VMEM] * (n_blocks + len(prev)),
        out_specs=[VMEM] * (1 + len(groups)),
        scratch_shapes=[
            pltpu.VMEM(((n_slots + BATCH) * GROUP, D), jnp.bfloat16),
            pltpu.VMEM((n_q, PREFIX), jnp.bfloat16),
            pltpu.VMEM((n_blocks * BLOCK, PREFIX), jnp.bfloat16),
            pltpu.SemaphoreType.DMA((n_slots,)),
            pltpu.SemaphoreType.DMA(()),
        ],
        compiler_params=pltpu.CompilerParams(vmem_limit_bytes=48 * 2**20),
        cost_estimate=pl.CostEstimate(
            flops=2 * n_blocks * BLOCK * (n_q * PREFIX + 4 * GROUP * D), bytes_accessed=n_blocks * 2**20, transcendentals=0
        ),
    )(*lists, q, *blocks, *prev)


def body(queries, corpus, shortlist):
    n_corpus = lax.axis_size("corpus")
    n_query = lax.axis_size("query")
    n_slots = n_corpus * n_query
    blk_dev = corpus.shape[0] // BLOCK
    j = lax.axis_index("query")

    def along(a, d):
        return lax.ppermute(a, "query", [(t, (t + d) % n_query) for t in range(n_query)])

    q = lax.all_gather(queries, "corpus", axis=0, tiled=True)

    pieces = []
    for l in range(blk_dev):
        own = corpus[l * BLOCK : (l + 1) * BLOCK]
        before = along(own, 1)
        after = along(own, -1)
        across = along(before, 1) if l % 2 == 0 else along(after, -1)
        pieces.append([own, after, across, before])

    wanted, _ = lax.optimization_barrier((shortlist.reshape(-1), pieces[0][3]))
    holder = wanted // blk_dev
    slot = (holder // n_query) * n_query + (holder - j) % n_query
    value = (jnp.arange(wanted.shape[0], dtype=jnp.int32) // SHORT) * blk_dev + wanted % blk_dev + 1
    ids = jnp.arange(n_slots, dtype=jnp.int32)
    tags = jnp.max(jnp.where(slot[None, :] == ids[:, None], value[None, :], 0), axis=1)
    tab = lax.all_to_all(
        tags.reshape(n_corpus, n_query), "corpus", split_axis=0, concat_axis=0, tiled=True
    ).reshape(-1)

    order = [(l, r) for r in (0, 1, 3, 2) for l in range(blk_dev)]
    lists = pl.pallas_call(
        functools.partial(list_kernel, order, blk_dev, n_corpus, n_query),
        out_shape=[jax.ShapeDtypeStruct((n,), jnp.int32) for n in (n_slots, n_slots, len(order) + 1)],
        in_specs=[SMEM],
        out_specs=[SMEM] * 3,
    )(tab)

    early = [pieces[l][r] for l, r in order[:-1]]
    late = [pieces[l][r] for l, r in order[-1:]]
    answers, c0, c1, c3, c2 = score(
        0, [(0, blk_dev)] * 3 + [(0, blk_dev - 1)], lists, q, early, [], blk_dev, n_slots
    )
    answers, c2 = score(len(order) - 1, [(blk_dev - 1, 1)], lists, q, late, [answers, c2], blk_dev, n_slots)

    back = jnp.stack([c0, along(c1, 1), along(c2, 2), along(c3, -1)])
    back = back.reshape(n_query, blk_dev, n_corpus, BLOCK)
    coarse = jnp.stack(
        [lax.dynamic_index_in_dim(back, (j - t) % n_query, 0, keepdims=False) for t in range(n_query)], axis=2
    ).reshape(blk_dev, -1)

    returned = lax.all_to_all(
        answers.reshape(n_corpus, n_query, GROUP, BLOCK), "corpus", split_axis=0, concat_axis=0, tiled=True
    )
    returned = returned.reshape(n_slots, GROUP, BLOCK)[slot]
    rescored = returned.reshape(-1, SHORT, GROUP, BLOCK).transpose(0, 2, 1, 3).reshape(-1, SHORT * BLOCK)
    return (coarse, rescored)


def solution(mesh):
    spec = P(("corpus", "query"), None)
    return jax.shard_map(
        body, mesh=mesh, in_specs=(spec, spec, spec), out_specs=(spec, spec), check_vma=False
    )
```

time: 224 us -> 220 us (0.982)
  Pallas kernels: 23.3 us -> 41.5 us
  matrix products: 12 us -> 0 us
  local copies, waits for them, and re-layouts: 21.1 us -> 13.4 us
  starting transfers between devices: 42.1 us -> 38.4 us
    pallas_call x2 -> x3, Pallas kernels: 23.3 us -> 41.5 us  [the longest x2 32 us: score(): pl.pallas_call(kernel, out_shape=[jax.ShapeDtypeStruct((n_slots, GROUP, B...]
    slice x15 -> x0, local copies, waits for them, and re-layouts: 13.3 us -> none  [body(): ch = jnp.concatenate([p[:, :PREFIX] for p in pieces[l]], axis=0)]
    dot_general x4 -> x0, matrix products: 12 us -> none  [body(): jnp.einsum('qd,pd->qp', heads, ch, preferred_element_type=jnp.float32)]
    unnamed x34 -> x24, local copies, waits for them, and re-layouts: 1.77 us -> 7.16 us
    all_to_all x1, starting transfers between devices: 13.3 us -> 10.6 us  [body(): lax.all_to_all(answers.reshape(n_corpus, n_query, GROUP, BLOCK), 'corpus'...]
    ppermute x15, waiting for transfers between devices: 101 us -> 98.5 us  [along(): lax.ppermute(a, 'query', [(t, (t + d) % n_query) for t in range(n_query)])]
  transfers between devices with their start and end apart: 18 -> 18, of which waited for: 8 -> 8; matrix products, arithmetic and copies ran while one was open for 8% -> 3% of each run, Pallas kernels for 0% -> 15%
where the time goes in v2:
time: 220 us; the launch traced here: 218 us
  waiting for transfers between devices  110 us (50%)
  Pallas kernels  41.5 us (19%)
  starting transfers between devices  38.4 us (17%)
  between operations  14.2 us (6%)
  local copies, waits for them, and re-layouts  13.4 us (6%)
    ppermute x15, waiting for transfers between devices, along(): lax.ppermute(a, 'query', [(t, (t + d) % n_query) for t in range(n_query)])  98.5 us
    pallas_call x2, Pallas kernels, score(): pl.pallas_call(kernel, out_shape=[jax.ShapeDtypeStruct((n_slots, GROUP, B...  32 us
    ppermute x15, starting transfers between devices, along(): lax.ppermute(a, 'query', [(t, (t + d) % n_query) for t in range(n_query)])  17.5 us
    all_to_all x1, starting transfers between devices, body(): lax.all_to_all(answers.reshape(n_corpus, n_query, GROUP, BLOCK), 'corpus'...  10.6 us
    all_to_all x1, starting transfers between devices, body(): lax.all_to_all(tags.reshape(n_corpus, n_query), 'corpus', split_axis=0, c...  10.3 us
    pallas_call x1, Pallas kernels, body(): pl.pallas_call(functools.partial(list_kernel, order, blk_dev, n_corpus, n...  9.55 us
    unnamed x24, local copies, waits for them, and re-layouts  7.16 us
    all_to_all x1, waiting for transfers between devices, body(): lax.all_to_all(tags.reshape(n_corpus, n_query), 'corpus', split_axis=0, c...  6.96 us
  transfers between devices with their start and end apart: 18, of which 8 were waited for; matrix products, arithmetic and copies ran while one was open for 3% of the time, Pallas kernels for 15%

profile of v2, /device:TPU:1, one launch (start us, length us, event | category | flops | bytes accessed | tf_op | source)
XLA Modules:
  0.0 218.4 jit_solution(4809580074138325957)
XLA Ops:
  7.2 0.0 all-gather.2.cloned.1.call-start
  7.2 0.7 all-gather.2.cloned.1.call-update
  7.9 0.0 copy-start.9
  7.9 2.7 %fusion.6 = (bf16[128,4096]{1,0:T(8,128)(2,1)S(1)}, bf16[128,4096]{1,0:T(8,128)(2,1)S(1)}, bf16[128,4096]{1,0:T(8,128)(2,1)S(1)}, bf16[128,4096]{1,0:T(8,128)(2,1)S(1)}) fusion(bf16[512,4096]{1,0:T(8,128)(2,1)} %param.4), kind=kLoop, calls=%fused_computation.36 | loop fusion | bytes 8388608 | tf_op jit(solution)/shard_map/slice | solution.py:162
  10.6 2.2 %collective-permute-start = (bf16[128,4096]{1,0:T(8,128)(2,1)S(1)}, bf16[128,4096]{1,0:T(8,128)(2,1)}, u32[]{:S(2)}, u32[]{:S(2)}) collective-permute-start(bf16[128,4096]{1,0:T(8,128)(2,1)S(1)} %get-tuple-element.28.refs_0_), channel_id=1, source_target_pairs={{0,1},{1,2},{2,3},{3,0},{4,5},{5,6},{6,7},{7,4},{8,9},{9,10},{10,1... | collective-permute-start | bytes 3145736 | tf_op jit(solution)/shard_map/ppermute | solution.py:156
  12.8 1.3 collective-permute-start.6
  14.1 1.4 collective-permute-start.2
  15.5 0.3 collective-permute-start.4
  15.8 1.4 collective-permute-start.1
  17.1 19.9 %collective-permute-done.refs_8_ = bf16[128,4096]{1,0:T(8,128)(2,1)} collective-permute-done((bf16[128,4096]{1,0:T(8,128)(2,1)S(1)}, bf16[128,4096]{1,0:T(8,128)(2,1)}, u32[]{:S(2)}, u32[]{:S(2)}) %collective-permute-start) | collective-permute-done | bytes 1048608 | tf_op jit(solution)/shard_map/ppermute | solution.py:156
  37.1 1.3 collective-permute-start.3
  38.3 0.0 copy-start
  38.3 1.0 copy-done
  39.3 20.2 %collective-permute-done.6.refs_10_ = bf16[128,4096]{1,0:T(8,128)(2,1)} collective-permute-done((bf16[128,4096]{1,0:T(8,128)(2,1)S(1)}, bf16[128,4096]{1,0:T(8,128)(2,1)}, u32[]{:S(2)}, u32[]{:S(2)}) %collective-permute-start.6) | collective-permute-done | bytes 1048608 | tf_op jit(solution)/shard_map/ppermute | solution.py:156
  59.5 0.0 collective-permute-start.5
  59.5 0.0 collective-permute-done.2.refs_5_
  59.5 1.1 collective-permute-start.7
  60.7 0.0 collective-permute-done.4.refs_7_
  60.7 1.0 collective-permute-start.8
  61.7 20.8 %collective-permute-done.1.refs_4_ = bf16[128,4096]{1,0:T(8,128)(2,1)S(1)} collective-permute-done((bf16[128,4096]{1,0:T(8,128)(2,1)S(1)}, bf16[128,4096]{1,0:T(8,128)(2,1)S(1)}, u32[]{:S(2)}, u32[]{:S(2)}) %collective-permute-start.1) | collective-permute-done | bytes 1048608 | tf_op jit(solution)/shard_map/ppermute | solution.py:156
  82.5 1.0 copy-done.2
  83.5 1.0 collective-permute-start.10
  84.5 20.5 %collective-permute-done.3.refs_6_ = bf16[128,4096]{1,0:T(8,128)(2,1)S(1)} collective-permute-done((bf16[128,4096]{1,0:T(8,128)(2,1)S(1)}, bf16[128,4096]{1,0:T(8,128)(2,1)S(1)}, u32[]{:S(2)}, u32[]{:S(2)}) %collective-permute-start.3) | collective-permute-done | bytes 1048608 | tf_op jit(solution)/shard_map/ppermute | solution.py:156
  105.0 0.0 copy-start.7
  105.0 2.6 %collective-permute-start.9 = (bf16[128,4096]{1,0:T(8,128)(2,1)}, bf16[128,4096]{1,0:T(8,128)(2,1)}, u32[]{:S(2)}, u32[]{:S(2)}) collective-permute-start(bf16[128,4096]{1,0:T(8,128)(2,1)} %collective-permute-done.2.refs_5_), channel_id=1, source_target_pairs={{0,3},{1,0},{2,1},{3,2},{4,7},{5,4},{6,5},{7,6},{8,11},{9,8},{10,9... | collective-permute-start | bytes 3145736 | tf_op jit(solution)/shard_map/ppermute | solution.py:156
  107.6 0.0 collective-permute-done.5.refs_9_
  107.6 0.0 copy-done.7
  107.6 1.0 collective-permute-start.12
  108.6 0.0 copy-done.8
  108.6 0.0 copy-done.9
  108.6 0.1 reshape.45
  108.8 0.1 select_reduce_fusion
  108.9 0.7 all_to_all.9
  109.6 10.3 %all-to-all-start = ((s32[32,1,4]{2,1,0:T(1,128)}), s32[32,1,4]{2,1,0:T(1,128)S(1)}, u32[]{:S(2)}, u32[]{:S(2)}) async-start(s32[32,1,4]{2,1,0:T(1,128)} %bitcast), calls=%async_computation | async-start | bytes 32768 | tf_op jit(solution)/shard_map/all_to_all | solution.py:174
  119.9 7.0 %all-to-all-done = s32[32,1,4]{2,1,0:T(1,128)S(1)} async-done(((s32[32,1,4]{2,1,0:T(1,128)}), s32[32,1,4]{2,1,0:T(1,128)S(1)}, u32[]{:S(2)}, u32[]{:S(2)}) %all-to-all-start) | async-done | bytes 544 | tf_op jit(solution)/shard_map/all_to_all | solution.py:174
  126.8 0.5 broadcast.59
  127.3 0.7 reduce.3
  128.0 0.6 reshape.46.tab
  128.6 9.5 %shard_map.50 = (s32[128]{0:T(128)}, s32[128]{0:T(128)}, s32[17]{0:T(128)}) custom-call(s32[128]{0:T(128)} %reshape.46.tab), custom_call_target="tpu_custom_call" | custom-call | tf_op jit(solution)/shard_map/pallas_call | solution.py:179
  138.2 0.0 collective-permute-done.7.refs_11_
  138.2 0.0 collective-permute-done.8.refs_12_
  138.2 13.3 %collective-permute-done.10.refs_14_ = bf16[128,4096]{1,0:T(8,128)(2,1)} collective-permute-done((bf16[128,4096]{1,0:T(8,128)(2,1)}, bf16[128,4096]{1,0:T(8,128)(2,1)}, u32[]{:S(2)}, u32[]{:S(2)}) %collective-permute-start.10) | collective-permute-done | bytes 1048608 | tf_op jit(solution)/shard_map/ppermute | solution.py:156
  151.5 0.0 collective-permute-done.9.refs_13_
  151.5 1.2 copy-done.1
  152.8 1.2 copy-done.3
  154.0 0.7 copy-done.4
  154.6 0.7 copy-done.5
  155.3 0.6 copy-done.6
  155.9 22.4 %shard_map.51 = (bf16[128,16,128]{2,1,0:T(8,128)(2,1)S(1)}, f32[4,4096]{1,0:T(4,128)S(1)}, f32[4,4096]{1,0:T(4,128)S(1)}, f32[4,4096]{1,0:T(4,128)S(1)}, f32[4,4096]{1,0:T(4,128)S(1)}) custom-call(s32[128]{0:T(128)S(1)} %copy-done.4, s32[128]{0:T(128)S(1)} %copy-done.5, s32[17]{0:T(128)S(1)} %copy-done.6, ...), custom_call_target="tpu_custom_call" | custom-call | flops 5033164800 | bytes 15728640 | tf_op jit(solution)/shard_map/pallas_call | solution.py:128
  178.4 0.0 collective-permute-done.12.refs_0_
  178.4 9.5 %shard_map.52 = (bf16[128,16,128]{2,1,0:T(8,128)(2,1)}, f32[4,4096]{1,0:T(4,128)S(1)}) custom-call(s32[128]{0:T(128)S(1)} %copy-done.4, s32[128]{0:T(128)S(1)} %copy-done.5, s32[17]{0:T(128)S(1)} %copy-done.6, bf16[4096,4096]{1,0:T(8,128)(2,1)} %all-gather.2.cloned.1.call-done.q_ref, bf16[128,4096]{1,0:T(8,128)(2,1)} %collective-permute-done.12.refs_0_, ...), custom_call_target="tpu_custom_call" | custom-call | flops 335544320 | bytes 1048576 | tf_op jit(solution)/shard_map/pallas_call | solution.py:128
  187.9 10.6 %all-to-all-start.1 = ((bf16[32,4,16,128]{3,2,1,0:T(8,128)(2,1)}), bf16[32,4,16,128]{3,2,1,0:T(8,128)(2,1)S(1)}, u32[]{:S(2)}, u32[]{:S(2)}) async-start(bf16[32,4,16,128]{3,2,1,0:T(8,128)(2,1)} %bitcast.5), calls=%async_computation.1 | async-start | bytes 1048576 | tf_op jit(solution)/shard_map/all_to_all | solution.py:199
  198.5 0.1 collective-permute-start.13
  198.6 0.4 collective-permute-start.11
  199.0 2.4 %collective-permute-start.14 = (f32[4,4096]{1,0:T(4,128)S(1)}, f32[4,4096]{1,0:T(4,128)S(1)}, u32[]{:S(2)}, u32[]{:S(2)}) collective-permute-start(f32[4,4096]{1,0:T(4,128)S(1)} %get-tuple-element.22), channel_id=1, source_target_pairs={{0,3},{1,0},{2,1},{3,2},{4,7},{5,4},{6,5},{7,6},{8,11},{9,8},{10,9... | collective-permute-start | bytes 196616 | tf_op jit(solution)/shard_map/ppermute | solution.py:156
  201.4 3.7 %collective-permute-done.11 = f32[4,4096]{1,0:T(4,128)S(1)} collective-permute-done((f32[4,4096]{1,0:T(4,128)S(1)}, f32[4,4096]{1,0:T(4,128)S(1)}, u32[]{:S(2)}, u32[]{:S(2)}) %collective-permute-start.11) | collective-permute-done | bytes 65568 | tf_op jit(solution)/shard_map/ppermute | solution.py:156
  205.1 0.0 collective-permute-done.13
  205.1 0.0 collective-permute-done.14
  205.2 0.2 pad_maximum_fusion
  205.5 0.9 reshape.47
  206.3 3.8 %all-to-all-done.1 = bf16[32,4,16,128]{3,2,1,0:T(8,128)(2,1)S(1)} async-done(((bf16[32,4,16,128]{3,2,1,0:T(8,128)(2,1)}), bf16[32,4,16,128]{3,2,1,0:T(8,128)(2,1)S(1)}, u32[]{:S(2)}, u32[]{:S(2)}) %all-to-all-start.1) | async-done | bytes 524320 | tf_op jit(solution)/shard_map/all_to_all | solution.py:199
  210.1 0.6 gather_fusion
  210.7 0.1 copy.9
  210.8 0.8 copy.20
  (15 shorter events, 0.1 us)
Async XLA Ops:
  7.2 144.4 %all-gather.2.cloned.1.call-start = ((), (), s32[]{:S(2)}) async-start(), calls=%async_computation.2 | async-start | bytes 34603008 | tf_op jit(solution)/shard_map/all_gather | solution.py:158
  7.9 100.7 %copy-start.9 = (s32[8,8]{1,0:T(8,128)S(1)}, s32[8,8]{1,0:T(8,128)}, u32[]{:S(2)}) copy-start(s32[8,8]{1,0:T(8,128)} %param.5) | copy-start | bytes 772
  10.6 26.5 %collective-permute-start = (bf16[128,4096]{1,0:T(8,128)(2,1)S(1)}, bf16[128,4096]{1,0:T(8,128)(2,1)}, u32[]{:S(2)}, u32[]{:S(2)}) collective-permute-start(bf16[128,4096]{1,0:T(8,128)(2,1)S(1)} %get-tuple-element.28.refs_0_), channel_id=1, source_target_pairs={{0,1},{1,2},{2,3},{3,0},{4,5},{5,6},{6,7},{7,4},{8,9},{9,10},{10,1... | collective-permute-start | bytes 3145736 | tf_op jit(solution)/shard_map/ppermute | solution.py:156
  12.8 46.8 %collective-permute-start.6 = (bf16[128,4096]{1,0:T(8,128)(2,1)S(1)}, bf16[128,4096]{1,0:T(8,128)(2,1)}, u32[]{:S(2)}, u32[]{:S(2)}) collective-permute-start(bf16[128,4096]{1,0:T(8,128)(2,1)S(1)} %get-tuple-element.29.refs_2_), channel_id=1, source_target_pairs={{0,1},{1,2},{2,3},{3,0},{4,5},{5,6},{6,7},{7,4},{8,9},{9,10},{10,1... | collective-permute-start | bytes 3145736 | tf_op jit(solution)/shard_map/ppermute | solution.py:156
  14.1 45.5 %collective-permute-start.2 = (bf16[128,4096]{1,0:T(8,128)(2,1)S(1)}, bf16[128,4096]{1,0:T(8,128)(2,1)}, u32[]{:S(2)}, u32[]{:S(2)}) collective-permute-start(bf16[128,4096]{1,0:T(8,128)(2,1)S(1)} %get-tuple-element.27.refs_1_), channel_id=1, source_target_pairs={{0,3},{1,0},{2,1},{3,2},{4,7},{5,4},{6,5},{7,6},{8,11},{9,8},{10,9... | collective-permute-start | bytes 3145736 | tf_op jit(solution)/shard_map/ppermute | solution.py:156
  15.5 45.2 %collective-permute-start.4 = (bf16[128,4096]{1,0:T(8,128)(2,1)S(1)}, bf16[128,4096]{1,0:T(8,128)(2,1)}, u32[]{:S(2)}, u32[]{:S(2)}) collective-permute-start(bf16[128,4096]{1,0:T(8,128)(2,1)S(1)} %get-tuple-element.26.refs_3_), channel_id=1, source_target_pairs={{0,3},{1,0},{2,1},{3,2},{4,7},{5,4},{6,5},{7,6},{8,11},{9,8},{10,9... | collective-permute-start | bytes 3145736 | tf_op jit(solution)/shard_map/ppermute | solution.py:156
  15.8 66.8 %collective-permute-start.1 = (bf16[128,4096]{1,0:T(8,128)(2,1)S(1)}, bf16[128,4096]{1,0:T(8,128)(2,1)S(1)}, u32[]{:S(2)}, u32[]{:S(2)}) collective-permute-start(bf16[128,4096]{1,0:T(8,128)(2,1)S(1)} %get-tuple-element.28.refs_0_), channel_id=1, source_target_pairs={{0,3},{1,0},{2,1},{3,2},{4,7},{5,4},{6,5},{7,6},{8,11},{9,8},{10,9... | collective-permute-start | bytes 3145736 | tf_op jit(solution)/shard_map/ppermute | solution.py:156
  37.1 67.9 %collective-permute-start.3 = (bf16[128,4096]{1,0:T(8,128)(2,1)S(1)}, bf16[128,4096]{1,0:T(8,128)(2,1)S(1)}, u32[]{:S(2)}, u32[]{:S(2)}) collective-permute-start(bf16[128,4096]{1,0:T(8,128)(2,1)S(1)} %get-tuple-element.29.refs_2_), channel_id=1, source_target_pairs={{0,3},{1,0},{2,1},{3,2},{4,7},{5,4},{6,5},{7,6},{8,11},{9,8},{10,9... | collective-permute-start | bytes 3145736 | tf_op jit(solution)/shard_map/ppermute | solution.py:156
  38.3 1.0 copy-start
  59.5 48.1 %collective-permute-start.5 = (bf16[128,4096]{1,0:T(8,128)(2,1)S(1)}, bf16[128,4096]{1,0:T(8,128)(2,1)S(1)}, u32[]{:S(2)}, u32[]{:S(2)}) collective-permute-start(bf16[128,4096]{1,0:T(8,128)(2,1)S(1)} %get-tuple-element.27.refs_1_), channel_id=1, source_target_pairs={{0,1},{1,2},{2,3},{3,0},{4,5},{5,6},{6,7},{7,4},{8,9},{9,10},{10,1... | collective-permute-start | bytes 3145736 | tf_op jit(solution)/shard_map/ppermute | solution.py:156
  59.5 78.7 %collective-permute-start.7 = (bf16[128,4096]{1,0:T(8,128)(2,1)S(1)}, bf16[128,4096]{1,0:T(8,128)(2,1)}, u32[]{:S(2)}, u32[]{:S(2)}) collective-permute-start(bf16[128,4096]{1,0:T(8,128)(2,1)S(1)} %get-tuple-element.26.refs_3_), channel_id=1, source_target_pairs={{0,1},{1,2},{2,3},{3,0},{4,5},{5,6},{6,7},{7,4},{8,9},{9,10},{10,1... | collective-permute-start | bytes 3145736 | tf_op jit(solution)/shard_map/ppermute | solution.py:156
  60.7 77.5 %collective-permute-start.8 = (bf16[128,4096]{1,0:T(8,128)(2,1)}, bf16[128,4096]{1,0:T(8,128)(2,1)}, u32[]{:S(2)}, u32[]{:S(2)}) collective-permute-start(bf16[128,4096]{1,0:T(8,128)(2,1)} %collective-permute-done.refs_8_), channel_id=1, source_target_pairs={{0,1},{1,2},{2,3},{3,0},{4,5},{5,6},{6,7},{7,4},{8,9},{9,10},{10,1... | collective-permute-start | bytes 3145736 | tf_op jit(solution)/shard_map/ppermute | solution.py:156
  82.5 1.0 copy-start.2
  83.5 68.0 %collective-permute-start.10 = (bf16[128,4096]{1,0:T(8,128)(2,1)}, bf16[128,4096]{1,0:T(8,128)(2,1)}, u32[]{:S(2)}, u32[]{:S(2)}) collective-permute-start(bf16[128,4096]{1,0:T(8,128)(2,1)} %collective-permute-done.6.refs_10_), channel_id=1, source_target_pairs={{0,1},{1,2},{2,3},{3,0},{4,5},{5,6},{6,7},{7,4},{8,9},{9,10},{10,1... | collective-permute-start | bytes 3145736 | tf_op jit(solution)/shard_map/ppermute | solution.py:156
  105.0 2.6 %copy-start.7 = (bf16[128,4096]{1,0:T(8,128)(2,1)}, bf16[128,4096]{1,0:T(8,128)(2,1)S(1)}, u32[]{:S(2)}) copy-start(bf16[128,4096]{1,0:T(8,128)(2,1)S(1)} %collective-permute-done.3.refs_6_) | copy-start | bytes 3145732
  105.0 46.5 %collective-permute-start.9 = (bf16[128,4096]{1,0:T(8,128)(2,1)}, bf16[128,4096]{1,0:T(8,128)(2,1)}, u32[]{:S(2)}, u32[]{:S(2)}) collective-permute-start(bf16[128,4096]{1,0:T(8,128)(2,1)} %collective-permute-done.2.refs_5_), channel_id=1, source_target_pairs={{0,3},{1,0},{2,1},{3,2},{4,7},{5,4},{6,5},{7,6},{8,11},{9,8},{10,9... | collective-permute-start | bytes 3145736 | tf_op jit(solution)/shard_map/ppermute | solution.py:156
  107.6 1.0 copy-start.8
  107.6 70.8 %collective-permute-start.12 = (bf16[128,4096]{1,0:T(8,128)(2,1)}, bf16[128,4096]{1,0:T(8,128)(2,1)}, u32[]{:S(2)}, u32[]{:S(2)}) collective-permute-start(bf16[128,4096]{1,0:T(8,128)(2,1)} %collective-permute-done.4.refs_7_), channel_id=1, source_target_pairs={{0,3},{1,0},{2,1},{3,2},{4,7},{5,4},{6,5},{7,6},{8,11},{9,8},{10,9... | collective-permute-start | bytes 3145736 | tf_op jit(solution)/shard_map/ppermute | solution.py:156
  109.6 17.2 %all-to-all-start = ((s32[32,1,4]{2,1,0:T(1,128)}), s32[32,1,4]{2,1,0:T(1,128)S(1)}, u32[]{:S(2)}, u32[]{:S(2)}) async-start(s32[32,1,4]{2,1,0:T(1,128)} %bitcast), calls=%async_computation | async-start | bytes 32768 | tf_op jit(solution)/shard_map/all_to_all | solution.py:174
  151.5 1.2 copy-start.1
  152.8 1.2 copy-start.3
  154.0 0.7 copy-start.4
  154.6 0.7 copy-start.5
  155.3 0.6 copy-start.6
  187.9 22.2 %all-to-all-start.1 = ((bf16[32,4,16,128]{3,2,1,0:T(8,128)(2,1)}), bf16[32,4,16,128]{3,2,1,0:T(8,128)(2,1)S(1)}, u32[]{:S(2)}, u32[]{:S(2)}) async-start(bf16[32,4,16,128]{3,2,1,0:T(8,128)(2,1)} %bitcast.5), calls=%async_computation.1 | async-start | bytes 1048576 | tf_op jit(solution)/shard_map/all_to_all | solution.py:199
  198.5 6.6 %collective-permute-start.13 = (f32[4,4096]{1,0:T(4,128)S(1)}, f32[4,4096]{1,0:T(4,128)S(1)}, u32[]{:S(2)}, u32[]{:S(2)}) collective-permute-start(f32[4,4096]{1,0:T(4,128)S(1)} %get-tuple-element.21), channel_id=1, source_target_pairs={{0,2},{1,3},{2,0},{3,1},{4,6},{5,7},{6,4},{7,5},{8,10},{9,11},{10,... | collective-permute-start | bytes 196616 | tf_op jit(solution)/shard_map/ppermute | solution.py:156
  198.6 6.5 %collective-permute-start.11 = (f32[4,4096]{1,0:T(4,128)S(1)}, f32[4,4096]{1,0:T(4,128)S(1)}, u32[]{:S(2)}, u32[]{:S(2)}) collective-permute-start(f32[4,4096]{1,0:T(4,128)S(1)} %get-tuple-element.18), channel_id=1, source_target_pairs={{0,1},{1,2},{2,3},{3,0},{4,5},{5,6},{6,7},{7,4},{8,9},{9,10},{10,1... | collective-permute-start | bytes 196616 | tf_op jit(solution)/shard_map/ppermute | solution.py:156
  199.0 6.1 %collective-permute-start.14 = (f32[4,4096]{1,0:T(4,128)S(1)}, f32[4,4096]{1,0:T(4,128)S(1)}, u32[]{:S(2)}, u32[]{:S(2)}) collective-permute-start(f32[4,4096]{1,0:T(4,128)S(1)} %get-tuple-element.22), channel_id=1, source_target_pairs={{0,3},{1,0},{2,1},{3,2},{4,7},{5,4},{6,5},{7,6},{8,11},{9,8},{10,9... | collective-permute-start | bytes 196616 | tf_op jit(solution)/shard_map/ppermute | solution.py:156
Sparse Core Ops, SparseCore 0:
  10.3 117.6 all-gather.1

commit v3 on v2

--- a/solution.py
+++ b/solution.py
@@ -47,12 +47,14 @@
 
 
 def score_kernel(b0, groups, n_prev, full_scale, head_scale, rows, slots, first, q_ref, *refs):
-    n_blocks = sum(n for _, n in groups)
-    blocks = refs[:n_blocks]
-    prev = refs[n_blocks : n_blocks + n_prev]
-    out = refs[n_blocks + n_prev]
-    best = refs[n_blocks + n_prev + 1 : n_blocks + n_prev + 1 + len(groups)]
-    qbuf, hbuf, cbuf, sems, hsem = refs[n_blocks + n_prev + 1 + len(groups) :]
+    n_blocks = sum(len(g) for g in groups)
+    refs = list(refs)
+    take = lambda n: [refs.pop(0) for _ in range(n)]
+    blocks, prev = take(n_blocks), take(n_prev)
+    (out,), best = take(1), take(len(groups))
+    heads = prev.pop(0) if n_prev else refs.pop(0)
+    qbuf, cbuf, sems, hsems = refs
+    n_tiles = heads.shape[0] // TILE
 
     def row_copy(src_row, pos):
         return pltpu.make_async_copy(
@@ -61,8 +63,13 @@
             sems.at[pos],
         )
 
-    heads = pltpu.make_async_copy(q_ref.at[:, pl.ds(0, PREFIX)], hbuf, hsem)
-    heads.start()
+    def head_copy(t):
+        span = pl.ds(pl.multiple_of(t * TILE, TILE), TILE)
+        return pltpu.make_async_copy(q_ref.at[span, pl.ds(0, PREFIX)], heads.at[span], hsems.at[t])
+
+    if not n_prev:
+        for t in range(n_tiles):
+            head_copy(t).start()
     base = first[b0]
     total = first[b0 + n_blocks] - base
 
@@ -75,24 +82,27 @@
     for b in range(n_blocks):
         cbuf[b * BLOCK : (b + 1) * BLOCK] = blocks[b][:, :PREFIX]
     if n_prev:
-        out[...] = prev[0][...]
-        for ref, old in zip(best, prev[1:]):
+        for ref, old in zip([out] + best, prev):
             ref[...] = old[...]
-    heads.wait()
 
     def coarse(t, _):
-        h = hbuf[pl.ds(pl.multiple_of(t * TILE, TILE), TILE), :]
+        span = pl.ds(pl.multiple_of(t * TILE, TILE), TILE)
+        if not n_prev:
+            head_copy(t).wait()
+        h = heads[span, :]
         at = 0
-        for ref, (l0, n) in zip(best, groups):
+        for ref, locals_ in zip(best, groups):
+            n = len(locals_)
             s = lax.dot_general(
                 cbuf[at * BLOCK : (at + n) * BLOCK], h, (((1,), (1,)), ((), ())), preferred_element_type=jnp.float32
             )
             top = jnp.max(s.reshape(n, BLOCK, TILE), axis=1) * head_scale
-            ref[l0 : l0 + n, pl.ds(pl.multiple_of(t * TILE, TILE), TILE)] = top
+            for m, l in enumerate(locals_):
+                ref[l : l + 1, span] = top[m : m + 1]
             at += n
         return 0
 
-    lax.fori_loop(0, hbuf.shape[0] // TILE, coarse, 0)
+    lax.fori_loop(0, n_tiles, coarse, 0)
 
     waited = jnp.int32(0)
     for b in range(n_blocks):
@@ -125,20 +135,22 @@
     n_q = q.shape[0]
     n_blocks = len(blocks)
     kernel = functools.partial(score_kernel, b0, groups, len(prev), D ** (-0.5), PREFIX ** (-0.5))
+    out_shape = [jax.ShapeDtypeStruct((n_slots, GROUP, BLOCK), jnp.bfloat16)]
+    out_shape += [jax.ShapeDtypeStruct((blk_dev, n_q), jnp.float32)] * len(groups)
+    if not prev:
+        out_shape.append(jax.ShapeDtypeStruct((n_q, PREFIX), jnp.bfloat16))
     return pl.pallas_call(
         kernel,
-        out_shape=[jax.ShapeDtypeStruct((n_slots, GROUP, BLOCK), jnp.bfloat16)]
-        + [jax.ShapeDtypeStruct((blk_dev, n_q), jnp.float32)] * len(groups),
+        out_shape=out_shape,
         in_specs=[SMEM] * 3 + [pl.BlockSpec(memory_space=pl.ANY)] + [VMEM] * (n_blocks + len(prev)),
-        out_specs=[VMEM] * (1 + len(groups)),
+        out_specs=[VMEM] * len(out_shape),
         scratch_shapes=[
             pltpu.VMEM(((n_slots + BATCH) * GROUP, D), jnp.bfloat16),
-            pltpu.VMEM((n_q, PREFIX), jnp.bfloat16),
             pltpu.VMEM((n_blocks * BLOCK, PREFIX), jnp.bfloat16),
             pltpu.SemaphoreType.DMA((n_slots,)),
-            pltpu.SemaphoreType.DMA(()),
+            pltpu.SemaphoreType.DMA((n_q // TILE,)),
         ],
-        compiler_params=pltpu.CompilerParams(vmem_limit_bytes=48 * 2**20),
+        compiler_params=pltpu.CompilerParams(vmem_limit_bytes=40 * 2**20),
         cost_estimate=pl.CostEstimate(
             flops=2 * n_blocks * BLOCK * (n_q * PREFIX + 4 * GROUP * D), bytes_accessed=n_blocks * 2**20, transcendentals=0
         ),
@@ -157,15 +169,7 @@
 
     q = lax.all_gather(queries, "corpus", axis=0, tiled=True)
 
-    pieces = []
-    for l in range(blk_dev):
-        own = corpus[l * BLOCK : (l + 1) * BLOCK]
-        before = along(own, 1)
-        after = along(own, -1)
-        across = along(before, 1) if l % 2 == 0 else along(after, -1)
-        pieces.append([own, after, across, before])
-
-    wanted, _ = lax.optimization_barrier((shortlist.reshape(-1), pieces[0][3]))
+    wanted = shortlist.reshape(-1)
     holder = wanted // blk_dev
     slot = (holder // n_query) * n_query + (holder - j) % n_query
     value = (jnp.arange(wanted.shape[0], dtype=jnp.int32) // SHORT) * blk_dev + wanted % blk_dev + 1
@@ -175,7 +179,8 @@
         tags.reshape(n_corpus, n_query), "corpus", split_axis=0, concat_axis=0, tiled=True
     ).reshape(-1)
 
-    order = [(l, r) for r in (0, 1, 3, 2) for l in range(blk_dev)]
+    order = [(l, 0) for l in range(4)] + [(l, 2) for l in range(4)] + [(0, 3), (3, 3), (1, 1), (2, 1)]
+    order += [(0, 1), (3, 1), (1, 3), (2, 3)]
     lists = pl.pallas_call(
         functools.partial(list_kernel, order, blk_dev, n_corpus, n_query),
         out_shape=[jax.ShapeDtypeStruct((n,), jnp.int32) for n in (n_slots, n_slots, len(order) + 1)],
@@ -183,12 +188,23 @@
         out_specs=[SMEM] * 3,
     )(tab)
 
-    early = [pieces[l][r] for l, r in order[:-1]]
-    late = [pieces[l][r] for l, r in order[-1:]]
-    answers, c0, c1, c3, c2 = score(
-        0, [(0, blk_dev)] * 3 + [(0, blk_dev - 1)], lists, q, early, [], blk_dev, n_slots
+    piece = {(l, 0): corpus[l * BLOCK : (l + 1) * BLOCK] for l in range(4)}
+    for l, r, step in ((0, 3, 1), (3, 3, 1), (1, 1, -1), (2, 1, -1)):
+        piece[l, r] = along(piece[l, 0], step)
+    for l, r, step in ((0, 3, 1), (3, 3, 1), (1, 1, -1), (2, 1, -1)):
+        block, _ = lax.optimization_barrier((piece[l, r], lists[0]))
+        piece[l, 2] = along(block, step)
+    for l, r, step, after in ((1, 3, 1, 0), (2, 3, 1, 3), (0, 1, -1, 1), (3, 1, -1, 2)):
+        own, _ = lax.optimization_barrier((piece[l, 0], piece[after, 2]))
+        piece[l, r] = along(own, step)
+
+    n_early = 12
+    early = [piece[lr] for lr in order[:n_early]]
+    late = [piece[lr] for lr in order[n_early:]]
+    answers, c0, c2, c3, c1, heads = score(
+        0, [range(4), range(4), (0, 3), (1, 2)], lists, q, early, [], blk_dev, n_slots
     )
-    answers, c2 = score(len(order) - 1, [(blk_dev - 1, 1)], lists, q, late, [answers, c2], blk_dev, n_slots)
+    answers, c1, c3 = score(n_early, [(0, 3), (1, 2)], lists, q, late, [heads, answers, c1, c3], blk_dev, n_slots)
 
     back = jnp.stack([c0, along(c1, 1), along(c2, 2), along(c3, -1)])
     back = back.reshape(n_query, blk_dev, n_corpus, BLOCK)

time: 220 us -> 203 us (0.923)
  waiting for transfers between devices: 110 us -> 82.9 us
  blocking collectives: 0 us -> 16.5 us
  starting transfers between devices: 38.4 us -> 31.1 us
  local copies, waits for them, and re-layouts: 13.4 us -> 19.7 us
  Pallas kernels: 41.5 us -> 37 us
    ppermute x15, waiting for transfers between devices: 98.5 us -> 55 us  [along(): lax.ppermute(a, 'query', [(t, (t + d) % n_query) for t in range(n_query)])]
    all_gather x1, waiting for transfers between devices: 0.01 us -> 16.9 us  [body(): q = lax.all_gather(queries, 'corpus', axis=0, tiled=True)]
    all_to_all x0 -> x1, blocking collectives: none -> 16.5 us  [body(): lax.all_to_all(tags.reshape(n_corpus, n_query), 'corpus', split_axis=0, c...]
    all_to_all x1 -> x0, starting transfers between devices: 10.3 us -> none  [body(): lax.all_to_all(tags.reshape(n_corpus, n_query), 'corpus', split_axis=0, c...]
    all_to_all x1 -> x0, waiting for transfers between devices: 6.96 us -> none  [body(): lax.all_to_all(tags.reshape(n_corpus, n_query), 'corpus', split_axis=0, c...]
    all_to_all x1, waiting for transfers between devices: 3.75 us -> 10.3 us  [body(): lax.all_to_all(answers.reshape(n_corpus, n_query, GROUP, BLOCK), 'corpus'...]
    unnamed x24 -> x30, local copies, waits for them, and re-layouts: 7.16 us -> 13.1 us
    pallas_call x2, Pallas kernels: 32 us -> 27.4 us  [score(): pl.pallas_call(kernel, out_shape=out_shape, in_specs=[SMEM] * 3 + [pl.Blo...]
  transfers between devices with their start and end apart: 18 -> 17, of which waited for: 8 -> 6; matrix products, arithmetic and copies ran while one was open for 3% -> 3% of each run, Pallas kernels for 15% -> 13%
where the time goes in v3:
time: 203 us; the launch traced here: 202 us
  waiting for transfers between devices  82.9 us (41%)
  Pallas kernels  37 us (18%)
  starting transfers between devices  31.1 us (15%)
  local copies, waits for them, and re-layouts  19.7 us (10%)
  blocking collectives  16.5 us (8%)
  between operations  14.2 us (7%)
    ppermute x15, waiting for transfers between devices, along(): lax.ppermute(a, 'query', [(t, (t + d) % n_query) for t in range(n_query)])  55 us
    pallas_call x2, Pallas kernels, score(): pl.pallas_call(kernel, out_shape=out_shape, in_specs=[SMEM] * 3 + [pl.Blo...  27.4 us
    ppermute x15, starting transfers between devices, along(): lax.ppermute(a, 'query', [(t, (t + d) % n_query) for t in range(n_query)])  18.3 us
    all_gather x1, waiting for transfers between devices, body(): q = lax.all_gather(queries, 'corpus', axis=0, tiled=True)  16.9 us
    all_to_all x1, blocking collectives, body(): lax.all_to_all(tags.reshape(n_corpus, n_query), 'corpus', split_axis=0, c...  16.5 us
    unnamed x30, local copies, waits for them, and re-layouts  13.1 us
    all_to_all x1, starting transfers between devices, body(): lax.all_to_all(answers.reshape(n_corpus, n_query, GROUP, BLOCK), 'corpus'...  12.7 us
    all_to_all x1, waiting for transfers between devices, body(): lax.all_to_all(answers.reshape(n_corpus, n_query, GROUP, BLOCK), 'corpus'...  10.3 us
  transfers between devices with their start and end apart: 17, of which 6 were waited for; matrix products, arithmetic and copies ran while one was open for 3% of the time, Pallas kernels for 13%

profile of v3, /device:TPU:1, one launch (start us, length us, event | category | flops | bytes accessed | tf_op | source)
XLA Modules:
  0.0 202.5 jit_solution(8422708423763923104)
XLA Ops:
  7.2 0.0 all-gather.2.cloned.1.call-start
  7.2 0.7 all-gather.2.cloned.1.call-update
  7.9 3.6 %fusion.8 = (bf16[128,4096]{1,0:T(8,128)(2,1)S(1)}, bf16[128,4096]{1,0:T(8,128)(2,1)}, bf16[128,4096]{1,0:T(8,128)(2,1)S(1)}, bf16[128,4096]{1,0:T(8,128)(2,1)S(1)}) fusion(bf16[512,4096]{1,0:T(8,128)(2,1)} %param.4), kind=kLoop, calls=%fused_computation.50 | loop fusion | bytes 8388608 | tf_op jit(solution)/shard_map/slice | solution.py:191
  11.5 2.1 %collective-permute-start = (bf16[128,4096]{1,0:T(8,128)(2,1)S(1)}, bf16[128,4096]{1,0:T(8,128)(2,1)}, u32[]{:S(2)}, u32[]{:S(2)}) collective-permute-start(bf16[128,4096]{1,0:T(8,128)(2,1)S(1)} %get-tuple-element.30.refs_0_), channel_id=1, source_target_pairs={{0,1},{1,2},{2,3},{3,0},{4,5},{5,6},{6,7},{7,4},{8,9},{9,10},{10,1... | collective-permute-start | bytes 3145736 | tf_op jit(solution)/shard_map/ppermute | solution.py:168
  13.7 1.3 collective-permute-start.6
  15.0 1.4 collective-permute-start.2
  16.3 0.3 collective-permute-start.4
  16.6 0.1 reshape.305
  16.7 0.1 select_reduce_fusion
  16.8 0.1 all_to_all.9
  16.9 16.5 %all_to_all.14 = s32[32,1,4]{2,1,0:T(1,128)S(1)} all-to-all(s32[32,1,4]{2,1,0:T(1,128)S(1)} %bitcast.45), channel_id=1, replica_groups=mesh['corpus'=32,'query'=4] {'corpus'}, dimensions={0} | all-to-all | bytes 1024 | tf_op jit(solution)/shard_map/all_to_all | solution.py:178
  33.4 0.5 broadcast.340
  33.9 0.7 reduce.3
  34.6 0.6 reshape.306.tab
  35.2 9.5 %shard_map.50 = (s32[128]{0:T(128)}, s32[128]{0:T(128)}, s32[17]{0:T(128)}) custom-call(s32[128]{0:T(128)} %reshape.306.tab), custom_call_target="tpu_custom_call" | custom-call | tf_op jit(solution)/shard_map/pallas_call | solution.py:184
  44.8 0.0 collective-permute-done.refs_8_
  44.8 1.4 collective-permute-start.1
  46.2 14.2 %collective-permute-done.6.refs_9_ = bf16[128,4096]{1,0:T(8,128)(2,1)} collective-permute-done((bf16[128,4096]{1,0:T(8,128)(2,1)S(1)}, bf16[128,4096]{1,0:T(8,128)(2,1)}, u32[]{:S(2)}, u32[]{:S(2)}) %collective-permute-start.6) | collective-permute-done | bytes 1048608 | tf_op jit(solution)/shard_map/ppermute | solution.py:168
  60.4 0.0 collective-permute-start.7
  60.4 0.0 collective-permute-done.2.refs_10_
  60.4 2.7 %collective-permute-start.3 = (bf16[128,4096]{1,0:T(8,128)(2,1)}, bf16[128,4096]{1,0:T(8,128)(2,1)S(1)}, u32[]{:S(2)}, u32[]{:S(2)}) collective-permute-start(bf16[128,4096]{1,0:T(8,128)(2,1)} %collective-permute-done.2.refs_10_), channel_id=1, source_target_pairs={{0,3},{1,0},{2,1},{3,2},{4,7},{5,4},{6,5},{7,6},{8,11},{9,8},{10,9... | collective-permute-start | bytes 3145736 | tf_op jit(solution)/shard_map/ppermute | solution.py:168
  63.1 0.0 collective-permute-done.4.refs_11_
  63.1 0.7 collective-permute-start.5
  63.8 19.1 %collective-permute-done.1.refs_4_ = bf16[128,4096]{1,0:T(8,128)(2,1)S(1)} collective-permute-done((bf16[128,4096]{1,0:T(8,128)(2,1)}, bf16[128,4096]{1,0:T(8,128)(2,1)S(1)}, u32[]{:S(2)}, u32[]{:S(2)}) %collective-permute-start.1) | collective-permute-done | bytes 1048608 | tf_op jit(solution)/shard_map/ppermute | solution.py:168
  82.9 1.0 copy-done.1
  83.9 0.0 collective-permute-start.10
  83.9 21.5 %collective-permute-done.7.refs_7_ = bf16[128,4096]{1,0:T(8,128)(2,1)S(1)} collective-permute-done((bf16[128,4096]{1,0:T(8,128)(2,1)}, bf16[128,4096]{1,0:T(8,128)(2,1)S(1)}, u32[]{:S(2)}, u32[]{:S(2)}) %collective-permute-start.7) | collective-permute-done | bytes 1048608 | tf_op jit(solution)/shard_map/ppermute | solution.py:168
  105.4 1.0 copy-done.3
  106.3 0.0 collective-permute-start.11
  106.3 0.0 collective-permute-done.3.refs_5_
  106.3 1.0 copy-done.5
  107.3 2.7 %collective-permute-start.8 = (bf16[128,4096]{1,0:T(8,128)(2,1)S(1)}, bf16[128,4096]{1,0:T(8,128)(2,1)}, u32[]{:S(2)}, u32[]{:S(2)}) collective-permute-start(bf16[128,4096]{1,0:T(8,128)(2,1)S(1)} %get-tuple-element.30.refs_0_), channel_id=1, source_target_pairs={{0,3},{1,0},{2,1},{3,2},{4,7},{5,4},{6,5},{7,6},{8,11},{9,8},{10,9... | collective-permute-start | bytes 3145736 | tf_op jit(solution)/shard_map/ppermute | solution.py:168
  110.0 0.0 collective-permute-done.5.refs_6_
  110.0 1.0 copy-done.7
  111.0 0.1 collective-permute-start.9
  111.1 0.1 reshape.310
  111.2 16.9 %all-gather.2.cloned.1.call-done.q_ref = bf16[4096,4096]{1,0:T(8,128)(2,1)} async-done(((bf16[128,4096]{1,0:T(8,128)(2,1)}), bf16[4096,4096]{1,0:T(8,128)(2,1)}) %all-gather.2.cloned.1.call-update) | async-done | bytes 33554448 | tf_op jit(solution)/shard_map/all_gather | solution.py:170
  128.1 1.2 copy-done.2
  129.3 1.2 copy-done.4
  130.5 1.2 copy-done.6
  131.7 1.2 copy-done.8
  133.0 0.7 copy-done.9
  133.6 0.6 copy-done.10
  134.2 0.6 copy-done.11
  134.8 17.3 %shard_map.51 = (bf16[128,16,128]{2,1,0:T(8,128)(2,1)S(1)}, f32[4,4096]{1,0:T(4,128)S(1)}, f32[4,4096]{1,0:T(4,128)S(1)}, f32[4,4096]{1,0:T(4,128)S(1)}, f32[4,4...) custom-call(s32[128]{0:T(128)S(1)} %copy-done.9, s32[128]{0:T(128)S(1)} %copy-done.10, s32[17]{0:T(128)S(1)} %copy-done.11, ...), custom_call_target="tpu_custom_call" | custom-call | flops 4026531840 | bytes 12582912 | tf_op jit(solution)/shard_map/pallas_call | solution.py:142
  152.2 0.0 collective-permute-done.10.refs_2_
  152.2 0.0 collective-permute-done.11.refs_3_
  152.2 0.0 collective-permute-done.8.refs_0_
  152.2 0.2 collective-permute-done.9.refs_1_
  152.4 1.6 copy-done
  154.0 10.1 %shard_map.52 = (bf16[128,16,128]{2,1,0:T(8,128)(2,1)}, f32[4,4096]{1,0:T(4,128)S(1)}, f32[4,4096]{1,0:T(4,128)S(1)}) custom-call(s32[128]{0:T(128)S(1)} %copy-done.9, s32[128]{0:T(128)S(1)} %copy-done.10, s32[17]{0:T(128)S(1)} %copy-done.11, bf16[4096,4096]{1,0:T(8,128)(2,1)} %all-gather.2.cloned.1.call-done.q_ref, ...), custom_call_target="tpu_custom_call" | custom-call | flops 1342177280 | bytes 4194304 | tf_op jit(solution)/shard_map/pallas_call | solution.py:142
  164.1 1.6 collective-permute-start.12
  165.6 4.2 %collective-permute-start.13 = (f32[4,4096]{1,0:T(4,128)S(1)}, f32[4,4096]{1,0:T(4,128)S(1)}, u32[]{:S(2)}, u32[]{:S(2)}) collective-permute-start(f32[4,4096]{1,0:T(4,128)S(1)} %get-tuple-element.39), channel_id=1, source_target_pairs={{0,2},{1,3},{2,0},{3,1},{4,6},{5,7},{6,4},{7,5},{8,10},{9,11},{10,... | collective-permute-start | bytes 196616 | tf_op jit(solution)/shard_map/ppermute | solution.py:168
  169.8 0.0 collective-permute-start.14
  169.8 12.7 %all-to-all-start.1 = ((bf16[32,4,16,128]{3,2,1,0:T(8,128)(2,1)}), bf16[32,4,16,128]{3,2,1,0:T(8,128)(2,1)S(1)}, u32[]{:S(2)}, u32[]{:S(2)}) async-start(bf16[32,4,16,128]{3,2,1,0:T(8,128)(2,1)} %bitcast.5), calls=%async_computation.1 | async-start | bytes 1048576 | tf_op jit(solution)/shard_map/all_to_all | solution.py:215
  182.6 0.0 collective-permute-done.12
  182.6 0.0 collective-permute-done.13
  182.7 0.0 collective-permute-done.14
  182.7 0.2 pad_maximum_fusion
  183.0 0.9 reshape.307
  183.8 10.3 %all-to-all-done.1 = bf16[32,4,16,128]{3,2,1,0:T(8,128)(2,1)S(1)} async-done(((bf16[32,4,16,128]{3,2,1,0:T(8,128)(2,1)}), bf16[32,4,16,128]{3,2,1,0:T(8,128)(2,1)S(1)}, u32[]{:S(2)}, u32[]{:S(2)}) %all-to-all-start.1) | async-done | bytes 524320 | tf_op jit(solution)/shard_map/all_to_all | solution.py:215
  194.2 0.6 gather_fusion
  194.8 0.1 copy.9
  194.9 0.8 copy.20
  (22 shorter events, 0.1 us)
Async XLA Ops:
  7.2 120.9 %all-gather.2.cloned.1.call-start = ((), (), s32[]{:S(2)}) async-start(), calls=%async_computation.2 | async-start | bytes 34603008 | tf_op jit(solution)/shard_map/all_gather | solution.py:170
  7.9 8.7 %copy-start.12 = (s32[8,8]{1,0:T(8,128)S(1)}, s32[8,8]{1,0:T(8,128)}, u32[]{:S(2)}) copy-start(s32[8,8]{1,0:T(8,128)} %param.5) | copy-start | bytes 772
  11.5 33.2 %collective-permute-start = (bf16[128,4096]{1,0:T(8,128)(2,1)S(1)}, bf16[128,4096]{1,0:T(8,128)(2,1)}, u32[]{:S(2)}, u32[]{:S(2)}) collective-permute-start(bf16[128,4096]{1,0:T(8,128)(2,1)S(1)} %get-tuple-element.30.refs_0_), channel_id=1, source_target_pairs={{0,1},{1,2},{2,3},{3,0},{4,5},{5,6},{6,7},{7,4},{8,9},{9,10},{10,1... | collective-permute-start | bytes 3145736 | tf_op jit(solution)/shard_map/ppermute | solution.py:168
  13.7 46.7 %collective-permute-start.6 = (bf16[128,4096]{1,0:T(8,128)(2,1)S(1)}, bf16[128,4096]{1,0:T(8,128)(2,1)}, u32[]{:S(2)}, u32[]{:S(2)}) collective-permute-start(bf16[128,4096]{1,0:T(8,128)(2,1)S(1)} %get-tuple-element.31.refs_3_), channel_id=1, source_target_pairs={{0,1},{1,2},{2,3},{3,0},{4,5},{5,6},{6,7},{7,4},{8,9},{9,10},{10,1... | collective-permute-start | bytes 3145736 | tf_op jit(solution)/shard_map/ppermute | solution.py:168
  15.0 45.5 %collective-permute-start.2 = (bf16[128,4096]{1,0:T(8,128)(2,1)}, bf16[128,4096]{1,0:T(8,128)(2,1)}, u32[]{:S(2)}, u32[]{:S(2)}) collective-permute-start(bf16[128,4096]{1,0:T(8,128)(2,1)} %get-tuple-element.32.refs_1_), channel_id=1, source_target_pairs={{0,3},{1,0},{2,1},{3,2},{4,7},{5,4},{6,5},{7,6},{8,11},{9,8},{10,9... | collective-permute-start | bytes 3145736 | tf_op jit(solution)/shard_map/ppermute | solution.py:168
  16.3 46.7 %collective-permute-start.4 = (bf16[128,4096]{1,0:T(8,128)(2,1)S(1)}, bf16[128,4096]{1,0:T(8,128)(2,1)}, u32[]{:S(2)}, u32[]{:S(2)}) collective-permute-start(bf16[128,4096]{1,0:T(8,128)(2,1)S(1)} %get-tuple-element.33.refs_2_), channel_id=1, source_target_pairs={{0,3},{1,0},{2,1},{3,2},{4,7},{5,4},{6,5},{7,6},{8,11},{9,8},{10,9... | collective-permute-start | bytes 3145736 | tf_op jit(solution)/shard_map/ppermute | solution.py:168
  44.8 38.1 %collective-permute-start.1 = (bf16[128,4096]{1,0:T(8,128)(2,1)}, bf16[128,4096]{1,0:T(8,128)(2,1)S(1)}, u32[]{:S(2)}, u32[]{:S(2)}) collective-permute-start(bf16[128,4096]{1,0:T(8,128)(2,1)} %collective-permute-done.refs_8_), channel_id=1, source_target_pairs={{0,1},{1,2},{2,3},{3,0},{4,5},{5,6},{6,7},{7,4},{8,9},{9,10},{10,1... | collective-permute-start | bytes 3145736 | tf_op jit(solution)/shard_map/ppermute | solution.py:168
  60.4 44.9 %collective-permute-start.7 = (bf16[128,4096]{1,0:T(8,128)(2,1)}, bf16[128,4096]{1,0:T(8,128)(2,1)S(1)}, u32[]{:S(2)}, u32[]{:S(2)}) collective-permute-start(bf16[128,4096]{1,0:T(8,128)(2,1)} %collective-permute-done.6.refs_9_), channel_id=1, source_target_pairs={{0,1},{1,2},{2,3},{3,0},{4,5},{5,6},{6,7},{7,4},{8,9},{9,10},{10,1... | collective-permute-start | bytes 3145736 | tf_op jit(solution)/shard_map/ppermute | solution.py:168
  60.4 45.9 %collective-permute-start.3 = (bf16[128,4096]{1,0:T(8,128)(2,1)}, bf16[128,4096]{1,0:T(8,128)(2,1)S(1)}, u32[]{:S(2)}, u32[]{:S(2)}) collective-permute-start(bf16[128,4096]{1,0:T(8,128)(2,1)} %collective-permute-done.2.refs_10_), channel_id=1, source_target_pairs={{0,3},{1,0},{2,1},{3,2},{4,7},{5,4},{6,5},{7,6},{8,11},{9,8},{10,9... | collective-permute-start | bytes 3145736 | tf_op jit(solution)/shard_map/ppermute | solution.py:168
  63.1 46.9 %collective-permute-start.5 = (bf16[128,4096]{1,0:T(8,128)(2,1)}, bf16[128,4096]{1,0:T(8,128)(2,1)S(1)}, u32[]{:S(2)}, u32[]{:S(2)}) collective-permute-start(bf16[128,4096]{1,0:T(8,128)(2,1)} %collective-permute-done.4.refs_11_), channel_id=1, source_target_pairs={{0,3},{1,0},{2,1},{3,2},{4,7},{5,4},{6,5},{7,6},{8,11},{9,8},{10,9... | collective-permute-start | bytes 3145736 | tf_op jit(solution)/shard_map/ppermute | solution.py:168
  82.9 1.0 copy-start.1
  83.9 68.3 %collective-permute-start.10 = (bf16[128,4096]{1,0:T(8,128)(2,1)}, bf16[128,4096]{1,0:T(8,128)(2,1)}, u32[]{:S(2)}, u32[]{:S(2)}) collective-permute-start(bf16[128,4096]{1,0:T(8,128)(2,1)} %get-tuple-element.32.refs_1_), channel_id=1, source_target_pairs={{0,1},{1,2},{2,3},{3,0},{4,5},{5,6},{6,7},{7,4},{8,9},{9,10},{10,1... | collective-permute-start | bytes 3145736 | tf_op jit(solution)/shard_map/ppermute | solution.py:168
  105.4 1.0 copy-start.3
  106.3 45.9 %collective-permute-start.11 = (bf16[128,4096]{1,0:T(8,128)(2,1)S(1)}, bf16[128,4096]{1,0:T(8,128)(2,1)}, u32[]{:S(2)}, u32[]{:S(2)}) collective-permute-start(bf16[128,4096]{1,0:T(8,128)(2,1)S(1)} %get-tuple-element.33.refs_2_), channel_id=1, source_target_pairs={{0,1},{1,2},{2,3},{3,0},{4,5},{5,6},{6,7},{7,4},{8,9},{9,10},{10,1... | collective-permute-start | bytes 3145736 | tf_op jit(solution)/shard_map/ppermute | solution.py:168
  106.3 1.0 copy-start.5
  107.3 44.9 %collective-permute-start.8 = (bf16[128,4096]{1,0:T(8,128)(2,1)S(1)}, bf16[128,4096]{1,0:T(8,128)(2,1)}, u32[]{:S(2)}, u32[]{:S(2)}) collective-permute-start(bf16[128,4096]{1,0:T(8,128)(2,1)S(1)} %get-tuple-element.30.refs_0_), channel_id=1, source_target_pairs={{0,3},{1,0},{2,1},{3,2},{4,7},{5,4},{6,5},{7,6},{8,11},{9,8},{10,9... | collective-permute-start | bytes 3145736 | tf_op jit(solution)/shard_map/ppermute | solution.py:168
  110.0 1.0 copy-start.7
  111.0 41.4 %collective-permute-start.9 = (bf16[128,4096]{1,0:T(8,128)(2,1)S(1)}, bf16[128,4096]{1,0:T(8,128)(2,1)}, u32[]{:S(2)}, u32[]{:S(2)}) collective-permute-start(bf16[128,4096]{1,0:T(8,128)(2,1)S(1)} %get-tuple-element.31.refs_3_), channel_id=1, source_target_pairs={{0,3},{1,0},{2,1},{3,2},{4,7},{5,4},{6,5},{7,6},{8,11},{9,8},{10,9... | collective-permute-start | bytes 3145736 | tf_op jit(solution)/shard_map/ppermute | solution.py:168
  128.1 1.2 copy-start.2
  129.3 1.2 copy-start.4
  130.5 1.2 copy-start.6
  131.7 1.2 copy-start.8
  133.0 0.7 copy-start.9
  133.6 0.6 copy-start.10
  134.2 0.6 copy-start.11
  152.4 1.6 copy-start
  164.1 18.6 %collective-permute-start.12 = (f32[4,4096]{1,0:T(4,128)S(1)}, f32[4,4096]{1,0:T(4,128)S(1)}, u32[]{:S(2)}, u32[]{:S(2)}) collective-permute-start(f32[4,4096]{1,0:T(4,128)S(1)} %get-tuple-element.38), channel_id=1, source_target_pairs={{0,1},{1,2},{2,3},{3,0},{4,5},{5,6},{6,7},{7,4},{8,9},{9,10},{10,1... | collective-permute-start | bytes 196616 | tf_op jit(solution)/shard_map/ppermute | solution.py:168
  165.6 17.0 %collective-permute-start.13 = (f32[4,4096]{1,0:T(4,128)S(1)}, f32[4,4096]{1,0:T(4,128)S(1)}, u32[]{:S(2)}, u32[]{:S(2)}) collective-permute-start(f32[4,4096]{1,0:T(4,128)S(1)} %get-tuple-element.39), channel_id=1, source_target_pairs={{0,2},{1,3},{2,0},{3,1},{4,6},{5,7},{6,4},{7,5},{8,10},{9,11},{10,... | collective-permute-start | bytes 196616 | tf_op jit(solution)/shard_map/ppermute | solution.py:168
  169.8 12.8 %collective-permute-start.14 = (f32[4,4096]{1,0:T(4,128)S(1)}, f32[4,4096]{1,0:T(4,128)S(1)}, u32[]{:S(2)}, u32[]{:S(2)}) collective-permute-start(f32[4,4096]{1,0:T(4,128)S(1)} %get-tuple-element.40), channel_id=1, source_target_pairs={{0,3},{1,0},{2,1},{3,2},{4,7},{5,4},{6,5},{7,6},{8,11},{9,8},{10,9... | collective-permute-start | bytes 196616 | tf_op jit(solution)/shard_map/ppermute | solution.py:168
  169.8 24.3 %all-to-all-start.1 = ((bf16[32,4,16,128]{3,2,1,0:T(8,128)(2,1)}), bf16[32,4,16,128]{3,2,1,0:T(8,128)(2,1)S(1)}, u32[]{:S(2)}, u32[]{:S(2)}) async-start(bf16[32,4,16,128]{3,2,1,0:T(8,128)(2,1)} %bitcast.5), calls=%async_computation.1 | async-start | bytes 1048576 | tf_op jit(solution)/shard_map/all_to_all | solution.py:215
Sparse Core Ops, SparseCore 0:
  10.3 117.7 all-gather.1

commit v4 on v2

v4 whole, which is shorter than its diff:
```python
import functools

import jax
import jax.numpy as jnp
from jax import lax
from jax.experimental import pallas as pl
from jax.experimental.pallas import tpu as pltpu
from jax.sharding import PartitionSpec as P

D = 4096
PREFIX = 256
BLOCK = 128
GROUP = 16
SHORT = 8
BATCH = 8
TILE = 256
MIB = 2**20

SMEM = pl.BlockSpec(memory_space=pltpu.SMEM)
VMEM = pl.BlockSpec(memory_space=pltpu.VMEM)
ANY = pl.BlockSpec(memory_space=pl.ANY)


def list_kernel(steps, blk_dev, n_src, n_rel, tab, rows, slots, first):
    def clear(n, _):
        rows[n] = 0
        slots[n] = 0
        return 0

    lax.fori_loop(0, n_src * n_rel, clear, 0)
    count = jnp.int32(0)
    for b in range(len(steps) * blk_dev):
        first[b] = count

        def scan(i, n, local=b % blk_dev, r=steps[b // blk_dev]):
            v = tab[i * n_rel + r] - 1
            hit = (v >= 0) & (v % blk_dev == local)

            @pl.when(hit)
            def _():
                slots[n] = i
                rows[n] = i * BLOCK + (v // blk_dev) * GROUP

            return n + hit.astype(jnp.int32)

        count = lax.fori_loop(0, n_src, scan, count)
    first[len(steps) * blk_dev] = count


def coarse_steps(heads, arrays, cbuf, best, scale):
    at = 0
    for group in arrays:
        for ref in group:
            cbuf[at : at + ref.shape[0]] = ref[:, :PREFIX]
            at += ref.shape[0]

    def tile(t, _):
        span = pl.ds(pl.multiple_of(t * TILE, TILE), TILE)
        h = heads[span, :]
        at = 0
        for group, out in zip(arrays, best):
            n = sum(ref.shape[0] for ref in group)
            s = lax.dot_general(
                cbuf[at : at + n], h, (((1,), (1,)), ((), ())), preferred_element_type=jnp.float32
            )
            out[:, span] = jnp.max(s.reshape(n // BLOCK, BLOCK, TILE), axis=1) * scale
            at += n
        return 0

    lax.fori_loop(0, heads.shape[0] // TILE, tile, 0)


def coarse_kernel(scale, heads, *refs):
    n = (len(refs) - 1) // 2
    coarse_steps(heads, [[ref] for ref in refs[:n]], refs[2 * n], refs[n : 2 * n], scale)


def score_kernel(b0, widths, scale, head_scale, rows, slots, first, q_ref, *refs):
    n_arrays = sum(widths)
    refs = list(refs)
    arrays = [refs.pop(0) for _ in range(n_arrays)]
    if len(widths) == 1:
        heads, out, best, qbuf, cbuf, sems = refs
    else:
        out, qbuf, sems = refs
    n_rel = len(widths)

    def row_copy(src_row, pos):
        return pltpu.make_async_copy(
            q_ref.at[pl.ds(pl.multiple_of(src_row, GROUP), GROUP)],
            qbuf.at[pl.ds(pl.multiple_of(pos * GROUP, GROUP), GROUP)],
            sems.at[pos],
        )

    n_blocks = sum(ref.shape[0] // BLOCK for ref in arrays)
    base = first[b0]
    total = first[b0 + n_blocks] - base

    def start(n, _):
        row_copy(rows[base + n], n).start()
        return 0

    lax.fori_loop(0, total, start, 0)
    if n_rel == 1:
        coarse_steps(heads, [arrays], cbuf, [best], head_scale)

    waited = jnp.int32(0)
    b = b0
    for ref, rel in zip(arrays, [k for k, n in enumerate(widths) for _ in range(n)]):
        for local in range(ref.shape[0] // BLOCK):
            lo, hi = first[b] - base, first[b + 1] - base
            b += 1

            def step(t, waited, lo=lo, hi=hi, ref=ref, local=local, rel=rel):
                at = lo + t * BATCH
                upto = jnp.minimum(at + BATCH, total)

                def wait(n, _):
                    row_copy(0, n).wait()
                    return 0

                lax.fori_loop(waited, upto, wait, 0)
                part = qbuf[pl.ds(pl.multiple_of(at * GROUP, GROUP), BATCH * GROUP), :]
                block = ref[local * BLOCK : (local + 1) * BLOCK, :]
                s = lax.dot_general(part, block, (((1,), (1,)), ((), ())), preferred_element_type=jnp.float32)
                s = (s * scale).astype(out.dtype)
                for m in range(BATCH):

                    @pl.when(at + m < hi)
                    def _():
                        out[slots[base + at + m] * n_rel + rel] = s[m * GROUP : (m + 1) * GROUP]

                return jnp.maximum(waited, upto)

            waited = lax.fori_loop(0, (hi - lo + BATCH - 1) // BATCH, step, waited)


def coarse_call(heads, arrays, blk_dev):
    out = jax.ShapeDtypeStruct((blk_dev, heads.shape[0]), jnp.float32)
    passages = sum(a.shape[0] for a in arrays)
    return pl.pallas_call(
        functools.partial(coarse_kernel, PREFIX ** (-0.5)),
        out_shape=[out] * len(arrays),
        in_specs=[VMEM] * (1 + len(arrays)),
        out_specs=[VMEM] * len(arrays),
        scratch_shapes=[pltpu.VMEM((passages, PREFIX), jnp.bfloat16)],
        compiler_params=pltpu.CompilerParams(vmem_limit_bytes=24 * MIB),
        cost_estimate=pl.CostEstimate(
            flops=2 * passages * heads.shape[0] * PREFIX, bytes_accessed=8 * MIB, transcendentals=0
        ),
    )(heads, *arrays)


def score_call(b0, groups, lists, q, heads, n_src, blk_dev):
    arrays = [a for group in groups for a in group]
    n_slots = n_src * len(groups)
    passages = sum(a.shape[0] for a in arrays)
    out_shape = [jax.ShapeDtypeStruct((n_slots, GROUP, BLOCK), jnp.bfloat16)]
    scratch = [pltpu.VMEM(((n_slots + BATCH) * GROUP, D), jnp.bfloat16)]
    more = []
    if len(groups) == 1:
        more = [heads]
        out_shape.append(jax.ShapeDtypeStruct((blk_dev, q.shape[0]), jnp.float32))
        scratch.append(pltpu.VMEM((passages, PREFIX), jnp.bfloat16))
    scratch.append(pltpu.SemaphoreType.DMA((n_slots,)))
    kernel = functools.partial(
        score_kernel, b0, [len(group) for group in groups], D ** (-0.5), PREFIX ** (-0.5)
    )
    return pl.pallas_call(
        kernel,
        out_shape=out_shape,
        in_specs=[SMEM] * 3 + [ANY] + [VMEM] * (len(arrays) + len(more)),
        out_specs=[VMEM] * len(out_shape),
        scratch_shapes=scratch,
        compiler_params=pltpu.CompilerParams(vmem_limit_bytes=(32 if len(groups) > 1 else 24) * MIB),
        cost_estimate=pl.CostEstimate(flops=2 * passages * 64 * D, bytes_accessed=passages * D * 4, transcendentals=0),
    )(*lists, q, *arrays, *more)


def pick_kernel(n_rel, slot, near, far, out):
    for e in range(slot.shape[0]):
        i, r = slot[e] // n_rel, slot[e] % n_rel
        k = jnp.where(r == 3, 2, jnp.minimum(r, 1))
        g, s = e // SHORT, e % SHORT
        out[g * GROUP : (g + 1) * GROUP, s * BLOCK : (s + 1) * BLOCK] = jnp.where(
            r == 2, far[i], near[i * (n_rel - 1) + k]
        )


def body(queries, corpus, shortlist):
    n_corpus = lax.axis_size("corpus")
    n_query = lax.axis_size("query")
    n_slots = n_corpus * n_query
    blk_dev = corpus.shape[0] // BLOCK
    half = corpus.shape[0] // 2
    j = lax.axis_index("query")

    def along(a, d):
        return lax.ppermute(a, "query", [(t, (t + d) % n_query) for t in range(n_query)])

    def exchange(a):
        return lax.all_to_all(a, "corpus", split_axis=0, concat_axis=0, tiled=True)

    q = lax.all_gather(queries, "corpus", axis=0, tiled=True)

    before = along(corpus, 1)
    after = along(corpus, -1)

    wanted = shortlist.reshape(-1)
    holder = wanted // blk_dev
    slot = (holder // n_query) * n_query + (holder - j) % n_query
    value = (jnp.arange(wanted.shape[0], dtype=jnp.int32) // SHORT) * blk_dev + wanted % blk_dev + 1
    ids = jnp.arange(n_slots, dtype=jnp.int32)
    tags = jnp.max(jnp.where(slot[None, :] == ids[:, None], value[None, :], 0), axis=1)
    tab = exchange(tags.reshape(n_corpus, n_query)).reshape(-1)
    steps = (0, 1, 3, 2)
    n_lists = len(steps) * blk_dev + 1
    lists = pl.pallas_call(
        functools.partial(list_kernel, steps, blk_dev, n_corpus, n_query),
        out_shape=[jax.ShapeDtypeStruct((n,), jnp.int32) for n in (n_slots, n_slots, n_lists)],
        in_specs=[SMEM],
        out_specs=[SMEM] * 3,
    )(tab)

    heads = exchange(jnp.broadcast_to(queries[None, :, :PREFIX], (n_corpus, queries.shape[0], PREFIX)))
    heads = heads.reshape(-1, PREFIX)

    before, after, heads, *lists = lax.optimization_barrier((before, after, heads, *lists))
    low = along(before[:half], 1)
    high = along(after[half:], -1)

    c0, c1, c3 = coarse_call(heads, [corpus, after, before], blk_dev)
    (near,) = score_call(0, [[corpus], [after], [before]], lists, q, None, n_corpus, blk_dev)
    near = exchange(near.reshape(n_corpus, -1, BLOCK))
    far, c2 = score_call(3 * blk_dev, [[low, high]], lists, q, heads, n_corpus, blk_dev)
    far = exchange(far)

    back = jnp.stack([c0, along(c1, 1), along(c2, 2), along(c3, -1)])
    back = back.reshape(n_query, blk_dev, n_corpus, BLOCK)
    coarse = jnp.stack(
        [lax.dynamic_index_in_dim(back, (j - t) % n_query, 0, keepdims=False) for t in range(n_query)], axis=2
    ).reshape(blk_dev, -1)

    rescored = pl.pallas_call(
        functools.partial(pick_kernel, n_query),
        out_shape=jax.ShapeDtypeStruct((queries.shape[0], SHORT * BLOCK), jnp.bfloat16),
        in_specs=[SMEM, VMEM, VMEM],
        out_specs=VMEM,
    )(slot, near.reshape(-1, GROUP, BLOCK), far)
    return (coarse, rescored)


def solution(mesh):
    spec = P(("corpus", "query"), None)
    return jax.shard_map(
        body, mesh=mesh, in_specs=(spec, spec, spec), out_specs=(spec, spec), check_vma=False
    )
```

time: 220 us -> 226 us (1.027)
  waiting for transfers between devices: 110 us -> 104 us
  starting transfers between devices: 38.4 us -> 44 us
  local copies, waits for them, and re-layouts: 13.4 us -> 17.5 us
  Pallas kernels: 41.5 us -> 44 us
    ppermute x15 -> x7, waiting for transfers between devices: 98.5 us -> 67 us  [along(): lax.ppermute(a, 'query', [(t, (t + d) % n_query) for t in range(n_query)])]
    all_to_all x2 -> x4, waiting for transfers between devices: 10.7 us -> 35.8 us  [exchange(): return lax.all_to_all(a, 'corpus', split_axis=0, concat_axis=0, tiled=True)]
    all_to_all x2 -> x4, starting transfers between devices: 20.9 us -> 36.1 us  [exchange(): return lax.all_to_all(a, 'corpus', split_axis=0, concat_axis=0, tiled=True)]
    ppermute x15 -> x7, starting transfers between devices: 17.5 us -> 7.93 us  [along(): lax.ppermute(a, 'query', [(t, (t + d) % n_query) for t in range(n_query)])]
    slice x1 -> x3, local copies, waits for them, and re-layouts: 2.66 us -> 7.24 us  [the longest x1 3.23 us: body(): low = along(before[:half], 1)]
    pallas_call x3 -> x5, Pallas kernels: 41.5 us -> 44 us  [the longest x2 19.8 us: score_call(): pl.pallas_call(kernel, out_shape=out_shape, in_specs=[SMEM] * 3 + [ANY] +...]
    unnamed x24 -> x19, local copies, waits for them, and re-layouts: 7.16 us -> 5.14 us
  transfers between devices with their start and end apart: 18 -> 12, of which waited for: 8 -> 6; matrix products, arithmetic and copies ran while one was open for 3% -> 6% of each run, Pallas kernels for 15% -> 19%
where the time goes in v4:
time: 226 us; the launch traced here: 224 us
  waiting for transfers between devices  104 us (46%)
  starting transfers between devices  44 us (19%)
  Pallas kernels  44 us (19%)
  local copies, waits for them, and re-layouts  17.5 us (8%)
  between operations  14.2 us (6%)
    ppermute x7, waiting for transfers between devices, along(): lax.ppermute(a, 'query', [(t, (t + d) % n_query) for t in range(n_query)])  67 us
    all_to_all x4, starting transfers between devices, exchange(): return lax.all_to_all(a, 'corpus', split_axis=0, concat_axis=0, tiled=True)  36.1 us
    all_to_all x4, waiting for transfers between devices, exchange(): return lax.all_to_all(a, 'corpus', split_axis=0, concat_axis=0, tiled=True)  35.8 us
    pallas_call x2, Pallas kernels, score_call(): pl.pallas_call(kernel, out_shape=out_shape, in_specs=[SMEM] * 3 + [ANY] +...  19.8 us
    pallas_call x1, Pallas kernels, body(): pl.pallas_call(functools.partial(list_kernel, steps, blk_dev, n_corpus, n...  11.4 us
    pallas_call x1, Pallas kernels, coarse_call(): pl.pallas_call(functools.partial(coarse_kernel, PREFIX ** (-0.5)), out_sh...  10.5 us
    ppermute x7, starting transfers between devices, along(): lax.ppermute(a, 'query', [(t, (t + d) % n_query) for t in range(n_query)])  7.93 us
    unnamed x19, local copies, waits for them, and re-layouts  5.14 us
  transfers between devices with their start and end apart: 12, of which 6 were waited for; matrix products, arithmetic and copies ran while one was open for 6% of the time, Pallas kernels for 19%

profile of v4, /device:TPU:1, one launch (start us, length us, event | category | flops | bytes accessed | tf_op | source)
XLA Modules:
  0.0 224.4 jit_solution(6674081746128256269)
XLA Ops:
  7.2 0.0 all-gather.2.cloned.1.call-start
  7.2 0.7 all-gather.2.cloned.1.call-update
  7.9 3.6 %collective-permute-start.1 = (bf16[512,4096]{1,0:T(8,128)(2,1)}, bf16[512,4096]{1,0:T(8,128)(2,1)}, u32[]{:S(2)}, u32[]{:S(2)}) collective-permute-start(bf16[512,4096]{1,0:T(8,128)(2,1)} %refs_0_.3), channel_id=1, source_target_pairs={{0,3},{1,0},{2,1},{3,2},{4,7},{5,4},{6,5},{7,6},{8,11},{9,8},{10,9... | collective-permute-start | bytes 12582920 | tf_op jit(solution)/shard_map/ppermute | solution.py:199
  11.5 0.0 collective-permute-start
  11.5 0.8 reshape.136
  12.3 0.0 copy-start.7
  12.3 0.1 select_reduce_fusion
  12.4 0.7 all_to_all.16
  13.2 8.9 %all-to-all-start.1 = ((s32[32,1,4]{2,1,0:T(1,128)}), s32[32,1,4]{2,1,0:T(1,128)S(1)}, u32[]{:S(2)}, u32[]{:S(2)}) async-start(s32[32,1,4]{2,1,0:T(1,128)} %bitcast.1), calls=%async_computation.1 | async-start | bytes 32768 | tf_op jit(solution)/shard_map/all_to_all | solution.py:202
  22.0 0.9 slice.9
  22.9 6.1 %all-to-all-done.1 = s32[32,1,4]{2,1,0:T(1,128)S(1)} async-done(((s32[32,1,4]{2,1,0:T(1,128)}), s32[32,1,4]{2,1,0:T(1,128)S(1)}, u32[]{:S(2)}, u32[]{:S(2)}) %all-to-all-start.1) | async-done | bytes 544 | tf_op jit(solution)/shard_map/all_to_all | solution.py:202
  29.0 1.6 broadcast_in_dim.14
  30.6 0.0 copy-done.7
  30.6 4.2 %all-to-all-start = ((bf16[32,128,256]{2,1,0:T(8,128)(2,1)}), bf16[32,128,256]{2,1,0:T(8,128)(2,1)S(1)}, u32[]{:S(2)}, u32[]{:S(2)}) async-start(bf16[32,128,256]{2,1,0:T(8,128)(2,1)} %broadcast_in_dim.14), calls=%async_computation | async-start | bytes 4194304 | tf_op jit(solution)/shard_map/all_to_all | solution.py:202
  34.8 0.5 broadcast.181
  35.4 0.7 reduce.3
  36.0 0.6 reshape.137.tab
  36.7 11.4 %shard_map.50 = (s32[128]{0:T(128)}, s32[128]{0:T(128)}, s32[17]{0:T(128)}) custom-call(s32[128]{0:T(128)} %reshape.137.tab), custom_call_target="tpu_custom_call" | custom-call | tf_op jit(solution)/shard_map/pallas_call | solution.py:218
  48.1 20.8 %all-to-all-done = bf16[32,128,256]{2,1,0:T(8,128)(2,1)S(1)} async-done(((bf16[32,128,256]{2,1,0:T(8,128)(2,1)}), bf16[32,128,256]{2,1,0:T(8,128)(2,1)S(1)}, u32[]{:S(2)}, u32[]{:S(2)}) %all-to-all-start) | async-done | bytes 2097184 | tf_op jit(solution)/shard_map/all_to_all | solution.py:202
  68.8 32.2 %collective-permute-done.1.refs_1_ = bf16[512,4096]{1,0:T(8,128)(2,1)} collective-permute-done((bf16[512,4096]{1,0:T(8,128)(2,1)}, bf16[512,4096]{1,0:T(8,128)(2,1)}, u32[]{:S(2)}, u32[]{:S(2)}) %collective-permute-start.1) | collective-permute-done | bytes 4194336 | tf_op jit(solution)/shard_map/ppermute | solution.py:199
  101.1 3.1 %collective-permute-done.refs_2_ = bf16[512,4096]{1,0:T(8,128)(2,1)} collective-permute-done((bf16[512,4096]{1,0:T(8,128)(2,1)}, bf16[512,4096]{1,0:T(8,128)(2,1)}, u32[]{:S(2)}, u32[]{:S(2)}) %collective-permute-start) | collective-permute-done | bytes 4194336 | tf_op jit(solution)/shard_map/ppermute | solution.py:199
  104.2 3.2 %slice.10 = bf16[256,4096]{1,0:T(8,128)(2,1)} slice(bf16[512,4096]{1,0:T(8,128)(2,1)} %collective-permute-done.refs_2_), slice={[0:256], [0:4096]} | slice | bytes 4194304 | tf_op jit(solution)/shard_map/slice | solution.py:229
  107.4 3.2 %slice.11 = bf16[256,4096]{1,0:T(8,128)(2,1)} slice(bf16[512,4096]{1,0:T(8,128)(2,1)} %collective-permute-done.1.refs_1_), slice={[256:512], [0:4096]} | slice | bytes 4194304 | tf_op jit(solution)/shard_map/slice | solution.py:230
  110.6 0.4 collective-permute-start.4
  111.0 1.0 collective-permute-start.3
  112.0 0.0 copy-start
  112.0 2.2 copy-done
  114.2 0.0 copy-start.2
  114.2 0.0 copy-start.3
  114.2 0.0 copy-start.4
  114.2 10.5 %shard_map.51 = (f32[4,4096]{1,0:T(4,128)S(1)}, f32[4,4096]{1,0:T(4,128)S(1)}, f32[4,4096]{1,0:T(4,128)S(1)}) custom-call(bf16[4096,256]{1,0:T(8,128)(2,1)S(1)} %bitcast.24, bf16[512,4096]{1,0:T(8,128)(2,1)S(1)} %copy-done, bf16[512,4096]{1,0:T(8,128)(2,1)} %collective-permute-done.1.refs_1_, bf16[512,4096]{1,0:T(8,128)(2,1)} %collective-permute-done.refs_2_), custom_call_target="tpu_custom_call" | custom-call | flops 3221225472 | bytes 8388608 | tf_op jit(solution)/shard_map/pallas_call | solution.py:141
  124.7 0.5 collective-permute-start.2
  125.2 2.3 %collective-permute-start.6 = (f32[4,4096]{1,0:T(4,128)S(1)}, f32[4,4096]{1,0:T(4,128)S(1)}, u32[]{:S(2)}, u32[]{:S(2)}) collective-permute-start(f32[4,4096]{1,0:T(4,128)S(1)} %get-tuple-element.28), channel_id=1, source_target_pairs={{0,3},{1,0},{2,1},{3,2},{4,7},{5,4},{6,5},{7,6},{8,11},{9,8},{10,9... | collective-permute-start | bytes 196616 | tf_op jit(solution)/shard_map/ppermute | solution.py:199
  127.5 31.7 %collective-permute-done.2 = f32[4,4096]{1,0:T(4,128)S(1)} collective-permute-done((f32[4,4096]{1,0:T(4,128)S(1)}, f32[4,4096]{1,0:T(4,128)S(1)}, u32[]{:S(2)}, u32[]{:S(2)}) %collective-permute-start.2) | collective-permute-done | bytes 65568 | tf_op jit(solution)/shard_map/ppermute | solution.py:199
  159.2 0.0 collective-permute-done.4.refs_1_
  159.2 0.0 collective-permute-done.3.refs_0_
  159.2 0.0 all-gather.2.cloned.1.call-done.q_ref
  159.2 0.0 copy-done.2
  159.2 0.0 copy-done.3
  159.2 0.0 copy-done.4
  159.2 9.8 %shard_map.52 = (bf16[32,16,128]{2,1,0:T(8,128)(2,1)}, f32[4,4096]{1,0:T(4,128)S(1)}) custom-call(s32[128]{0:T(128)S(1)} %copy-done.2, s32[128]{0:T(128)S(1)} %copy-done.3, s32[17]{0:T(128)S(1)} %copy-done.4, bf16[4096,4096]{1,0:T(8,128)(2,1)} %all-gather.2.cloned.1.call-done.q_ref, bf16[256,4096]{1,0:T(8,128)(2,1)} %collective-permute-done.3.refs_0_, ...), custom_call_target="tpu_custom_call" | custom-call | flops 268435456 | bytes 8388608 | tf_op jit(solution)/shard_map/pallas_call | solution.py:169
  169.0 11.4 %all-to-all-start.3 = ((bf16[32,16,128]{2,1,0:T(8,128)(2,1)}), bf16[32,16,128]{2,1,0:T(8,128)(2,1)S(1)}, u32[]{:S(2)}, u32[]{:S(2)}) async-start(bf16[32,16,128]{2,1,0:T(8,128)(2,1)} %get-tuple-element.29), calls=%async_computation.3 | async-start | bytes 262144 | tf_op jit(solution)/shard_map/all_to_all | solution.py:202
  180.4 0.1 collective-permute-start.5
  180.5 0.0 copy-start.1
  180.6 2.2 copy-done.1
  182.7 10.0 %shard_map.53 = bf16[96,16,128]{2,1,0:T(8,128)(2,1)} custom-call(s32[128]{0:T(128)S(1)} %copy-done.2, s32[128]{0:T(128)S(1)} %copy-done.3, s32[17]{0:T(128)S(1)} %copy-done.4, bf16[4096,4096]{1,0:T(8,128)(2,1)} %all-gather.2.cloned.1.call-done.q_ref, bf16[512,4096]{1,0:T(8,128)(2,1)S(1)} %copy-done.1, bf16[512,4096]{1,0:T(8,128)(2,1)} %collective-permute-done.1.refs_1_, ...), custom_call_target="tpu_custom_call" | custom-call | flops 805306368 | bytes 25165824 | tf_op jit(solution)/shard_map/pallas_call | solution.py:169
  192.8 0.0 collective-permute-done.5
  192.8 0.0 all-to-all-done.3.far
  192.8 0.0 copy-start.6
  192.8 11.5 %all-to-all-start.2 = ((bf16[32,48,128]{2,1,0:T(8,128)(2,1)}), bf16[32,48,128]{2,1,0:T(8,128)(2,1)S(1)}, u32[]{:S(2)}, u32[]{:S(2)}) async-start(bf16[32,48,128]{2,1,0:T(8,128)(2,1)} %bitcast.6), calls=%async_computation.2 | async-start | bytes 786432 | tf_op jit(solution)/shard_map/all_to_all | solution.py:202
  204.4 0.0 collective-permute-done.6
  204.4 0.2 pad_maximum_fusion
  204.7 0.9 reshape.138
  205.6 9.0 %all-to-all-done.2 = bf16[32,48,128]{2,1,0:T(8,128)(2,1)S(1)} async-done(((bf16[32,48,128]{2,1,0:T(8,128)(2,1)}), bf16[32,48,128]{2,1,0:T(8,128)(2,1)S(1)}, u32[]{:S(2)}, u32[]{:S(2)}) %all-to-all-start.2) | async-done | bytes 393248 | tf_op jit(solution)/shard_map/all_to_all | solution.py:202
  214.5 0.0 copy-start.5
  214.5 0.0 copy-done.6
  214.5 0.7 copy-done.5
  215.3 2.3 %shard_map.54 = bf16[128,1024]{1,0:T(8,128)(2,1)} custom-call(s32[64]{0:T(128)} %copy-done.7, bf16[96,16,128]{2,1,0:T(8,128)(2,1)} %bitcast.27, bf16[32,16,128]{2,1,0:T(8,128)(2,1)} %copy-done.6), custom_call_target="tpu_custom_call" | custom-call | tf_op jit(solution)/shard_map/pallas_call | solution.py:244
  (6 shorter events, 0.1 us)
Async XLA Ops:
  7.2 152.0 %all-gather.2.cloned.1.call-start = ((), (), s32[]{:S(2)}) async-start(), calls=%async_computation.4 | async-start | bytes 34603008 | tf_op jit(solution)/shard_map/all_gather | solution.py:204
  7.9 93.2 %collective-permute-start.1 = (bf16[512,4096]{1,0:T(8,128)(2,1)}, bf16[512,4096]{1,0:T(8,128)(2,1)}, u32[]{:S(2)}, u32[]{:S(2)}) collective-permute-start(bf16[512,4096]{1,0:T(8,128)(2,1)} %refs_0_.3), channel_id=1, source_target_pairs={{0,3},{1,0},{2,1},{3,2},{4,7},{5,4},{6,5},{7,6},{8,11},{9,8},{10,9... | collective-permute-start | bytes 12582920 | tf_op jit(solution)/shard_map/ppermute | solution.py:199
  11.5 92.6 %collective-permute-start = (bf16[512,4096]{1,0:T(8,128)(2,1)}, bf16[512,4096]{1,0:T(8,128)(2,1)}, u32[]{:S(2)}, u32[]{:S(2)}) collective-permute-start(bf16[512,4096]{1,0:T(8,128)(2,1)} %refs_0_.3), channel_id=1, source_target_pairs={{0,1},{1,2},{2,3},{3,0},{4,5},{5,6},{6,7},{7,4},{8,9},{9,10},{10,1... | collective-permute-start | bytes 12582920 | tf_op jit(solution)/shard_map/ppermute | solution.py:199
  12.3 18.3 %copy-start.7 = (s32[64]{0:T(128)}, s32[64]{0:T(128)S(1)}, u32[]{:S(2)}) copy-start(s32[64]{0:T(128)S(1)} %get-tuple-element.34.slot) | copy-start | bytes 772
  13.2 15.8 %all-to-all-start.1 = ((s32[32,1,4]{2,1,0:T(1,128)}), s32[32,1,4]{2,1,0:T(1,128)S(1)}, u32[]{:S(2)}, u32[]{:S(2)}) async-start(s32[32,1,4]{2,1,0:T(1,128)} %bitcast.1), calls=%async_computation.1 | async-start | bytes 32768 | tf_op jit(solution)/shard_map/all_to_all | solution.py:202
  30.6 38.3 %all-to-all-start = ((bf16[32,128,256]{2,1,0:T(8,128)(2,1)}), bf16[32,128,256]{2,1,0:T(8,128)(2,1)S(1)}, u32[]{:S(2)}, u32[]{:S(2)}) async-start(bf16[32,128,256]{2,1,0:T(8,128)(2,1)} %broadcast_in_dim.14), calls=%async_computation | async-start | bytes 4194304 | tf_op jit(solution)/shard_map/all_to_all | solution.py:202
  110.6 48.6 %collective-permute-start.4 = (bf16[256,4096]{1,0:T(8,128)(2,1)}, bf16[256,4096]{1,0:T(8,128)(2,1)}, u32[]{:S(2)}, u32[]{:S(2)}) collective-permute-start(bf16[256,4096]{1,0:T(8,128)(2,1)} %slice.11), channel_id=1, source_target_pairs={{0,3},{1,0},{2,1},{3,2},{4,7},{5,4},{6,5},{7,6},{8,11},{9,8},{10,9... | collective-permute-start | bytes 6291464 | tf_op jit(solution)/shard_map/ppermute | solution.py:199
  111.0 48.2 %collective-permute-start.3 = (bf16[256,4096]{1,0:T(8,128)(2,1)}, bf16[256,4096]{1,0:T(8,128)(2,1)}, u32[]{:S(2)}, u32[]{:S(2)}) collective-permute-start(bf16[256,4096]{1,0:T(8,128)(2,1)} %slice.10), channel_id=1, source_target_pairs={{0,1},{1,2},{2,3},{3,0},{4,5},{5,6},{6,7},{7,4},{8,9},{9,10},{10,1... | collective-permute-start | bytes 6291464 | tf_op jit(solution)/shard_map/ppermute | solution.py:199
  112.0 2.2 copy-start
  114.2 45.0 %copy-start.2 = (s32[128]{0:T(128)S(1)}, s32[128]{0:T(128)}, u32[]{:S(2)}) copy-start(s32[128]{0:T(128)} %get-tuple-element.24.rows) | copy-start | bytes 1540
  114.2 45.0 %copy-start.3 = (s32[128]{0:T(128)S(1)}, s32[128]{0:T(128)}, u32[]{:S(2)}) copy-start(s32[128]{0:T(128)} %get-tuple-element.25.slots) | copy-start | bytes 1540
  114.2 45.0 %copy-start.4 = (s32[17]{0:T(128)S(1)}, s32[17]{0:T(128)}, u32[]{:S(2)}) copy-start(s32[17]{0:T(128)} %get-tuple-element.26.first) | copy-start | bytes 208
  124.7 34.4 %collective-permute-start.2 = (f32[4,4096]{1,0:T(4,128)S(1)}, f32[4,4096]{1,0:T(4,128)S(1)}, u32[]{:S(2)}, u32[]{:S(2)}) collective-permute-start(f32[4,4096]{1,0:T(4,128)S(1)} %get-tuple-element.23), channel_id=1, source_target_pairs={{0,1},{1,2},{2,3},{3,0},{4,5},{5,6},{6,7},{7,4},{8,9},{9,10},{10,1... | collective-permute-start | bytes 196616 | tf_op jit(solution)/shard_map/ppermute | solution.py:199
  125.2 79.2 %collective-permute-start.6 = (f32[4,4096]{1,0:T(4,128)S(1)}, f32[4,4096]{1,0:T(4,128)S(1)}, u32[]{:S(2)}, u32[]{:S(2)}) collective-permute-start(f32[4,4096]{1,0:T(4,128)S(1)} %get-tuple-element.28), channel_id=1, source_target_pairs={{0,3},{1,0},{2,1},{3,2},{4,7},{5,4},{6,5},{7,6},{8,11},{9,8},{10,9... | collective-permute-start | bytes 196616 | tf_op jit(solution)/shard_map/ppermute | solution.py:199
  169.0 23.8 %all-to-all-start.3 = ((bf16[32,16,128]{2,1,0:T(8,128)(2,1)}), bf16[32,16,128]{2,1,0:T(8,128)(2,1)S(1)}, u32[]{:S(2)}, u32[]{:S(2)}) async-start(bf16[32,16,128]{2,1,0:T(8,128)(2,1)} %get-tuple-element.29), calls=%async_computation.3 | async-start | bytes 262144 | tf_op jit(solution)/shard_map/all_to_all | solution.py:202
  180.4 12.3 %collective-permute-start.5 = (f32[4,4096]{1,0:T(4,128)S(1)}, f32[4,4096]{1,0:T(4,128)S(1)}, u32[]{:S(2)}, u32[]{:S(2)}) collective-permute-start(f32[4,4096]{1,0:T(4,128)S(1)} %get-tuple-element.27), channel_id=1, source_target_pairs={{0,2},{1,3},{2,0},{3,1},{4,6},{5,7},{6,4},{7,5},{8,10},{9,11},{10,... | collective-permute-start | bytes 196616 | tf_op jit(solution)/shard_map/ppermute | solution.py:199
  180.5 2.2 copy-start.1
  192.8 21.7 %copy-start.6 = (bf16[32,16,128]{2,1,0:T(8,128)(2,1)}, bf16[32,16,128]{2,1,0:T(8,128)(2,1)S(1)}, u32[]{:S(2)}) copy-start(bf16[32,16,128]{2,1,0:T(8,128)(2,1)S(1)} %all-to-all-done.3.far) | copy-start | bytes 393220
  192.8 21.7 %all-to-all-start.2 = ((bf16[32,48,128]{2,1,0:T(8,128)(2,1)}), bf16[32,48,128]{2,1,0:T(8,128)(2,1)S(1)}, u32[]{:S(2)}, u32[]{:S(2)}) async-start(bf16[32,48,128]{2,1,0:T(8,128)(2,1)} %bitcast.6), calls=%async_computation.2 | async-start | bytes 786432 | tf_op jit(solution)/shard_map/all_to_all | solution.py:202
  214.5 0.7 copy-start.5
Sparse Core Ops, SparseCore 0:
  10.3 140.0 all-gather.1

commit v5 on v2

v5 whole, which is shorter than its diff:
```python
import functools

import jax
import jax.numpy as jnp
from jax import lax
from jax.experimental import pallas as pl
from jax.experimental.pallas import tpu as pltpu
from jax.sharding import PartitionSpec as P

D = 4096
PREFIX = 256
BLOCK = 128
GROUP = 16
SHORT = 8
BATCH = 8
PAIR = 2
TILE = 512
MIB = 2**20

SMEM = pl.BlockSpec(memory_space=pltpu.SMEM)
VMEM = pl.BlockSpec(memory_space=pltpu.VMEM)
ANY = pl.BlockSpec(memory_space=pl.ANY)


def list_kernel(order, blk_dev, n_src, n_rel, tab, lists):
    most = n_src * n_rel

    def clear(n, _):
        lists[n] = 0
        return 0

    lax.fori_loop(0, 2 * most, clear, 0)
    count = jnp.int32(0)
    for b, (local, r) in enumerate(order):
        lists[2 * most + b] = count

        def scan(i, n, local=local, r=r):
            v = tab[i * n_rel + r] - 1
            hit = (v >= 0) & (v % blk_dev == local)

            @pl.when(hit)
            def _():
                lists[n] = i * BLOCK + (v // blk_dev) * GROUP
                lists[most + n] = i

            return n + hit.astype(jnp.int32)

        count = lax.fori_loop(0, n_src, scan, count)
    lists[2 * most + len(order)] = count


def score_kernel(b0, order, most, n_rel, scale, head_scale, lists, q_ref, *refs):
    n_arrays = len(order) // PAIR
    arrays, refs = refs[:n_arrays], refs[n_arrays:]
    coarse = len(refs) > 5
    if coarse:
        prev, heads, out, best, cbuf, hsems, qbuf, abuf, sems, asems = refs
    else:
        out, qbuf, abuf, sems, asems = refs
    wide = PAIR * BLOCK
    wholes = [pltpu.make_async_copy(ref, abuf.at[k], asems.at[k]) for k, ref in enumerate(arrays)]
    if coarse:
        tops = [
            pltpu.make_async_copy(ref.at[:, pl.ds(0, PREFIX)], cbuf.at[pl.ds(k * wide, wide)], hsems.at[k])
            for k, ref in enumerate(arrays)
        ]
        for copy in tops:
            copy.start()

    def row_copy(src_row, pos):
        return pltpu.make_async_copy(
            q_ref.at[pl.ds(pl.multiple_of(src_row, GROUP), GROUP)],
            qbuf.at[pl.ds(pl.multiple_of(pos * GROUP, GROUP), GROUP)],
            sems.at[pos],
        )

    first = 2 * most + b0
    base = lists[first]
    total = lists[first + len(order)] - base

    def start(n, _):
        row_copy(lists[base + n], n).start()
        return 0

    lax.fori_loop(0, total, start, 0)
    for copy in wholes:
        copy.start()
    if coarse:
        out[...] = prev[...]
        for copy in tops:
            copy.wait()

        def tile(t, _):
            span = pl.ds(pl.multiple_of(t * TILE, TILE), TILE)
            h = heads[span, :]
            for k in range(n_arrays):
                s = lax.dot_general(
                    cbuf[k * wide : (k + 1) * wide], h, (((1,), (1,)), ((), ())), preferred_element_type=jnp.float32
                )
                top = jnp.max(s.reshape(PAIR, BLOCK, TILE), axis=1) * head_scale
                best[k * PAIR : (k + 1) * PAIR, span] = top
            return 0

        lax.fori_loop(0, heads.shape[0] // TILE, tile, 0, unroll=2)

    waited = jnp.int32(0)
    for b, (_, rel) in enumerate(order):
        if b % PAIR == 0:
            wholes[b // PAIR].wait()
        lo, hi = lists[first + b] - base, lists[first + b + 1] - base

        def step(t, waited, lo=lo, hi=hi, block=abuf.at[b // PAIR, pl.ds(b % PAIR * BLOCK, BLOCK)], rel=rel):
            at = lo + t * BATCH
            upto = jnp.minimum(at + BATCH, total)

            def wait(n, _):
                row_copy(0, n).wait()
                return 0

            lax.fori_loop(waited, upto, wait, 0)
            part = qbuf[pl.ds(pl.multiple_of(at * GROUP, GROUP), BATCH * GROUP), :]
            s = lax.dot_general(part, block[...], (((1,), (1,)), ((), ())), preferred_element_type=jnp.float32)
            s = (s * scale).astype(out.dtype)
            for m in range(BATCH):

                @pl.when(at + m < hi)
                def _():
                    out[lists[most + base + at + m] * n_rel + rel] = s[m * GROUP : (m + 1) * GROUP]

            return jnp.maximum(waited, upto)

        waited = lax.fori_loop(0, (hi - lo + BATCH - 1) // BATCH, step, waited)


def score(b0, order, arrays, lists, q, more, n_src, n_rel):
    most = n_src * len({r for _, r in order})
    passages = len(order) * BLOCK
    out_shape = [jax.ShapeDtypeStruct((n_src * n_rel, GROUP, BLOCK), jnp.bfloat16)]
    scratch = [
        pltpu.VMEM(((most + BATCH) * GROUP, D), jnp.bfloat16),
        pltpu.VMEM((len(arrays), PAIR * BLOCK, D), jnp.bfloat16),
        pltpu.SemaphoreType.DMA((most,)),
        pltpu.SemaphoreType.DMA((len(arrays),)),
    ]
    if more:
        out_shape.append(jax.ShapeDtypeStruct((len(order), q.shape[0]), jnp.float32))
        scratch = [pltpu.VMEM((passages, PREFIX), jnp.bfloat16), pltpu.SemaphoreType.DMA((len(arrays),))] + scratch
    return pl.pallas_call(
        functools.partial(score_kernel, b0, order, n_src * n_rel, n_rel, D ** (-0.5), PREFIX ** (-0.5)),
        out_shape=out_shape,
        in_specs=[SMEM, ANY] + [ANY] * len(arrays) + [VMEM] * len(more),
        out_specs=[VMEM] * len(out_shape),
        scratch_shapes=scratch,
        compiler_params=pltpu.CompilerParams(vmem_limit_bytes=36 * MIB),
        cost_estimate=pl.CostEstimate(flops=2 * passages * 64 * D, bytes_accessed=passages * D * 4, transcendentals=0),
    )(lists, q, *arrays, *more)


def coarse_part(heads, arrays):
    tops = jnp.concatenate([a[:, :PREFIX] for a in arrays], axis=0)
    s = jnp.einsum("qd,pd->qp", heads, tops, preferred_element_type=jnp.float32) * PREFIX ** (-0.5)
    return jnp.max(s.reshape(heads.shape[0], -1, BLOCK), axis=2).T


def pick_kernel(n_rel, slot, answers, out):
    for e in range(slot.shape[0]):
        g, s = e // SHORT, e % SHORT
        out[g * GROUP : (g + 1) * GROUP, s * BLOCK : (s + 1) * BLOCK] = answers[slot[e]]


def body(queries, corpus, shortlist):
    n_corpus = lax.axis_size("corpus")
    n_query = lax.axis_size("query")
    n_slots = n_corpus * n_query
    blk_dev = corpus.shape[0] // BLOCK
    j = lax.axis_index("query")

    def along(a, d):
        return lax.ppermute(a, "query", [(t, (t + d) % n_query) for t in range(n_query)])

    def exchange(a):
        return lax.all_to_all(a, "corpus", split_axis=0, concat_axis=0, tiled=True)

    q = lax.all_gather(queries, "corpus", axis=0, tiled=True)

    wanted = shortlist.reshape(-1)
    holder = wanted // blk_dev
    slot = (holder // n_query) * n_query + (holder - j) % n_query
    value = (jnp.arange(wanted.shape[0], dtype=jnp.int32) // SHORT) * blk_dev + wanted % blk_dev + 1
    ids = jnp.arange(n_slots, dtype=jnp.int32)
    tags = jnp.max(jnp.where(slot[None, :] == ids[:, None], value[None, :], 0), axis=1)
    tab = exchange(tags.reshape(n_corpus, n_query)).reshape(-1)
    order = [(l, r) for r in (0, 1, 3, 2) for l in range(blk_dev)]
    lists = pl.pallas_call(
        functools.partial(list_kernel, order, blk_dev, n_corpus, n_query),
        out_shape=jax.ShapeDtypeStruct((2 * n_slots + len(order) + 1,), jnp.int32),
        in_specs=[SMEM],
        out_specs=SMEM,
    )(tab)

    own = [corpus[: PAIR * BLOCK], corpus[PAIR * BLOCK :]]
    before = [along(a, 1) for a in own]
    after = [along(a, -1) for a in own]
    low, high, lists = lax.optimization_barrier((before[0], after[1], lists))
    across = [along(low, 1), along(high, -1)]

    early = own + after + before
    n_early = PAIR * len(early)
    (answers,) = score(0, order[:n_early], early, lists, q, [], n_corpus, n_query)
    heads = q[:, :PREFIX]
    c01 = coarse_part(heads, own + after)
    c3 = coarse_part(heads, before)
    c0, c1, c3 = c01[:blk_dev], along(c01[blk_dev:], 1), along(c3, -1)
    answers, c0, c1, c3 = lax.optimization_barrier((answers, c0, c1, c3))
    answers, c2 = score(n_early, order[n_early:], across, lists, q, [answers, heads], n_corpus, n_query)
    returned = exchange(answers.reshape(n_corpus, n_query * GROUP, BLOCK))

    back = jnp.stack([c0, c1, along(c2, 2), c3])
    back = back.reshape(n_query, blk_dev, n_corpus, BLOCK)
    coarse = jnp.stack(
        [lax.dynamic_index_in_dim(back, (j - t) % n_query, 0, keepdims=False) for t in range(n_query)], axis=2
    ).reshape(blk_dev, -1)

    rescored = pl.pallas_call(
        functools.partial(pick_kernel, n_query),
        out_shape=jax.ShapeDtypeStruct((queries.shape[0], SHORT * BLOCK), jnp.bfloat16),
        in_specs=[SMEM, VMEM],
        out_specs=VMEM,
    )(slot, returned.reshape(-1, GROUP, BLOCK))
    return (coarse, rescored)


def solution(mesh):
    spec = P(("corpus", "query"), None)
    return jax.shard_map(
        body, mesh=mesh, in_specs=(spec, spec, spec), out_specs=(spec, spec), check_vma=False
    )
```

time: 220 us -> 193 us (0.88)
  waiting for transfers between devices: 110 us -> 85.4 us
  blocking collectives: 0 us -> 16.5 us
  starting transfers between devices: 38.4 us -> 22.7 us
  Pallas kernels: 41.5 us -> 32.9 us
  matrix products: 0 us -> 6.89 us
    ppermute x15 -> x9, waiting for transfers between devices: 98.5 us -> 53.5 us  [along(): lax.ppermute(a, 'query', [(t, (t + d) % n_query) for t in range(n_query)])]
    all_gather x1, waiting for transfers between devices: 0.01 us -> 20.8 us  [body(): q = lax.all_gather(queries, 'corpus', axis=0, tiled=True)]
    all_to_all x0 -> x1, blocking collectives: none -> 16.5 us  [exchange(): return lax.all_to_all(a, 'corpus', split_axis=0, concat_axis=0, tiled=True)]
    all_to_all x2 -> x1, starting transfers between devices: 20.9 us -> 9.33 us  [exchange(): return lax.all_to_all(a, 'corpus', split_axis=0, concat_axis=0, tiled=True)]
    pallas_call x2 -> x3, Pallas kernels: 32 us -> 20.8 us  [the longest x2 18.9 us: score(): pl.pallas_call(functools.partial(score_kernel, b0, order, n_src * n_rel,...]
    slice x1 -> x9, local copies, waits for them, and re-layouts: 2.66 us -> 9.59 us  [the longest x1 4.13 us: body(): own = [corpus[:PAIR * BLOCK], corpus[PAIR * BLOCK:]]]
    dot_general x0 -> x2, matrix products: none -> 6.89 us  [coarse_part(): jnp.einsum('qd,pd->qp', heads, tops, preferred_element_type=jnp.float32)]
    unnamed x24 -> x11, local copies, waits for them, and re-layouts: 7.16 us -> 0.83 us
  transfers between devices with their start and end apart: 18 -> 11, of which waited for: 8 -> 5; matrix products, arithmetic and copies ran while one was open for 3% -> 10% of each run, Pallas kernels for 15% -> 13%
where the time goes in v5:
time: 193 us; the launch traced here: 192 us
  waiting for transfers between devices  85.4 us (44%)
  Pallas kernels  32.9 us (17%)
  starting transfers between devices  22.7 us (12%)
  blocking collectives  16.5 us (9%)
  between operations  14.2 us (7%)
  local copies, waits for them, and re-layouts  12.6 us (7%)
  matrix products  6.89 us (4%)
    ppermute x9, waiting for transfers between devices, along(): lax.ppermute(a, 'query', [(t, (t + d) % n_query) for t in range(n_query)])  53.5 us
    all_gather x1, waiting for transfers between devices, body(): q = lax.all_gather(queries, 'corpus', axis=0, tiled=True)  20.8 us
    pallas_call x2, Pallas kernels, score(): pl.pallas_call(functools.partial(score_kernel, b0, order, n_src * n_rel,...  18.9 us
    all_to_all x1, blocking collectives, exchange(): return lax.all_to_all(a, 'corpus', split_axis=0, concat_axis=0, tiled=True)  16.5 us
    ppermute x9, starting transfers between devices, along(): lax.ppermute(a, 'query', [(t, (t + d) % n_query) for t in range(n_query)])  13.4 us
    pallas_call x1, Pallas kernels, body(): pl.pallas_call(functools.partial(list_kernel, order, blk_dev, n_corpus, n...  12.2 us
    all_to_all x1, waiting for transfers between devices, exchange(): return lax.all_to_all(a, 'corpus', split_axis=0, concat_axis=0, tiled=True)  10.3 us
    all_to_all x1, starting transfers between devices, exchange(): return lax.all_to_all(a, 'corpus', split_axis=0, concat_axis=0, tiled=True)  9.33 us
  transfers between devices with their start and end apart: 11, of which 5 were waited for; matrix products, arithmetic and copies ran while one was open for 10% of the time, Pallas kernels for 13%

profile of v5, /device:TPU:1, one launch (start us, length us, event | category | flops | bytes accessed | tf_op | source)
XLA Modules:
  0.0 192.4 jit_solution(6957293013359533531)
XLA Ops:
  7.2 0.0 all-gather.2.cloned.1.call-start
  7.2 0.7 all-gather.2.cloned.1.call-update
  7.9 0.0 copy-start.2
  7.9 0.0 slice-start
  7.9 4.1 %fusion.17 = (bf16[256,4096]{1,0:T(8,128)(2,1)S(1)}, bf16[256,4096]{1,0:T(8,128)(2,1)}) fusion(bf16[512,4096]{1,0:T(8,128)(2,1)} %param.4), kind=kLoop, calls=%fused_computation.48 | loop fusion | bytes 8388608 | tf_op jit(solution)/shard_map/slice | solution.py:201
  12.1 2.1 %collective-permute-start = (bf16[256,4096]{1,0:T(8,128)(2,1)}, bf16[256,4096]{1,0:T(8,128)(2,1)}, u32[]{:S(2)}, u32[]{:S(2)}) collective-permute-start(bf16[256,4096]{1,0:T(8,128)(2,1)} %get-tuple-element.21.refs_0_), channel_id=1, source_target_pairs={{0,1},{1,2},{2,3},{3,0},{4,5},{5,6},{6,7},{7,4},{8,9},{9,10},{10,1... | collective-permute-start | bytes 6291464 | tf_op jit(solution)/shard_map/ppermute | solution.py:179
  14.2 1.4 collective-permute-start.1
  15.6 1.5 collective-permute-start.2
  17.1 0.0 collective-permute-start.3
  17.1 0.0 copy-done.2
  17.1 0.1 reshape.137
  17.2 0.0 copy-start.3
  17.2 0.1 select_reduce_fusion
  17.3 0.1 all_to_all.9
  17.4 16.5 %all_to_all.14 = s32[32,1,4]{2,1,0:T(1,128)S(1)} all-to-all(s32[32,1,4]{2,1,0:T(1,128)S(1)} %bitcast.43), channel_id=1, replica_groups=mesh['corpus'=32,'query'=4] {'corpus'}, dimensions={0} | all-to-all | bytes 1024 | tf_op jit(solution)/shard_map/all_to_all | solution.py:182
  33.9 0.5 broadcast.184
  34.4 0.7 reduce.3
  35.1 0.6 reshape.138.tab
  35.8 12.2 %shard_map.50.lists = s32[273]{0:T(512)} custom-call(s32[128]{0:T(128)} %reshape.138.tab), custom_call_target="tpu_custom_call" | custom-call | tf_op jit(solution)/shard_map/pallas_call | solution.py:194
  47.9 13.2 %collective-permute-done.refs_4_ = bf16[256,4096]{1,0:T(8,128)(2,1)} collective-permute-done((bf16[256,4096]{1,0:T(8,128)(2,1)}, bf16[256,4096]{1,0:T(8,128)(2,1)}, u32[]{:S(2)}, u32[]{:S(2)}) %collective-permute-start) | collective-permute-done | bytes 2097184 | tf_op jit(solution)/shard_map/ppermute | solution.py:179
  61.1 0.0 collective-permute-done.1.refs_3_
  61.1 0.6 collective-permute-start.6
  61.8 2.1 %collective-permute-start.7 = (bf16[256,4096]{1,0:T(8,128)(2,1)}, bf16[256,4096]{1,0:T(8,128)(2,1)}, u32[]{:S(2)}, u32[]{:S(2)}) collective-permute-start(bf16[256,4096]{1,0:T(8,128)(2,1)} %collective-permute-done.1.refs_3_), channel_id=1, source_target_pairs={{0,3},{1,0},{2,1},{3,2},{4,7},{5,4},{6,5},{7,6},{8,11},{9,8},{10,9... | collective-permute-start | bytes 6291464 | tf_op jit(solution)/shard_map/ppermute | solution.py:179
  63.8 0.9 slice.45
  64.8 0.9 slice.49
  65.7 39.7 %collective-permute-done.2.refs_2_ = bf16[256,4096]{1,0:T(8,128)(2,1)} collective-permute-done((bf16[256,4096]{1,0:T(8,128)(2,1)}, bf16[256,4096]{1,0:T(8,128)(2,1)}, u32[]{:S(2)}, u32[]{:S(2)}) %collective-permute-start.2) | collective-permute-done | bytes 2097184 | tf_op jit(solution)/shard_map/ppermute | solution.py:179
  105.4 0.9 slice.44
  106.3 0.0 collective-permute-done.3.refs_5_
  106.3 0.9 slice.50
  107.3 20.8 %all-gather.2.cloned.1.call-done.q_ref = bf16[4096,4096]{1,0:T(8,128)(2,1)} async-done(((bf16[128,4096]{1,0:T(8,128)(2,1)}), bf16[4096,4096]{1,0:T(8,128)(2,1)}) %all-gather.2.cloned.1.call-update) | async-done | bytes 33554448 | tf_op jit(solution)/shard_map/all_gather | solution.py:184
  128.1 0.0 slice-done
  128.1 4.0 %bitcast_reduce_fusion = f32[4096,8]{0,1:T(8,128)S(1)} fusion(bf16[256,256]{1,0:T(8,128)(2,1)S(1)} %slice.45, bf16[256,256]{1,0:T(8,128)(2,1)S(1)} %slice.44, bf16[512,256]{1,0:T(8,128)(2,1)S(1)} %slice-done, bf16[4096,4096]{1,0:T(8,128)(2,1)} %all-gather.2.cloned.1.call-done.q_ref), kind=kOutput, calls=%fused_computation | convolution fusion | flops 2157412352 | bytes 2752512 | tf_op jit(solution)/shard_map/qd,pd->qp/dot_general | solution.py:161
  132.1 0.0 copy-done.3
  132.1 1.3 collective-permute-start.4
  133.4 2.9 %bitcast_reduce_fusion.1 = f32[4096,4]{0,1:T(4,128)S(1)} fusion(bf16[256,256]{1,0:T(8,128)(2,1)S(1)} %slice.50, bf16[256,256]{1,0:T(8,128)(2,1)S(1)} %slice.49, bf16[4096,4096]{1,0:T(8,128)(2,1)} %all-gather.2.cloned.1.call-done.q_ref), kind=kOutput, calls=%fused_computation.2 | convolution fusion | flops 1078444032 | bytes 2424832 | tf_op jit(solution)/shard_map/qd,pd->qp/dot_general | solution.py:161
  136.3 0.0 copy-start
  136.3 1.5 collective-permute-start.5
  137.8 1.7 slice.46.refs_3_
  139.6 0.0 copy-done
  139.6 12.2 %shard_map.51.refs_2_ = bf16[128,16,128]{2,1,0:T(8,128)(2,1)S(1)} custom-call(s32[273]{0:T(512)S(1)} %copy-done, bf16[4096,4096]{1,0:T(8,128)(2,1)} %all-gather.2.cloned.1.call-done.q_ref, bf16[256,4096]{1,0:T(8,128)(2,1)} %get-tuple-element.21.refs_0_, bf16[256,4096]{1,0:T(8,128)(2,1)S(1)} %get-tuple-element.20.refs_1_, ...), custom_call_target="tpu_custom_call" | custom-call | flops 805306368 | bytes 25165824 | tf_op jit(solution)/shard_map/pallas_call | solution.py:148
  151.8 0.6 collective-permute-done.4
  152.4 0.0 collective-permute-done.5
  152.4 0.0 collective-permute-done.6.refs_0_
  152.4 0.0 collective-permute-done.7.refs_1_
  152.4 6.7 %shard_map.52 = (bf16[128,16,128]{2,1,0:T(8,128)(2,1)}, f32[4,4096]{1,0:T(4,128)S(1)}) custom-call(s32[273]{0:T(512)S(1)} %copy-done, bf16[4096,4096]{1,0:T(8,128)(2,1)} %all-gather.2.cloned.1.call-done.q_ref, bf16[256,4096]{1,0:T(8,128)(2,1)} %collective-permute-done.6.refs_0_, bf16[256,4096]{1,0:T(8,128)(2,1)} %collective-permute-done.7.refs_1_, ...), custom_call_target="tpu_custom_call" | custom-call | flops 268435456 | bytes 8388608 | tf_op jit(solution)/shard_map/pallas_call | solution.py:148
  159.2 2.8 %collective-permute-start.8 = (f32[4,4096]{1,0:T(4,128)S(1)}, f32[4,4096]{1,0:T(4,128)S(1)}, u32[]{:S(2)}, u32[]{:S(2)}) collective-permute-start(f32[4,4096]{1,0:T(4,128)S(1)} %get-tuple-element.17), channel_id=1, source_target_pairs={{0,2},{1,3},{2,0},{3,1},{4,6},{5,7},{6,4},{7,5},{8,10},{9,11},{10,... | collective-permute-start | bytes 196616 | tf_op jit(solution)/shard_map/ppermute | solution.py:179
  162.0 9.3 %all-to-all-start.1 = ((bf16[32,64,128]{2,1,0:T(8,128)(2,1)}), bf16[32,64,128]{2,1,0:T(8,128)(2,1)S(1)}, u32[]{:S(2)}, u32[]{:S(2)}) async-start(bf16[32,64,128]{2,1,0:T(8,128)(2,1)} %bitcast.11), calls=%async_computation.1 | async-start | bytes 1048576 | tf_op jit(solution)/shard_map/all_to_all | solution.py:182
  171.4 0.0 collective-permute-done.8
  171.4 0.2 pad_maximum_fusion
  171.7 0.9 reshape.141
  172.6 10.3 %all-to-all-done.1 = bf16[32,64,128]{2,1,0:T(8,128)(2,1)S(1)} async-done(((bf16[32,64,128]{2,1,0:T(8,128)(2,1)}), bf16[32,64,128]{2,1,0:T(8,128)(2,1)S(1)}, u32[]{:S(2)}, u32[]{:S(2)}) %all-to-all-start.1) | async-done | bytes 524320 | tf_op jit(solution)/shard_map/all_to_all | solution.py:182
  182.9 0.0 copy-start.1
  182.9 0.8 copy-done.1
  183.7 1.8 shard_map.53
  (7 shorter events, 0.1 us)
Async XLA Ops:
  7.2 120.9 %all-gather.2.cloned.1.call-start = ((), (), s32[]{:S(2)}) async-start(), calls=%async_computation.2 | async-start | bytes 34603008 | tf_op jit(solution)/shard_map/all_gather | solution.py:184
  7.9 9.2 %copy-start.2 = (s32[8,8]{1,0:T(8,128)S(1)}, s32[8,8]{1,0:T(8,128)}, u32[]{:S(2)}) copy-start(s32[8,8]{1,0:T(8,128)} %param.5) | copy-start | bytes 772
  7.9 120.2 %slice-start = ((bf16[512,4096]{1,0:T(8,128)(2,1)}), bf16[512,256]{1,0:T(8,128)(2,1)S(1)}, s32[]{:S(2)}) async-start(bf16[512,4096]{1,0:T(8,128)(2,1)} %param.4), calls=%async_computation.3 | async-start | bytes 524288 | tf_op jit(solution)/shard_map/slice | solution.py:160
  12.1 49.1 %collective-permute-start = (bf16[256,4096]{1,0:T(8,128)(2,1)}, bf16[256,4096]{1,0:T(8,128)(2,1)}, u32[]{:S(2)}, u32[]{:S(2)}) collective-permute-start(bf16[256,4096]{1,0:T(8,128)(2,1)} %get-tuple-element.21.refs_0_), channel_id=1, source_target_pairs={{0,1},{1,2},{2,3},{3,0},{4,5},{5,6},{6,7},{7,4},{8,9},{9,10},{10,1... | collective-permute-start | bytes 6291464 | tf_op jit(solution)/shard_map/ppermute | solution.py:179
  14.2 47.0 %collective-permute-start.1 = (bf16[256,4096]{1,0:T(8,128)(2,1)S(1)}, bf16[256,4096]{1,0:T(8,128)(2,1)}, u32[]{:S(2)}, u32[]{:S(2)}) collective-permute-start(bf16[256,4096]{1,0:T(8,128)(2,1)S(1)} %get-tuple-element.20.refs_1_), channel_id=1, source_target_pairs={{0,3},{1,0},{2,1},{3,2},{4,7},{5,4},{6,5},{7,6},{8,11},{9,8},{10,9... | collective-permute-start | bytes 6291464 | tf_op jit(solution)/shard_map/ppermute | solution.py:179
  15.6 89.8 %collective-permute-start.2 = (bf16[256,4096]{1,0:T(8,128)(2,1)}, bf16[256,4096]{1,0:T(8,128)(2,1)}, u32[]{:S(2)}, u32[]{:S(2)}) collective-permute-start(bf16[256,4096]{1,0:T(8,128)(2,1)} %get-tuple-element.21.refs_0_), channel_id=1, source_target_pairs={{0,3},{1,0},{2,1},{3,2},{4,7},{5,4},{6,5},{7,6},{8,11},{9,8},{10,9... | collective-permute-start | bytes 6291464 | tf_op jit(solution)/shard_map/ppermute | solution.py:179
  17.1 89.2 %collective-permute-start.3 = (bf16[256,4096]{1,0:T(8,128)(2,1)S(1)}, bf16[256,4096]{1,0:T(8,128)(2,1)}, u32[]{:S(2)}, u32[]{:S(2)}) collective-permute-start(bf16[256,4096]{1,0:T(8,128)(2,1)S(1)} %get-tuple-element.20.refs_1_), channel_id=1, source_target_pairs={{0,1},{1,2},{2,3},{3,0},{4,5},{5,6},{6,7},{7,4},{8,9},{9,10},{10,1... | collective-permute-start | bytes 6291464 | tf_op jit(solution)/shard_map/ppermute | solution.py:179
  17.2 114.9 %copy-start.3 = (s32[64]{0:T(128)}, s32[64]{0:T(128)S(1)}, u32[]{:S(2)}) copy-start(s32[64]{0:T(128)S(1)} %get-tuple-element.28.slot) | copy-start | bytes 772
  61.1 91.3 %collective-permute-start.6 = (bf16[256,4096]{1,0:T(8,128)(2,1)}, bf16[256,4096]{1,0:T(8,128)(2,1)}, u32[]{:S(2)}, u32[]{:S(2)}) collective-permute-start(bf16[256,4096]{1,0:T(8,128)(2,1)} %collective-permute-done.refs_4_), channel_id=1, source_target_pairs={{0,1},{1,2},{2,3},{3,0},{4,5},{5,6},{6,7},{7,4},{8,9},{9,10},{10,1... | collective-permute-start | bytes 6291464 | tf_op jit(solution)/shard_map/ppermute | solution.py:179
  61.8 90.7 %collective-permute-start.7 = (bf16[256,4096]{1,0:T(8,128)(2,1)}, bf16[256,4096]{1,0:T(8,128)(2,1)}, u32[]{:S(2)}, u32[]{:S(2)}) collective-permute-start(bf16[256,4096]{1,0:T(8,128)(2,1)} %collective-permute-done.1.refs_3_), channel_id=1, source_target_pairs={{0,3},{1,0},{2,1},{3,2},{4,7},{5,4},{6,5},{7,6},{8,11},{9,8},{10,9... | collective-permute-start | bytes 6291464 | tf_op jit(solution)/shard_map/ppermute | solution.py:179
  132.1 20.3 %collective-permute-start.4 = (f32[4,4096]{1,0:T(4,128)S(1)}, f32[4,4096]{1,0:T(4,128)S(1)}, u32[]{:S(2)}, u32[]{:S(2)}) collective-permute-start(f32[4,4096]{1,0:T(4,128)S(1)} %get-tuple-element.26), channel_id=1, source_target_pairs={{0,1},{1,2},{2,3},{3,0},{4,5},{5,6},{6,7},{7,4},{8,9},{9,10},{10,1... | collective-permute-start | bytes 196616 | tf_op jit(solution)/shard_map/ppermute | solution.py:179
  136.3 3.3 %copy-start = (s32[273]{0:T(512)S(1)}, s32[273]{0:T(512)}, u32[]{:S(2)}) copy-start(s32[273]{0:T(512)} %shard_map.50.lists) | copy-start | bytes 3280
  136.3 16.1 %collective-permute-start.5 = (f32[4,4096]{1,0:T(4,128)S(1)}, f32[4,4096]{1,0:T(4,128)S(1)}, u32[]{:S(2)}, u32[]{:S(2)}) collective-permute-start(f32[4,4096]{1,0:T(4,128)S(1)} %bitcast.44), channel_id=1, source_target_pairs={{0,3},{1,0},{2,1},{3,2},{4,7},{5,4},{6,5},{7,6},{8,11},{9,8},{10,9... | collective-permute-start | bytes 196616 | tf_op jit(solution)/shard_map/ppermute | solution.py:179
  159.2 12.2 %collective-permute-start.8 = (f32[4,4096]{1,0:T(4,128)S(1)}, f32[4,4096]{1,0:T(4,128)S(1)}, u32[]{:S(2)}, u32[]{:S(2)}) collective-permute-start(f32[4,4096]{1,0:T(4,128)S(1)} %get-tuple-element.17), channel_id=1, source_target_pairs={{0,2},{1,3},{2,0},{3,1},{4,6},{5,7},{6,4},{7,5},{8,10},{9,11},{10,... | collective-permute-start | bytes 196616 | tf_op jit(solution)/shard_map/ppermute | solution.py:179
  162.0 20.9 %all-to-all-start.1 = ((bf16[32,64,128]{2,1,0:T(8,128)(2,1)}), bf16[32,64,128]{2,1,0:T(8,128)(2,1)S(1)}, u32[]{:S(2)}, u32[]{:S(2)}) async-start(bf16[32,64,128]{2,1,0:T(8,128)(2,1)} %bitcast.11), calls=%async_computation.1 | async-start | bytes 1048576 | tf_op jit(solution)/shard_map/all_to_all | solution.py:182
  182.9 0.8 copy-start.1
Sparse Core Ops, SparseCore 0:
  10.3 117.7 all-gather.1

commit v6 on v5

--- a/solution.py
+++ b/solution.py
@@ -12,9 +12,10 @@
 BLOCK = 128
 GROUP = 16
 SHORT = 8
-BATCH = 8
+BATCH = 16
 PAIR = 2
 TILE = 512
+CUTS = 4
 MIB = 2**20
 
 SMEM = pl.BlockSpec(memory_space=pltpu.SMEM)
@@ -22,7 +23,7 @@
 ANY = pl.BlockSpec(memory_space=pl.ANY)
 
 
-def list_kernel(order, blk_dev, n_src, n_rel, tab, lists):
+def list_kernel(order, blk_dev, n_src, n_rel, tab, slot, lists):
     most = n_src * n_rel
 
     def clear(n, _):
@@ -46,7 +47,14 @@
             return n + hit.astype(jnp.int32)
 
         count = lax.fori_loop(0, n_src, scan, count)
-    lists[2 * most + len(order)] = count
+    last = 2 * most + len(order)
+    lists[last] = count
+
+    def keep(n, _):
+        lists[last + 1 + n] = slot[n]
+        return 0
+
+    lax.fori_loop(0, slot.shape[0], keep, 0)
 
 
 def score_kernel(b0, order, most, n_rel, scale, head_scale, lists, q_ref, *refs):
@@ -54,7 +62,7 @@
     arrays, refs = refs[:n_arrays], refs[n_arrays:]
     coarse = len(refs) > 5
     if coarse:
-        prev, heads, out, best, cbuf, hsems, qbuf, abuf, sems, asems = refs
+        _, heads, out, best, found, fsem, cbuf, hsems, qbuf, abuf, sems, asems = refs
     else:
         out, qbuf, abuf, sems, asems = refs
     wide = PAIR * BLOCK
@@ -86,7 +94,6 @@
     for copy in wholes:
         copy.start()
     if coarse:
-        out[...] = prev[...]
         for copy in tops:
             copy.wait()
 
@@ -104,12 +111,12 @@
         lax.fori_loop(0, heads.shape[0] // TILE, tile, 0, unroll=2)
 
     waited = jnp.int32(0)
-    for b, (_, rel) in enumerate(order):
-        if b % PAIR == 0:
-            wholes[b // PAIR].wait()
-        lo, hi = lists[first + b] - base, lists[first + b + 1] - base
-
-        def step(t, waited, lo=lo, hi=hi, block=abuf.at[b // PAIR, pl.ds(b % PAIR * BLOCK, BLOCK)], rel=rel):
+    for k in range(n_arrays):
+        wholes[k].wait()
+        lo, mid, hi = [lists[first + PAIR * k + n] - base for n in range(PAIR + 1)]
+        rel = order[PAIR * k][1]
+
+        def step(t, waited, lo=lo, mid=mid, hi=hi, pair=abuf.at[k], rel=rel):
             at = lo + t * BATCH
             upto = jnp.minimum(at + BATCH, total)
 
@@ -119,23 +126,34 @@
 
             lax.fori_loop(waited, upto, wait, 0)
             part = qbuf[pl.ds(pl.multiple_of(at * GROUP, GROUP), BATCH * GROUP), :]
-            s = lax.dot_general(part, block[...], (((1,), (1,)), ((), ())), preferred_element_type=jnp.float32)
-            s = (s * scale).astype(out.dtype)
+            s = lax.dot_general(pair[...], part, (((1,), (1,)), ((), ())), preferred_element_type=jnp.float32)
+            s = s.T * scale
             for m in range(BATCH):
 
                 @pl.when(at + m < hi)
                 def _():
-                    out[lists[most + base + at + m] * n_rel + rel] = s[m * GROUP : (m + 1) * GROUP]
+                    both = s[m * GROUP : (m + 1) * GROUP]
+                    one = jnp.where(at + m < mid, both[:, :BLOCK], both[:, BLOCK:]).astype(out.dtype)
+                    source = lists[most + base + at + m]
+                    if coarse:
+                        found[source] = one
+                    else:
+                        out[source, rel] = one
 
             return jnp.maximum(waited, upto)
 
         waited = lax.fori_loop(0, (hi - lo + BATCH - 1) // BATCH, step, waited)
+
+    if coarse:
+        put = pltpu.make_async_copy(found, out.at[:, order[0][1]], fsem)
+        put.start()
+        put.wait()
 
 
 def score(b0, order, arrays, lists, q, more, n_src, n_rel):
     most = n_src * len({r for _, r in order})
     passages = len(order) * BLOCK
-    out_shape = [jax.ShapeDtypeStruct((n_src * n_rel, GROUP, BLOCK), jnp.bfloat16)]
+    out_shape = [jax.ShapeDtypeStruct((n_src, n_rel, GROUP, BLOCK), jnp.bfloat16)]
     scratch = [
         pltpu.VMEM(((most + BATCH) * GROUP, D), jnp.bfloat16),
         pltpu.VMEM((len(arrays), PAIR * BLOCK, D), jnp.bfloat16),
@@ -144,28 +162,58 @@
     ]
     if more:
         out_shape.append(jax.ShapeDtypeStruct((len(order), q.shape[0]), jnp.float32))
-        scratch = [pltpu.VMEM((passages, PREFIX), jnp.bfloat16), pltpu.SemaphoreType.DMA((len(arrays),))] + scratch
+        scratch = [
+            pltpu.VMEM((n_src, GROUP, BLOCK), jnp.bfloat16),
+            pltpu.SemaphoreType.DMA(()),
+            pltpu.VMEM((passages, PREFIX), jnp.bfloat16),
+            pltpu.SemaphoreType.DMA((len(arrays),)),
+        ] + scratch
     return pl.pallas_call(
         functools.partial(score_kernel, b0, order, n_src * n_rel, n_rel, D ** (-0.5), PREFIX ** (-0.5)),
         out_shape=out_shape,
-        in_specs=[SMEM, ANY] + [ANY] * len(arrays) + [VMEM] * len(more),
-        out_specs=[VMEM] * len(out_shape),
+        in_specs=[SMEM, ANY] + [ANY] * len(arrays) + [ANY, VMEM][: len(more)],
+        out_specs=[ANY, VMEM] if more else [VMEM],
+        input_output_aliases={2 + len(arrays): 0} if more else {},
         scratch_shapes=scratch,
         compiler_params=pltpu.CompilerParams(vmem_limit_bytes=36 * MIB),
         cost_estimate=pl.CostEstimate(flops=2 * passages * 64 * D, bytes_accessed=passages * D * 4, transcendentals=0),
     )(lists, q, *arrays, *more)
 
 
+def cut_kernel(row, source, out, sems):
+    rows = out.shape[0] // CUTS
+    copies = [
+        pltpu.make_async_copy(source.at[pl.ds(row + k * rows, rows)], out.at[pl.ds(k * rows, rows)], sems.at[k])
+        for k in range(CUTS)
+    ]
+    for copy in copies:
+        copy.start()
+    for copy in copies:
+        copy.wait()
+
+
+def cut(source, row, rows):
+    return pl.pallas_call(
+        functools.partial(cut_kernel, row),
+        out_shape=jax.ShapeDtypeStruct((rows, source.shape[1]), source.dtype),
+        in_specs=[ANY],
+        out_specs=VMEM,
+        scratch_shapes=[pltpu.SemaphoreType.DMA((CUTS,))],
+        compiler_params=pltpu.CompilerParams(vmem_limit_bytes=8 * MIB),
+    )(source)
+
+
 def coarse_part(heads, arrays):
     tops = jnp.concatenate([a[:, :PREFIX] for a in arrays], axis=0)
     s = jnp.einsum("qd,pd->qp", heads, tops, preferred_element_type=jnp.float32) * PREFIX ** (-0.5)
     return jnp.max(s.reshape(heads.shape[0], -1, BLOCK), axis=2).T
 
 
-def pick_kernel(n_rel, slot, answers, out):
-    for e in range(slot.shape[0]):
+def pick_kernel(n_entries, lists, answers, out):
+    at = lists.shape[0] - n_entries
+    for e in range(n_entries):
         g, s = e // SHORT, e % SHORT
-        out[g * GROUP : (g + 1) * GROUP, s * BLOCK : (s + 1) * BLOCK] = answers[slot[e]]
+        out[g * GROUP : (g + 1) * GROUP, s * BLOCK : (s + 1) * BLOCK] = answers[lists[at + e]]
 
 
 def body(queries, corpus, shortlist):
@@ -193,12 +241,12 @@
     order = [(l, r) for r in (0, 1, 3, 2) for l in range(blk_dev)]
     lists = pl.pallas_call(
         functools.partial(list_kernel, order, blk_dev, n_corpus, n_query),
-        out_shape=jax.ShapeDtypeStruct((2 * n_slots + len(order) + 1,), jnp.int32),
-        in_specs=[SMEM],
+        out_shape=jax.ShapeDtypeStruct((2 * n_slots + len(order) + 1 + slot.shape[0],), jnp.int32),
+        in_specs=[SMEM, SMEM],
         out_specs=SMEM,
-    )(tab)
-
-    own = [corpus[: PAIR * BLOCK], corpus[PAIR * BLOCK :]]
+    )(tab, slot)
+
+    own = [cut(corpus, 0, PAIR * BLOCK), cut(corpus, PAIR * BLOCK, PAIR * BLOCK)]
     before = [along(a, 1) for a in own]
     after = [along(a, -1) for a in own]
     low, high, lists = lax.optimization_barrier((before[0], after[1], lists))
@@ -210,23 +258,24 @@
     heads = q[:, :PREFIX]
     c01 = coarse_part(heads, own + after)
     c3 = coarse_part(heads, before)
-    c0, c1, c3 = c01[:blk_dev], along(c01[blk_dev:], 1), along(c3, -1)
-    answers, c0, c1, c3 = lax.optimization_barrier((answers, c0, c1, c3))
+    answers, c01, c3 = lax.optimization_barrier((answers, c01, c3))
     answers, c2 = score(n_early, order[n_early:], across, lists, q, [answers, heads], n_corpus, n_query)
+    c01, c2, c3 = lax.optimization_barrier((c01, c2, c3))
+    c0, c1 = c01[:blk_dev], c01[blk_dev:]
     returned = exchange(answers.reshape(n_corpus, n_query * GROUP, BLOCK))
 
-    back = jnp.stack([c0, c1, along(c2, 2), c3])
+    back = jnp.stack([c0, along(c1, 1), along(c2, 2), along(c3, -1)])
     back = back.reshape(n_query, blk_dev, n_corpus, BLOCK)
     coarse = jnp.stack(
         [lax.dynamic_index_in_dim(back, (j - t) % n_query, 0, keepdims=False) for t in range(n_query)], axis=2
     ).reshape(blk_dev, -1)
 
     rescored = pl.pallas_call(
-        functools.partial(pick_kernel, n_query),
+        functools.partial(pick_kernel, wanted.shape[0]),
         out_shape=jax.ShapeDtypeStruct((queries.shape[0], SHORT * BLOCK), jnp.bfloat16),
         in_specs=[SMEM, VMEM],
         out_specs=VMEM,
-    )(slot, returned.reshape(-1, GROUP, BLOCK))
+    )(lists, returned.reshape(-1, GROUP, BLOCK))
     return (coarse, rescored)
 
 

time: 193 us -> 189 us (0.979)
  waiting for transfers between devices: 85.4 us -> 83.1 us
    all_to_all x1, waiting for transfers between devices: 10.3 us -> 3.41 us  [exchange(): return lax.all_to_all(a, 'corpus', split_axis=0, concat_axis=0, tiled=True)]
    ppermute x9, waiting for transfers between devices: 53.5 us -> 58.3 us  [along(): lax.ppermute(a, 'query', [(t, (t + d) % n_query) for t in range(n_query)])]
    slice x2 -> x1, local copies, waits for them, and re-layouts: 4.16 us -> 0.02 us  [body(): c0, c1 = (c01[:blk_dev], c01[blk_dev:])]
    pallas_call x2, Pallas kernels: 18.9 us -> 14.9 us  [score(): pl.pallas_call(functools.partial(score_kernel, b0, order, n_src * n_rel,...]
    unnamed x11 -> x15, local copies, waits for them, and re-layouts: 0.83 us -> 3.69 us
    all_to_all x1, starting transfers between devices: 9.33 us -> 12 us  [exchange(): return lax.all_to_all(a, 'corpus', split_axis=0, concat_axis=0, tiled=True)]
  transfers between devices with their start and end apart: 11 -> 11, of which waited for: 5 -> 10; matrix products, arithmetic and copies ran while one was open for 10% -> 9% of each run, Pallas kernels for 13% -> 13%
where the time goes in v6:
time: 189 us
  waiting for transfers between devices  83.1 us (44%)
  Pallas kernels  31.1 us (16%)
  starting transfers between devices  23.8 us (13%)
  blocking collectives  16.5 us (9%)
  between operations  14.3 us (8%)
  local copies, waits for them, and re-layouts  12.3 us (7%)
  matrix products  6.89 us (4%)
    ppermute x9, waiting for transfers between devices, along(): lax.ppermute(a, 'query', [(t, (t + d) % n_query) for t in range(n_query)])  58.3 us
    all_gather x1, waiting for transfers between devices, body(): q = lax.all_gather(queries, 'corpus', axis=0, tiled=True)  20.7 us
    all_to_all x1, blocking collectives, exchange(): return lax.all_to_all(a, 'corpus', split_axis=0, concat_axis=0, tiled=True)  16.5 us
    pallas_call x2, Pallas kernels, score(): pl.pallas_call(functools.partial(score_kernel, b0, order, n_src * n_rel,...  14.9 us
    pallas_call x1, Pallas kernels, body(): pl.pallas_call(functools.partial(list_kernel, order, blk_dev, n_corpus, n...  12.6 us
    all_to_all x1, starting transfers between devices, exchange(): return lax.all_to_all(a, 'corpus', split_axis=0, concat_axis=0, tiled=True)  12 us
    ppermute x9, starting transfers between devices, along(): lax.ppermute(a, 'query', [(t, (t + d) % n_query) for t in range(n_query)])  11.8 us
    dot_general x2, matrix products, coarse_part(): jnp.einsum('qd,pd->qp', heads, tops, preferred_element_type=jnp.float32)  6.89 us
  transfers between devices with their start and end apart: 11, of which 10 were waited for; matrix products, arithmetic and copies ran while one was open for 9% of the time, Pallas kernels for 13%

profile of v6, /device:TPU:1, one launch (start us, length us, event | category | flops | bytes accessed | tf_op | source)
XLA Modules:
  0.0 189.0 jit_solution(15774582823117621461)
XLA Ops:
  7.2 0.0 all-gather.2.cloned.1.call-start
  7.2 0.7 all-gather.2.cloned.1.call-update
  7.9 0.0 copy-start
  7.9 2.2 %copy-done = bf16[512,4096]{1,0:T(8,128)(2,1)S(1)} copy-done((bf16[512,4096]{1,0:T(8,128)(2,1)S(1)}, bf16[512,4096]{1,0:T(8,128)(2,1)}, u32[]{:S(2)}) %copy-start) | copy-done | bytes 4194328
  10.1 0.2 shard_map.50.refs_0_
  10.3 0.0 copy-start.4
  10.3 2.2 %collective-permute-start = (bf16[256,4096]{1,0:T(8,128)(2,1)S(1)}, bf16[256,4096]{1,0:T(8,128)(2,1)}, u32[]{:S(2)}, u32[]{:S(2)}) collective-permute-start(bf16[256,4096]{1,0:T(8,128)(2,1)S(1)} %shard_map.50.refs_0_), channel_id=1, source_target_pairs={{0,1},{1,2},{2,3},{3,0},{4,5},{5,6},{6,7},{7,4},{8,9},{9,10},{10,1... | collective-permute-start | bytes 6291464 | tf_op jit(solution)/shard_map/ppermute | solution.py:227
  12.5 1.6 shard_map.51.refs_1_
  14.1 1.5 collective-permute-start.1
  15.6 1.4 collective-permute-start.2
  17.0 0.0 collective-permute-start.3
  17.1 0.0 copy-done.4
  17.1 0.1 reshape.137
  17.2 0.0 copy-start.5
  17.2 0.1 select_reduce_fusion
  17.3 0.1 all_to_all.9
  17.4 16.5 %all_to_all.14 = s32[32,1,4]{2,1,0:T(1,128)S(1)} all-to-all(s32[32,1,4]{2,1,0:T(1,128)S(1)} %bitcast.43), channel_id=1, replica_groups=mesh['corpus'=32,'query'=4] {'corpus'}, dimensions={0} | all-to-all | bytes 1024 | tf_op jit(solution)/shard_map/all_to_all | solution.py:230
  33.9 0.5 broadcast.184
  34.4 0.7 reduce.3
  35.1 0.6 reshape.138.tab
  35.7 0.0 copy-done.5
  35.7 12.6 %shard_map.52.lists = s32[337]{0:T(512)} custom-call(s32[128]{0:T(128)} %reshape.138.tab, s32[64]{0:T(128)} %copy-done.5), custom_call_target="tpu_custom_call" | custom-call | tf_op jit(solution)/shard_map/pallas_call | solution.py:242
  48.3 10.9 %collective-permute-done.refs_4_ = bf16[256,4096]{1,0:T(8,128)(2,1)} collective-permute-done((bf16[256,4096]{1,0:T(8,128)(2,1)S(1)}, bf16[256,4096]{1,0:T(8,128)(2,1)}, u32[]{:S(2)}, u32[]{:S(2)}) %collective-permute-start) | collective-permute-done | bytes 2097184 | tf_op jit(solution)/shard_map/ppermute | solution.py:227
  59.2 1.4 collective-permute-done.1.refs_3_
  60.6 1.3 collective-permute-start.4
  61.9 1.6 collective-permute-start.5
  63.5 1.0 slice.37
  64.6 0.9 slice.39
  65.5 0.9 slice.41
  66.4 39.1 %collective-permute-done.2.refs_2_ = bf16[256,4096]{1,0:T(8,128)(2,1)} collective-permute-done((bf16[256,4096]{1,0:T(8,128)(2,1)S(1)}, bf16[256,4096]{1,0:T(8,128)(2,1)}, u32[]{:S(2)}, u32[]{:S(2)}) %collective-permute-start.2) | collective-permute-done | bytes 2097184 | tf_op jit(solution)/shard_map/ppermute | solution.py:227
  105.6 0.9 slice.38
  106.5 0.0 collective-permute-done.3.refs_5_
  106.5 0.9 slice.42
  107.4 20.7 %all-gather.2.cloned.1.call-done.q_ref = bf16[4096,4096]{1,0:T(8,128)(2,1)} async-done(((bf16[128,4096]{1,0:T(8,128)(2,1)}), bf16[4096,4096]{1,0:T(8,128)(2,1)}) %all-gather.2.cloned.1.call-update) | async-done | bytes 33554448 | tf_op jit(solution)/shard_map/all_gather | solution.py:232
  128.1 0.0 copy-start.1
  128.1 0.7 copy-done.1
  128.7 9.5 %shard_map.53.refs_2_ = bf16[32,4,16,128]{3,2,1,0:T(8,128)(2,1)} custom-call(s32[337]{0:T(512)S(1)} %copy-done.1, bf16[4096,4096]{1,0:T(8,128)(2,1)} %all-gather.2.cloned.1.call-done.q_ref, bf16[256,4096]{1,0:T(8,128)(2,1)S(1)} %shard_map.50.refs_0_, bf16[256,4096]{1,0:T(8,128)(2,1)} %shard_map.51.refs_1_, bf16[256,4096]{1,0:T(8,128)(2,1)} %collective-permute-done.2.refs_2_, ...), custom_call_target="tpu_custom_call" | custom-call | flops 805306368 | bytes 25165824 | tf_op jit(solution)/shard_map/pallas_call | solution.py:171
  138.2 2.9 %bitcast_reduce_fusion.1 = f32[4096,4]{0,1:T(4,128)S(1)} fusion(bf16[256,256]{1,0:T(8,128)(2,1)S(1)} %slice.42, bf16[256,256]{1,0:T(8,128)(2,1)S(1)} %slice.41, bf16[4096,4096]{1,0:T(8,128)(2,1)} %all-gather.2.cloned.1.call-done.q_ref), kind=kOutput, calls=%fused_computation.2 | convolution fusion | flops 1078444032 | bytes 2424832 | tf_op jit(solution)/shard_map/qd,pd->qp/dot_general | solution.py:208
  141.1 4.0 %bitcast_reduce_fusion = f32[4096,8]{0,1:T(8,128)S(1)} fusion(bf16[256,256]{1,0:T(8,128)(2,1)S(1)} %slice.39, bf16[256,256]{1,0:T(8,128)(2,1)S(1)} %slice.38, bf16[256,256]{1,0:T(8,128)(2,1)S(1)} %slice.37, bf16[256,256]{1,0:T(8,128)(2,1)S(1)} %slice.36, bf16[4096,4096]{1,0:T(8,128)(2,1)} %all-gather.2.cloned.1.call-done.q_ref), kind=kOutput, calls=%fused_computation | convolution fusion | flops 2157936640 | bytes 2752512 | tf_op jit(solution)/shard_map/qd,pd->qp/dot_general | solution.py:208
  145.1 0.0 copy-start.2
  145.1 1.7 slice.40.refs_3_
  146.9 2.3 %collective-permute-done.4.refs_0_ = bf16[256,4096]{1,0:T(8,128)(2,1)} collective-permute-done((bf16[256,4096]{1,0:T(8,128)(2,1)}, bf16[256,4096]{1,0:T(8,128)(2,1)}, u32[]{:S(2)}, u32[]{:S(2)}) %collective-permute-start.4) | collective-permute-done | bytes 2097184 | tf_op jit(solution)/shard_map/ppermute | solution.py:227
  149.1 1.4 collective-permute-done.5.refs_1_
  150.5 0.0 copy-done.2
  150.5 5.4 %shard_map.54 = (bf16[32,4,16,128]{3,2,1,0:T(8,128)(2,1)}, f32[4,4096]{1,0:T(4,128)S(1)}) custom-call(s32[337]{0:T(512)S(1)} %copy-done.2, bf16[4096,4096]{1,0:T(8,128)(2,1)} %all-gather.2.cloned.1.call-done.q_ref, bf16[256,4096]{1,0:T(8,128)(2,1)} %collective-permute-done.4.refs_0_, ...), custom_call_target="tpu_custom_call", output_to_operand_aliasing={{0}: (4, {})} | custom-call | flops 268435456 | bytes 8388608 | tf_op jit(solution)/shard_map/pallas_call | solution.py:171
  155.9 12.0 %all-to-all-start.1 = ((bf16[32,64,128]{2,1,0:T(8,128)(2,1)}), bf16[32,64,128]{2,1,0:T(8,128)(2,1)S(1)}, u32[]{:S(2)}, u32[]{:S(2)}) async-start(bf16[32,64,128]{2,1,0:T(8,128)(2,1)} %bitcast.11), calls=%async_computation.1 | async-start | bytes 1048576 | tf_op jit(solution)/shard_map/all_to_all | solution.py:230
  168.0 1.0 collective-permute-start.6
  169.0 2.5 %collective-permute-start.7 = (f32[4,4096]{1,0:T(4,128)S(1)}, f32[4,4096]{1,0:T(4,128)S(1)}, u32[]{:S(2)}, u32[]{:S(2)}) collective-permute-start(f32[4,4096]{1,0:T(4,128)S(1)} %get-tuple-element.21), channel_id=1, source_target_pairs={{0,2},{1,3},{2,0},{3,1},{4,6},{5,7},{6,4},{7,5},{8,10},{9,11},{10,... | collective-permute-start | bytes 196616 | tf_op jit(solution)/shard_map/ppermute | solution.py:227
  171.5 0.2 collective-permute-start.8
  171.7 1.0 collective-permute-done.6
  172.8 2.1 %collective-permute-done.7 = f32[4,4096]{1,0:T(4,128)S(1)} collective-permute-done((f32[4,4096]{1,0:T(4,128)S(1)}, f32[4,4096]{1,0:T(4,128)S(1)}, u32[]{:S(2)}, u32[]{:S(2)}) %collective-permute-start.7) | collective-permute-done | bytes 65568 | tf_op jit(solution)/shard_map/ppermute | solution.py:227
  174.9 0.1 collective-permute-done.8
  175.0 0.2 pad_maximum_fusion
  175.2 0.9 reshape.141
  176.1 3.4 %all-to-all-done.1 = bf16[32,64,128]{2,1,0:T(8,128)(2,1)S(1)} async-done(((bf16[32,64,128]{2,1,0:T(8,128)(2,1)}), bf16[32,64,128]{2,1,0:T(8,128)(2,1)S(1)}, u32[]{:S(2)}, u32[]{:S(2)}) %all-to-all-start.1) | async-done | bytes 524320 | tf_op jit(solution)/shard_map/all_to_all | solution.py:230
  179.5 0.0 copy-start.3
  179.5 0.8 copy-done.3
  180.3 1.8 shard_map.55
  (8 shorter events, 0.1 us)
Async XLA Ops:
  7.2 120.9 %all-gather.2.cloned.1.call-start = ((), (), s32[]{:S(2)}) async-start(), calls=%async_computation.2 | async-start | bytes 34603008 | tf_op jit(solution)/shard_map/all_gather | solution.py:232
  7.9 2.2 %copy-start = (bf16[512,4096]{1,0:T(8,128)(2,1)S(1)}, bf16[512,4096]{1,0:T(8,128)(2,1)}, u32[]{:S(2)}) copy-start(bf16[512,4096]{1,0:T(8,128)(2,1)} %source.3) | copy-start | bytes 12582916
  10.3 6.8 %copy-start.4 = (s32[8,8]{1,0:T(8,128)S(1)}, s32[8,8]{1,0:T(8,128)}, u32[]{:S(2)}) copy-start(s32[8,8]{1,0:T(8,128)} %param.5) | copy-start | bytes 772
  10.3 48.9 %collective-permute-start = (bf16[256,4096]{1,0:T(8,128)(2,1)S(1)}, bf16[256,4096]{1,0:T(8,128)(2,1)}, u32[]{:S(2)}, u32[]{:S(2)}) collective-permute-start(bf16[256,4096]{1,0:T(8,128)(2,1)S(1)} %shard_map.50.refs_0_), channel_id=1, source_target_pairs={{0,1},{1,2},{2,3},{3,0},{4,5},{5,6},{6,7},{7,4},{8,9},{9,10},{10,1... | collective-permute-start | bytes 6291464 | tf_op jit(solution)/shard_map/ppermute | solution.py:227
  14.1 46.6 %collective-permute-start.1 = (bf16[256,4096]{1,0:T(8,128)(2,1)}, bf16[256,4096]{1,0:T(8,128)(2,1)}, u32[]{:S(2)}, u32[]{:S(2)}) collective-permute-start(bf16[256,4096]{1,0:T(8,128)(2,1)} %shard_map.51.refs_1_), channel_id=1, source_target_pairs={{0,3},{1,0},{2,1},{3,2},{4,7},{5,4},{6,5},{7,6},{8,11},{9,8},{10,9... | collective-permute-start | bytes 6291464 | tf_op jit(solution)/shard_map/ppermute | solution.py:227
  15.6 90.0 %collective-permute-start.2 = (bf16[256,4096]{1,0:T(8,128)(2,1)S(1)}, bf16[256,4096]{1,0:T(8,128)(2,1)}, u32[]{:S(2)}, u32[]{:S(2)}) collective-permute-start(bf16[256,4096]{1,0:T(8,128)(2,1)S(1)} %shard_map.50.refs_0_), channel_id=1, source_target_pairs={{0,3},{1,0},{2,1},{3,2},{4,7},{5,4},{6,5},{7,6},{8,11},{9,8},{10,9... | collective-permute-start | bytes 6291464 | tf_op jit(solution)/shard_map/ppermute | solution.py:227
  17.0 89.5 %collective-permute-start.3 = (bf16[256,4096]{1,0:T(8,128)(2,1)}, bf16[256,4096]{1,0:T(8,128)(2,1)}, u32[]{:S(2)}, u32[]{:S(2)}) collective-permute-start(bf16[256,4096]{1,0:T(8,128)(2,1)} %shard_map.51.refs_1_), channel_id=1, source_target_pairs={{0,1},{1,2},{2,3},{3,0},{4,5},{5,6},{6,7},{7,4},{8,9},{9,10},{10,1... | collective-permute-start | bytes 6291464 | tf_op jit(solution)/shard_map/ppermute | solution.py:227
  17.2 18.5 %copy-start.5 = (s32[64]{0:T(128)}, s32[64]{0:T(128)S(1)}, u32[]{:S(2)}) copy-start(s32[64]{0:T(128)S(1)} %get-tuple-element.30.slot) | copy-start | bytes 772
  60.6 88.5 %collective-permute-start.4 = (bf16[256,4096]{1,0:T(8,128)(2,1)}, bf16[256,4096]{1,0:T(8,128)(2,1)}, u32[]{:S(2)}, u32[]{:S(2)}) collective-permute-start(bf16[256,4096]{1,0:T(8,128)(2,1)} %collective-permute-done.refs_4_), channel_id=1, source_target_pairs={{0,1},{1,2},{2,3},{3,0},{4,5},{5,6},{6,7},{7,4},{8,9},{9,10},{10,1... | collective-permute-start | bytes 6291464 | tf_op jit(solution)/shard_map/ppermute | solution.py:227
  61.9 88.6 %collective-permute-start.5 = (bf16[256,4096]{1,0:T(8,128)(2,1)}, bf16[256,4096]{1,0:T(8,128)(2,1)}, u32[]{:S(2)}, u32[]{:S(2)}) collective-permute-start(bf16[256,4096]{1,0:T(8,128)(2,1)} %collective-permute-done.1.refs_3_), channel_id=1, source_target_pairs={{0,3},{1,0},{2,1},{3,2},{4,7},{5,4},{6,5},{7,6},{8,11},{9,8},{10,9... | collective-permute-start | bytes 6291464 | tf_op jit(solution)/shard_map/ppermute | solution.py:227
  128.1 0.7 copy-start.1
  145.1 5.4 %copy-start.2 = (s32[337]{0:T(512)S(1)}, s32[337]{0:T(512)}, u32[]{:S(2)}) copy-start(s32[337]{0:T(512)} %shard_map.52.lists) | copy-start | bytes 4048
  155.9 23.6 %all-to-all-start.1 = ((bf16[32,64,128]{2,1,0:T(8,128)(2,1)}), bf16[32,64,128]{2,1,0:T(8,128)(2,1)S(1)}, u32[]{:S(2)}, u32[]{:S(2)}) async-start(bf16[32,64,128]{2,1,0:T(8,128)(2,1)} %bitcast.11), calls=%async_computation.1 | async-start | bytes 1048576 | tf_op jit(solution)/shard_map/all_to_all | solution.py:230
  168.0 4.7 %collective-permute-start.6 = (f32[4,4096]{1,0:T(4,128)S(1)}, f32[4,4096]{1,0:T(4,128)S(1)}, u32[]{:S(2)}, u32[]{:S(2)}) collective-permute-start(f32[4,4096]{1,0:T(4,128)S(1)} %get-tuple-element.28), channel_id=1, source_target_pairs={{0,1},{1,2},{2,3},{3,0},{4,5},{5,6},{6,7},{7,4},{8,9},{9,10},{10,1... | collective-permute-start | bytes 196616 | tf_op jit(solution)/shard_map/ppermute | solution.py:227
  169.0 5.9 %collective-permute-start.7 = (f32[4,4096]{1,0:T(4,128)S(1)}, f32[4,4096]{1,0:T(4,128)S(1)}, u32[]{:S(2)}, u32[]{:S(2)}) collective-permute-start(f32[4,4096]{1,0:T(4,128)S(1)} %get-tuple-element.21), channel_id=1, source_target_pairs={{0,2},{1,3},{2,0},{3,1},{4,6},{5,7},{6,4},{7,5},{8,10},{9,11},{10,... | collective-permute-start | bytes 196616 | tf_op jit(solution)/shard_map/ppermute | solution.py:227
  171.5 3.5 %collective-permute-start.8 = (f32[4,4096]{1,0:T(4,128)S(1)}, f32[4,4096]{1,0:T(4,128)S(1)}, u32[]{:S(2)}, u32[]{:S(2)}) collective-permute-start(f32[4,4096]{1,0:T(4,128)S(1)} %bitcast.44), channel_id=1, source_target_pairs={{0,3},{1,0},{2,1},{3,2},{4,7},{5,4},{6,5},{7,6},{8,11},{9,8},{10,9... | collective-permute-start | bytes 196616 | tf_op jit(solution)/shard_map/ppermute | solution.py:227
  179.5 0.8 copy-start.3
Sparse Core Ops, SparseCore 0:
  10.3 117.7 all-gather.1

commit v7 on v6

--- a/solution.py
+++ b/solution.py
@@ -180,10 +180,14 @@
     )(lists, q, *arrays, *more)
 
 
-def cut_kernel(row, source, out, sems):
-    rows = out.shape[0] // CUTS
+def cut_kernel(source, *refs):
+    outs, sems = refs[:PAIR], refs[PAIR]
+    rows = outs[0].shape[0] // CUTS
     copies = [
-        pltpu.make_async_copy(source.at[pl.ds(row + k * rows, rows)], out.at[pl.ds(k * rows, rows)], sems.at[k])
+        pltpu.make_async_copy(
+            source.at[pl.ds((n * CUTS + k) * rows, rows)], out.at[pl.ds(k * rows, rows)], sems.at[n * CUTS + k]
+        )
+        for n, out in enumerate(outs)
         for k in range(CUTS)
     ]
     for copy in copies:
@@ -192,14 +196,15 @@
         copy.wait()
 
 
-def cut(source, row, rows):
+def cut(source):
+    half = jax.ShapeDtypeStruct((source.shape[0] // PAIR, source.shape[1]), source.dtype)
     return pl.pallas_call(
-        functools.partial(cut_kernel, row),
-        out_shape=jax.ShapeDtypeStruct((rows, source.shape[1]), source.dtype),
+        cut_kernel,
+        out_shape=[half] * PAIR,
         in_specs=[ANY],
-        out_specs=VMEM,
-        scratch_shapes=[pltpu.SemaphoreType.DMA((CUTS,))],
-        compiler_params=pltpu.CompilerParams(vmem_limit_bytes=8 * MIB),
+        out_specs=[VMEM] * PAIR,
+        scratch_shapes=[pltpu.SemaphoreType.DMA((PAIR * CUTS,))],
+        compiler_params=pltpu.CompilerParams(vmem_limit_bytes=55 * MIB),
     )(source)
 
 
@@ -246,7 +251,7 @@
         out_specs=SMEM,
     )(tab, slot)
 
-    own = [cut(corpus, 0, PAIR * BLOCK), cut(corpus, PAIR * BLOCK, PAIR * BLOCK)]
+    own = list(cut(corpus))
     before = [along(a, 1) for a in own]
     after = [along(a, -1) for a in own]
     low, high, lists = lax.optimization_barrier((before[0], after[1], lists))

time: 189 us -> 190 us (level)
  Pallas kernels: 31.1 us -> 37 us
  waiting for transfers between devices: 83.1 us -> 78.3 us
  starting transfers between devices: 23.8 us -> 21.7 us
    ppermute x9, waiting for transfers between devices: 58.3 us -> 53.8 us  [along(): lax.ppermute(a, 'query', [(t, (t + d) % n_query) for t in range(n_query)])]
    pallas_call x2, Pallas kernels: 14.9 us -> 18.4 us  [score(): pl.pallas_call(functools.partial(score_kernel, b0, order, n_src * n_rel,...]
    all_to_all x1, starting transfers between devices: 12 us -> 8.94 us  [exchange(): return lax.all_to_all(a, 'corpus', split_axis=0, concat_axis=0, tiled=True)]
    pallas_call x2 -> x1, Pallas kernels: 1.74 us -> 4.22 us  [cut(): pl.pallas_call(cut_kernel, out_shape=[half] * PAIR, in_specs=[ANY], out_s...]
  transfers between devices with their start and end apart: 11 -> 11, of which waited for: 10 -> 6; matrix products, arithmetic and copies ran while one was open for 9% -> 9% of each run, Pallas kernels for 13% -> 15%
where the time goes in v7:
time: 190 us; the launch traced here: 189 us
  waiting for transfers between devices  78.3 us (41%)
  Pallas kernels  37 us (19%)
  starting transfers between devices  21.7 us (11%)
  blocking collectives  16.4 us (9%)
  between operations  14.3 us (8%)
  local copies, waits for them, and re-layouts  13.2 us (7%)
  matrix products  6.9 us (4%)
    ppermute x9, waiting for transfers between devices, along(): lax.ppermute(a, 'query', [(t, (t + d) % n_query) for t in range(n_query)])  53.8 us
    all_gather x1, waiting for transfers between devices, body(): q = lax.all_gather(queries, 'corpus', axis=0, tiled=True)  20.4 us
    pallas_call x2, Pallas kernels, score(): pl.pallas_call(functools.partial(score_kernel, b0, order, n_src * n_rel,...  18.4 us
    all_to_all x1, blocking collectives, exchange(): return lax.all_to_all(a, 'corpus', split_axis=0, concat_axis=0, tiled=True)  16.4 us
    ppermute x9, starting transfers between devices, along(): lax.ppermute(a, 'query', [(t, (t + d) % n_query) for t in range(n_query)])  12.7 us
    pallas_call x1, Pallas kernels, body(): pl.pallas_call(functools.partial(list_kernel, order, blk_dev, n_corpus, n...  12.6 us
    all_to_all x1, starting transfers between devices, exchange(): return lax.all_to_all(a, 'corpus', split_axis=0, concat_axis=0, tiled=True)  8.94 us
    dot_general x2, matrix products, coarse_part(): jnp.einsum('qd,pd->qp', heads, tops, preferred_element_type=jnp.float32)  6.9 us
  transfers between devices with their start and end apart: 11, of which 6 were waited for; matrix products, arithmetic and copies ran while one was open for 9% of the time, Pallas kernels for 15%

profile of v7, /device:TPU:1, one launch (start us, length us, event | category | flops | bytes accessed | tf_op | source)
XLA Modules:
  0.0 189.0 jit_solution(3743187169830200847)
XLA Ops:
  7.2 0.0 all-gather.2.cloned.1.call-start
  7.2 0.7 all-gather.2.cloned.1.call-update
  7.9 0.0 copy-start.4
  7.9 4.2 %shard_map.50 = (bf16[256,4096]{1,0:T(8,128)(2,1)}, bf16[256,4096]{1,0:T(8,128)(2,1)}) custom-call(bf16[512,4096]{1,0:T(8,128)(2,1)} %source.1), custom_call_target="tpu_custom_call" | custom-call | tf_op jit(solution)/shard_map/pallas_call | solution.py:201
  12.1 2.2 %collective-permute-start = (bf16[256,4096]{1,0:T(8,128)(2,1)}, bf16[256,4096]{1,0:T(8,128)(2,1)S(1)}, u32[]{:S(2)}, u32[]{:S(2)}) collective-permute-start(bf16[256,4096]{1,0:T(8,128)(2,1)} %get-tuple-element.15.refs_0_), channel_id=1, source_target_pairs={{0,1},{1,2},{2,3},{3,0},{4,5},{5,6},{6,7},{7,4},{8,9},{9,10},{10,1... | collective-permute-start | bytes 6291464 | tf_op jit(solution)/shard_map/ppermute | solution.py:232
  14.3 1.5 collective-permute-start.1
  15.8 1.4 collective-permute-start.2
  17.2 0.1 collective-permute-start.3
  17.3 0.0 copy-done.4
  17.3 0.1 reshape.137
  17.4 0.0 copy-start.5
  17.4 0.1 select_reduce_fusion
  17.5 0.1 all_to_all.9
  17.6 16.4 %all_to_all.14 = s32[32,1,4]{2,1,0:T(1,128)S(1)} all-to-all(s32[32,1,4]{2,1,0:T(1,128)S(1)} %bitcast.43), channel_id=1, replica_groups=mesh['corpus'=32,'query'=4] {'corpus'}, dimensions={0} | all-to-all | bytes 1024 | tf_op jit(solution)/shard_map/all_to_all | solution.py:235
  34.1 0.5 broadcast.184
  34.6 0.7 reduce.3
  35.3 0.6 reshape.138.tab
  35.9 0.0 copy-done.5
  35.9 12.6 %shard_map.51.lists = s32[337]{0:T(512)} custom-call(s32[128]{0:T(128)} %reshape.138.tab, s32[64]{0:T(128)} %copy-done.5), custom_call_target="tpu_custom_call" | custom-call | tf_op jit(solution)/shard_map/pallas_call | solution.py:247
  48.5 12.8 %collective-permute-done.refs_4_ = bf16[256,4096]{1,0:T(8,128)(2,1)S(1)} collective-permute-done((bf16[256,4096]{1,0:T(8,128)(2,1)}, bf16[256,4096]{1,0:T(8,128)(2,1)S(1)}, u32[]{:S(2)}, u32[]{:S(2)}) %collective-permute-start) | collective-permute-done | bytes 2097184 | tf_op jit(solution)/shard_map/ppermute | solution.py:232
  61.3 0.0 collective-permute-done.1.refs_3_
  61.3 0.8 collective-permute-start.4
  62.1 1.8 collective-permute-start.5
  64.0 0.9 slice.27
  64.9 0.9 slice.28
  65.9 0.9 slice.37
  66.8 38.9 %collective-permute-done.2.refs_2_ = bf16[256,4096]{1,0:T(8,128)(2,1)} collective-permute-done((bf16[256,4096]{1,0:T(8,128)(2,1)}, bf16[256,4096]{1,0:T(8,128)(2,1)}, u32[]{:S(2)}, u32[]{:S(2)}) %collective-permute-start.2) | collective-permute-done | bytes 2097184 | tf_op jit(solution)/shard_map/ppermute | solution.py:232
  105.8 0.9 slice.36
  106.7 0.0 collective-permute-done.3.refs_5_
  106.7 0.9 slice.40
  107.6 20.4 %all-gather.2.cloned.1.call-done.q_ref = bf16[4096,4096]{1,0:T(8,128)(2,1)} async-done(((bf16[128,4096]{1,0:T(8,128)(2,1)}), bf16[4096,4096]{1,0:T(8,128)(2,1)}) %all-gather.2.cloned.1.call-update) | async-done | bytes 33554448 | tf_op jit(solution)/shard_map/all_gather | solution.py:237
  128.1 0.0 copy-start
  128.1 1.6 copy-done
  129.7 0.0 copy-start.1
  129.7 1.6 copy-done.1
  131.2 0.0 copy-start.2
  131.2 0.7 copy-done.2
  131.9 10.7 %shard_map.52.refs_2_ = bf16[32,4,16,128]{3,2,1,0:T(8,128)(2,1)} custom-call(s32[337]{0:T(512)S(1)} %copy-done.2, bf16[4096,4096]{1,0:T(8,128)(2,1)} %all-gather.2.cloned.1.call-done.q_ref, bf16[256,4096]{1,0:T(8,128)(2,1)S(1)} %copy-done, bf16[256,4096]{1,0:T(8,128)(2,1)S(1)} %copy-done.1, bf16[256,4096]{1,0:T(8,128)(2,1)} %collective-permute-done.2.refs_2_, ...), custom_call_target="tpu_custom_call" | custom-call | flops 805306368 | bytes 25165824 | tf_op jit(solution)/shard_map/pallas_call | solution.py:171
  142.6 2.9 %bitcast_reduce_fusion.1 = f32[4096,4]{0,1:T(4,128)S(1)} fusion(bf16[256,256]{1,0:T(8,128)(2,1)S(1)} %slice.40, bf16[256,256]{1,0:T(8,128)(2,1)S(1)} %slice.39, bf16[4096,4096]{1,0:T(8,128)(2,1)} %all-gather.2.cloned.1.call-done.q_ref), kind=kOutput, calls=%fused_computation.2 | convolution fusion | flops 1078444032 | bytes 2424832 | tf_op jit(solution)/shard_map/qd,pd->qp/dot_general | solution.py:213
  145.6 4.0 %bitcast_reduce_fusion = f32[4096,8]{0,1:T(8,128)S(1)} fusion(bf16[256,256]{1,0:T(8,128)(2,1)S(1)} %slice.37, bf16[256,256]{1,0:T(8,128)(2,1)S(1)} %slice.36, bf16[256,256]{1,0:T(8,128)(2,1)S(1)} %slice.28, bf16[256,256]{1,0:T(8,128)(2,1)S(1)} %slice.27, bf16[4096,4096]{1,0:T(8,128)(2,1)} %all-gather.2.cloned.1.call-done.q_ref), kind=kOutput, calls=%fused_computation | convolution fusion | flops 2157936640 | bytes 2752512 | tf_op jit(solution)/shard_map/qd,pd->qp/dot_general | solution.py:213
  149.6 1.7 slice.38.refs_3_
  151.3 0.0 collective-permute-done.4.refs_0_
  151.3 0.0 collective-permute-done.5.refs_1_
  151.3 7.7 %shard_map.53 = (bf16[32,4,16,128]{3,2,1,0:T(8,128)(2,1)}, f32[4,4096]{1,0:T(4,128)S(1)}) custom-call(s32[337]{0:T(512)S(1)} %copy-done.2, bf16[4096,4096]{1,0:T(8,128)(2,1)} %all-gather.2.cloned.1.call-done.q_ref, bf16[256,4096]{1,0:T(8,128)(2,1)} %collective-permute-done.4.refs_0_, ...), custom_call_target="tpu_custom_call", output_to_operand_aliasing={{0}: (4, {})} | custom-call | flops 268435456 | bytes 8388608 | tf_op jit(solution)/shard_map/pallas_call | solution.py:171
  159.0 8.9 %all-to-all-start.1 = ((bf16[32,64,128]{2,1,0:T(8,128)(2,1)}), bf16[32,64,128]{2,1,0:T(8,128)(2,1)S(1)}, u32[]{:S(2)}, u32[]{:S(2)}) async-start(bf16[32,64,128]{2,1,0:T(8,128)(2,1)} %bitcast.11), calls=%async_computation.1 | async-start | bytes 1048576 | tf_op jit(solution)/shard_map/all_to_all | solution.py:235
  168.0 1.6 collective-permute-start.6
  169.6 1.5 collective-permute-start.7
  171.1 1.8 collective-permute-start.8
  172.8 0.0 collective-permute-done.6
  172.9 1.7 collective-permute-done.7
  174.5 0.4 collective-permute-done.8
  174.9 0.2 pad_maximum_fusion
  175.2 0.9 reshape.141
  176.1 3.4 %all-to-all-done.1 = bf16[32,64,128]{2,1,0:T(8,128)(2,1)S(1)} async-done(((bf16[32,64,128]{2,1,0:T(8,128)(2,1)}), bf16[32,64,128]{2,1,0:T(8,128)(2,1)S(1)}, u32[]{:S(2)}, u32[]{:S(2)}) %all-to-all-start.1) | async-done | bytes 524320 | tf_op jit(solution)/shard_map/all_to_all | solution.py:235
  179.5 0.0 copy-start.3
  179.5 0.8 copy-done.3
  180.3 1.8 shard_map.54
  (8 shorter events, 0.1 us)
Async XLA Ops:
  7.2 120.9 %all-gather.2.cloned.1.call-start = ((), (), s32[]{:S(2)}) async-start(), calls=%async_computation.2 | async-start | bytes 34603008 | tf_op jit(solution)/shard_map/all_gather | solution.py:237
  7.9 9.4 %copy-start.4 = (s32[8,8]{1,0:T(8,128)S(1)}, s32[8,8]{1,0:T(8,128)}, u32[]{:S(2)}) copy-start(s32[8,8]{1,0:T(8,128)} %param.5) | copy-start | bytes 772
  12.1 49.2 %collective-permute-start = (bf16[256,4096]{1,0:T(8,128)(2,1)}, bf16[256,4096]{1,0:T(8,128)(2,1)S(1)}, u32[]{:S(2)}, u32[]{:S(2)}) collective-permute-start(bf16[256,4096]{1,0:T(8,128)(2,1)} %get-tuple-element.15.refs_0_), channel_id=1, source_target_pairs={{0,1},{1,2},{2,3},{3,0},{4,5},{5,6},{6,7},{7,4},{8,9},{9,10},{10,1... | collective-permute-start | bytes 6291464 | tf_op jit(solution)/shard_map/ppermute | solution.py:232
  14.3 47.0 %collective-permute-start.1 = (bf16[256,4096]{1,0:T(8,128)(2,1)}, bf16[256,4096]{1,0:T(8,128)(2,1)}, u32[]{:S(2)}, u32[]{:S(2)}) collective-permute-start(bf16[256,4096]{1,0:T(8,128)(2,1)} %get-tuple-element.16.refs_1_), channel_id=1, source_target_pairs={{0,3},{1,0},{2,1},{3,2},{4,7},{5,4},{6,5},{7,6},{8,11},{9,8},{10,9... | collective-permute-start | bytes 6291464 | tf_op jit(solution)/shard_map/ppermute | solution.py:232
  15.8 89.9 %collective-permute-start.2 = (bf16[256,4096]{1,0:T(8,128)(2,1)}, bf16[256,4096]{1,0:T(8,128)(2,1)}, u32[]{:S(2)}, u32[]{:S(2)}) collective-permute-start(bf16[256,4096]{1,0:T(8,128)(2,1)} %get-tuple-element.15.refs_0_), channel_id=1, source_target_pairs={{0,3},{1,0},{2,1},{3,2},{4,7},{5,4},{6,5},{7,6},{8,11},{9,8},{10,9... | collective-permute-start | bytes 6291464 | tf_op jit(solution)/shard_map/ppermute | solution.py:232
  17.2 89.5 %collective-permute-start.3 = (bf16[256,4096]{1,0:T(8,128)(2,1)}, bf16[256,4096]{1,0:T(8,128)(2,1)}, u32[]{:S(2)}, u32[]{:S(2)}) collective-permute-start(bf16[256,4096]{1,0:T(8,128)(2,1)} %get-tuple-element.16.refs_1_), channel_id=1, source_target_pairs={{0,1},{1,2},{2,3},{3,0},{4,5},{5,6},{6,7},{7,4},{8,9},{9,10},{10,1... | collective-permute-start | bytes 6291464 | tf_op jit(solution)/shard_map/ppermute | solution.py:232
  17.4 18.5 %copy-start.5 = (s32[64]{0:T(128)}, s32[64]{0:T(128)S(1)}, u32[]{:S(2)}) copy-start(s32[64]{0:T(128)S(1)} %get-tuple-element.34.slot) | copy-start | bytes 772
  61.3 90.0 %collective-permute-start.4 = (bf16[256,4096]{1,0:T(8,128)(2,1)S(1)}, bf16[256,4096]{1,0:T(8,128)(2,1)}, u32[]{:S(2)}, u32[]{:S(2)}) collective-permute-start(bf16[256,4096]{1,0:T(8,128)(2,1)S(1)} %collective-permute-done.refs_4_), channel_id=1, source_target_pairs={{0,1},{1,2},{2,3},{3,0},{4,5},{5,6},{6,7},{7,4},{8,9},{9,10},{10,1... | collective-permute-start | bytes 6291464 | tf_op jit(solution)/shard_map/ppermute | solution.py:232
  62.1 89.2 %collective-permute-start.5 = (bf16[256,4096]{1,0:T(8,128)(2,1)}, bf16[256,4096]{1,0:T(8,128)(2,1)}, u32[]{:S(2)}, u32[]{:S(2)}) collective-permute-start(bf16[256,4096]{1,0:T(8,128)(2,1)} %collective-permute-done.1.refs_3_), channel_id=1, source_target_pairs={{0,3},{1,0},{2,1},{3,2},{4,7},{5,4},{6,5},{7,6},{8,11},{9,8},{10,9... | collective-permute-start | bytes 6291464 | tf_op jit(solution)/shard_map/ppermute | solution.py:232
  128.1 1.6 copy-start
  129.7 1.6 copy-start.1
  131.2 0.7 copy-start.2
  159.0 20.5 %all-to-all-start.1 = ((bf16[32,64,128]{2,1,0:T(8,128)(2,1)}), bf16[32,64,128]{2,1,0:T(8,128)(2,1)S(1)}, u32[]{:S(2)}, u32[]{:S(2)}) async-start(bf16[32,64,128]{2,1,0:T(8,128)(2,1)} %bitcast.11), calls=%async_computation.1 | async-start | bytes 1048576 | tf_op jit(solution)/shard_map/all_to_all | solution.py:235
  168.0 4.9 %collective-permute-start.6 = (f32[4,4096]{1,0:T(4,128)S(1)}, f32[4,4096]{1,0:T(4,128)S(1)}, u32[]{:S(2)}, u32[]{:S(2)}) collective-permute-start(f32[4,4096]{1,0:T(4,128)S(1)} %get-tuple-element.32), channel_id=1, source_target_pairs={{0,1},{1,2},{2,3},{3,0},{4,5},{5,6},{6,7},{7,4},{8,9},{9,10},{10,1... | collective-permute-start | bytes 196616 | tf_op jit(solution)/shard_map/ppermute | solution.py:232
  169.6 4.9 %collective-permute-start.7 = (f32[4,4096]{1,0:T(4,128)S(1)}, f32[4,4096]{1,0:T(4,128)S(1)}, u32[]{:S(2)}, u32[]{:S(2)}) collective-permute-start(f32[4,4096]{1,0:T(4,128)S(1)} %get-tuple-element.25), channel_id=1, source_target_pairs={{0,2},{1,3},{2,0},{3,1},{4,6},{5,7},{6,4},{7,5},{8,10},{9,11},{10,... | collective-permute-start | bytes 196616 | tf_op jit(solution)/shard_map/ppermute | solution.py:232
  171.1 3.9 %collective-permute-start.8 = (f32[4,4096]{1,0:T(4,128)S(1)}, f32[4,4096]{1,0:T(4,128)S(1)}, u32[]{:S(2)}, u32[]{:S(2)}) collective-permute-start(f32[4,4096]{1,0:T(4,128)S(1)} %bitcast.44), channel_id=1, source_target_pairs={{0,3},{1,0},{2,1},{3,2},{4,7},{5,4},{6,5},{7,6},{8,11},{9,8},{10,9... | collective-permute-start | bytes 196616 | tf_op jit(solution)/shard_map/ppermute | solution.py:232
  179.5 0.8 copy-start.3
Sparse Core Ops, SparseCore 0:
  10.3 117.7 all-gather.1

commit v8 on v7

--- a/solution.py
+++ b/solution.py
@@ -260,7 +260,7 @@
     early = own + after + before
     n_early = PAIR * len(early)
     (answers,) = score(0, order[:n_early], early, lists, q, [], n_corpus, n_query)
-    heads = q[:, :PREFIX]
+    answers, heads = lax.optimization_barrier((answers, q[:, :PREFIX]))
     c01 = coarse_part(heads, own + after)
     c3 = coarse_part(heads, before)
     answers, c01, c3 = lax.optimization_barrier((answers, c01, c3))

time: 190 us -> 194 us (1.021)
  waiting for transfers between devices: 78.3 us -> 91 us
  matrix products: 6.9 us -> 3.71 us
  Pallas kernels: 37 us -> 34 us
  local copies, waits for them, and re-layouts: 13.2 us -> 10.5 us
    all_to_all x1, waiting for transfers between devices: 3.41 us -> 10.3 us  [exchange(): return lax.all_to_all(a, 'corpus', split_axis=0, concat_axis=0, tiled=True)]
    ppermute x9, waiting for transfers between devices: 53.8 us -> 59.6 us  [along(): lax.ppermute(a, 'query', [(t, (t + d) % n_query) for t in range(n_query)])]
    dot_general x2, matrix products: 6.9 us -> 3.71 us  [coarse_part(): jnp.einsum('qd,pd->qp', heads, tops, preferred_element_type=jnp.float32)]
    pallas_call x2, Pallas kernels: 18.4 us -> 15.4 us  [score(): pl.pallas_call(functools.partial(score_kernel, b0, order, n_src * n_rel,...]
    unnamed x15, local copies, waits for them, and re-layouts: 4.68 us -> 1.81 us
  transfers between devices with their start and end apart: 11 -> 11, of which waited for: 6 -> 5; matrix products, arithmetic and copies ran while one was open for 9% -> 7% of each run, Pallas kernels for 15% -> 13%
where the time goes in v8:
time: 194 us
  waiting for transfers between devices  91 us (47%)
  Pallas kernels  34 us (18%)
  starting transfers between devices  22.6 us (12%)
  blocking collectives  16.4 us (8%)
  between operations  14.3 us (7%)
  local copies, waits for them, and re-layouts  10.5 us (5%)
  matrix products  3.71 us (2%)
    ppermute x9, waiting for transfers between devices, along(): lax.ppermute(a, 'query', [(t, (t + d) % n_query) for t in range(n_query)])  59.6 us
    all_gather x1, waiting for transfers between devices, body(): q = lax.all_gather(queries, 'corpus', axis=0, tiled=True)  20.4 us
    all_to_all x1, blocking collectives, exchange(): return lax.all_to_all(a, 'corpus', split_axis=0, concat_axis=0, tiled=True)  16.4 us
    pallas_call x2, Pallas kernels, score(): pl.pallas_call(functools.partial(score_kernel, b0, order, n_src * n_rel,...  15.4 us
    pallas_call x1, Pallas kernels, body(): pl.pallas_call(functools.partial(list_kernel, order, blk_dev, n_corpus, n...  12.6 us
    ppermute x9, starting transfers between devices, along(): lax.ppermute(a, 'query', [(t, (t + d) % n_query) for t in range(n_query)])  11.8 us
    all_to_all x1, starting transfers between devices, exchange(): return lax.all_to_all(a, 'corpus', split_axis=0, concat_axis=0, tiled=True)  10.7 us
    all_to_all x1, waiting for transfers between devices, exchange(): return lax.all_to_all(a, 'corpus', split_axis=0, concat_axis=0, tiled=True)  10.3 us
  transfers between devices with their start and end apart: 11, of which 5 were waited for; matrix products, arithmetic and copies ran while one was open for 7% of the time, Pallas kernels for 13%

profile of v8, /device:TPU:1, one launch (start us, length us, event | category | flops | bytes accessed | tf_op | source)
XLA Modules:
  0.0 193.7 jit_solution(14150103612396840935)
XLA Ops:
  7.2 0.0 all-gather.2.cloned.1.call-start
  7.2 0.7 all-gather.2.cloned.1.call-update
  7.9 0.0 copy-start.4
  7.9 4.2 %shard_map.50 = (bf16[256,4096]{1,0:T(8,128)(2,1)}, bf16[256,4096]{1,0:T(8,128)(2,1)}) custom-call(bf16[512,4096]{1,0:T(8,128)(2,1)} %source.1), custom_call_target="tpu_custom_call" | custom-call | tf_op jit(solution)/shard_map/pallas_call | solution.py:201
  12.1 2.2 %collective-permute-start = (bf16[256,4096]{1,0:T(8,128)(2,1)}, bf16[256,4096]{1,0:T(8,128)(2,1)S(1)}, u32[]{:S(2)}, u32[]{:S(2)}) collective-permute-start(bf16[256,4096]{1,0:T(8,128)(2,1)} %get-tuple-element.17.refs_0_), channel_id=1, source_target_pairs={{0,1},{1,2},{2,3},{3,0},{4,5},{5,6},{6,7},{7,4},{8,9},{9,10},{10,1... | collective-permute-start | bytes 6291464 | tf_op jit(solution)/shard_map/ppermute | solution.py:232
  14.3 1.5 collective-permute-start.1
  15.8 1.4 collective-permute-start.2
  17.2 0.1 collective-permute-start.3
  17.3 0.0 copy-done.4
  17.3 0.1 reshape.137
  17.4 0.0 copy-start.5
  17.4 0.1 select_reduce_fusion
  17.5 0.1 all_to_all.9
  17.6 16.4 %all_to_all.14 = s32[32,1,4]{2,1,0:T(1,128)S(1)} all-to-all(s32[32,1,4]{2,1,0:T(1,128)S(1)} %bitcast.41), channel_id=1, replica_groups=mesh['corpus'=32,'query'=4] {'corpus'}, dimensions={0} | all-to-all | bytes 1024 | tf_op jit(solution)/shard_map/all_to_all | solution.py:235
  34.1 0.5 broadcast.180
  34.6 0.7 reduce.3
  35.3 0.6 reshape.138.tab
  35.9 0.0 copy-done.5
  35.9 12.6 %shard_map.51.lists = s32[337]{0:T(512)} custom-call(s32[128]{0:T(128)} %reshape.138.tab, s32[64]{0:T(128)} %copy-done.5), custom_call_target="tpu_custom_call" | custom-call | tf_op jit(solution)/shard_map/pallas_call | solution.py:247
  48.5 12.8 %collective-permute-done.refs_4_ = bf16[256,4096]{1,0:T(8,128)(2,1)S(1)} collective-permute-done((bf16[256,4096]{1,0:T(8,128)(2,1)}, bf16[256,4096]{1,0:T(8,128)(2,1)S(1)}, u32[]{:S(2)}, u32[]{:S(2)}) %collective-permute-start) | collective-permute-done | bytes 2097184 | tf_op jit(solution)/shard_map/ppermute | solution.py:232
  61.3 0.0 collective-permute-done.1.refs_3_
  61.3 0.8 collective-permute-start.4
  62.1 1.8 collective-permute-start.5
  64.0 0.9 slice.29
  64.9 0.9 slice.28
  65.9 0.9 slice.38
  66.8 38.9 %collective-permute-done.2.refs_2_ = bf16[256,4096]{1,0:T(8,128)(2,1)} collective-permute-done((bf16[256,4096]{1,0:T(8,128)(2,1)}, bf16[256,4096]{1,0:T(8,128)(2,1)}, u32[]{:S(2)}, u32[]{:S(2)}) %collective-permute-start.2) | collective-permute-done | bytes 2097184 | tf_op jit(solution)/shard_map/ppermute | solution.py:232
  105.8 0.9 slice.37
  106.7 0.0 collective-permute-done.3.refs_5_
  106.7 0.0 copy-start.2
  106.7 0.9 slice.40
  107.6 20.4 %all-gather.2.cloned.1.call-done.q_ref = bf16[4096,4096]{1,0:T(8,128)(2,1)} async-done(((bf16[128,4096]{1,0:T(8,128)(2,1)}), bf16[4096,4096]{1,0:T(8,128)(2,1)}) %all-gather.2.cloned.1.call-update) | async-done | bytes 33554448 | tf_op jit(solution)/shard_map/all_gather | solution.py:237
  128.1 0.0 copy-start
  128.1 0.0 copy-start.1
  128.1 1.9 slice.36.refs_3_
  129.9 0.0 copy-done.2
  130.0 0.3 copy-done
  130.3 0.6 copy-done.1
  130.9 8.6 %shard_map.52.refs_2_ = bf16[32,4,16,128]{3,2,1,0:T(8,128)(2,1)} custom-call(s32[337]{0:T(512)S(1)} %copy-done.2, bf16[4096,4096]{1,0:T(8,128)(2,1)} %all-gather.2.cloned.1.call-done.q_ref, bf16[256,4096]{1,0:T(8,128)(2,1)S(1)} %copy-done, bf16[256,4096]{1,0:T(8,128)(2,1)S(1)} %copy-done.1, bf16[256,4096]{1,0:T(8,128)(2,1)} %collective-permute-done.2.refs_2_, ...), custom_call_target="tpu_custom_call" | custom-call | flops 805306368 | bytes 25165824 | tf_op jit(solution)/shard_map/pallas_call | solution.py:171
  139.6 1.3 bitcast_reduce_fusion.1
  140.9 2.4 %bitcast_reduce_fusion = f32[4096,8]{0,1:T(8,128)S(1)} fusion(bf16[4096,256]{1,0:T(8,128)(2,1)S(1)} %slice.36.refs_3_, bf16[256,256]{1,0:T(8,128)(2,1)S(1)} %slice.38, bf16[256,256]{1,0:T(8,128)(2,1)S(1)} %slice.37, bf16[256,256]{1,0:T(8,128)(2,1)S(1)} %slice.29, bf16[256,256]{1,0:T(8,128)(2,1)S(1)} %slice.28), kind=kOutput, calls=%fused_computation | convolution fusion | flops 2157936640 | bytes 2752512 | tf_op jit(solution)/shard_map/qd,pd->qp/dot_general | solution.py:213
  143.3 7.9 %collective-permute-done.4.refs_0_ = bf16[256,4096]{1,0:T(8,128)(2,1)} collective-permute-done((bf16[256,4096]{1,0:T(8,128)(2,1)S(1)}, bf16[256,4096]{1,0:T(8,128)(2,1)}, u32[]{:S(2)}, u32[]{:S(2)}) %collective-permute-start.4) | collective-permute-done | bytes 2097184 | tf_op jit(solution)/shard_map/ppermute | solution.py:232
  151.2 0.0 collective-permute-done.5.refs_1_
  151.2 6.7 %shard_map.53 = (bf16[32,4,16,128]{3,2,1,0:T(8,128)(2,1)}, f32[4,4096]{1,0:T(4,128)S(1)}) custom-call(s32[337]{0:T(512)S(1)} %copy-done.2, bf16[4096,4096]{1,0:T(8,128)(2,1)} %all-gather.2.cloned.1.call-done.q_ref, bf16[256,4096]{1,0:T(8,128)(2,1)} %collective-permute-done.4.refs_0_, ...), custom_call_target="tpu_custom_call", output_to_operand_aliasing={{0}: (4, {})} | custom-call | flops 268435456 | bytes 8388608 | tf_op jit(solution)/shard_map/pallas_call | solution.py:171
  157.9 0.6 collective-permute-start.6
  158.5 1.4 collective-permute-start.7
  159.9 2.0 %collective-permute-start.8 = (f32[4,4096]{1,0:T(4,128)S(1)}, f32[4,4096]{1,0:T(4,128)S(1)}, u32[]{:S(2)}, u32[]{:S(2)}) collective-permute-start(f32[4,4096]{1,0:T(4,128)S(1)} %bitcast.42), channel_id=1, source_target_pairs={{0,3},{1,0},{2,1},{3,2},{4,7},{5,4},{6,5},{7,6},{8,11},{9,8},{10,9... | collective-permute-start | bytes 196616 | tf_op jit(solution)/shard_map/ppermute | solution.py:232
  161.9 10.7 %all-to-all-start.1 = ((bf16[32,64,128]{2,1,0:T(8,128)(2,1)}), bf16[32,64,128]{2,1,0:T(8,128)(2,1)S(1)}, u32[]{:S(2)}, u32[]{:S(2)}) async-start(bf16[32,64,128]{2,1,0:T(8,128)(2,1)} %bitcast.9), calls=%async_computation.1 | async-start | bytes 1048576 | tf_op jit(solution)/shard_map/all_to_all | solution.py:235
  172.6 0.0 collective-permute-done.6
  172.7 0.0 collective-permute-done.7
  172.7 0.0 collective-permute-done.8
  172.8 0.2 pad_maximum_fusion
  173.0 0.9 reshape.141
  173.9 10.3 %all-to-all-done.1 = bf16[32,64,128]{2,1,0:T(8,128)(2,1)S(1)} async-done(((bf16[32,64,128]{2,1,0:T(8,128)(2,1)}), bf16[32,64,128]{2,1,0:T(8,128)(2,1)S(1)}, u32[]{:S(2)}, u32[]{:S(2)}) %all-to-all-start.1) | async-done | bytes 524320 | tf_op jit(solution)/shard_map/all_to_all | solution.py:235
  184.2 0.0 copy-start.3
  184.2 0.8 copy-done.3
  185.0 1.8 shard_map.54
  (8 shorter events, 0.1 us)
Async XLA Ops:
  7.2 120.9 %all-gather.2.cloned.1.call-start = ((), (), s32[]{:S(2)}) async-start(), calls=%async_computation.2 | async-start | bytes 34603008 | tf_op jit(solution)/shard_map/all_gather | solution.py:237
  7.9 9.4 %copy-start.4 = (s32[8,8]{1,0:T(8,128)S(1)}, s32[8,8]{1,0:T(8,128)}, u32[]{:S(2)}) copy-start(s32[8,8]{1,0:T(8,128)} %param.5) | copy-start | bytes 772
  12.1 49.2 %collective-permute-start = (bf16[256,4096]{1,0:T(8,128)(2,1)}, bf16[256,4096]{1,0:T(8,128)(2,1)S(1)}, u32[]{:S(2)}, u32[]{:S(2)}) collective-permute-start(bf16[256,4096]{1,0:T(8,128)(2,1)} %get-tuple-element.17.refs_0_), channel_id=1, source_target_pairs={{0,1},{1,2},{2,3},{3,0},{4,5},{5,6},{6,7},{7,4},{8,9},{9,10},{10,1... | collective-permute-start | bytes 6291464 | tf_op jit(solution)/shard_map/ppermute | solution.py:232
  14.3 47.0 %collective-permute-start.1 = (bf16[256,4096]{1,0:T(8,128)(2,1)}, bf16[256,4096]{1,0:T(8,128)(2,1)}, u32[]{:S(2)}, u32[]{:S(2)}) collective-permute-start(bf16[256,4096]{1,0:T(8,128)(2,1)} %get-tuple-element.18.refs_1_), channel_id=1, source_target_pairs={{0,3},{1,0},{2,1},{3,2},{4,7},{5,4},{6,5},{7,6},{8,11},{9,8},{10,9... | collective-permute-start | bytes 6291464 | tf_op jit(solution)/shard_map/ppermute | solution.py:232
  15.8 89.9 %collective-permute-start.2 = (bf16[256,4096]{1,0:T(8,128)(2,1)}, bf16[256,4096]{1,0:T(8,128)(2,1)}, u32[]{:S(2)}, u32[]{:S(2)}) collective-permute-start(bf16[256,4096]{1,0:T(8,128)(2,1)} %get-tuple-element.17.refs_0_), channel_id=1, source_target_pairs={{0,3},{1,0},{2,1},{3,2},{4,7},{5,4},{6,5},{7,6},{8,11},{9,8},{10,9... | collective-permute-start | bytes 6291464 | tf_op jit(solution)/shard_map/ppermute | solution.py:232
  17.2 89.5 %collective-permute-start.3 = (bf16[256,4096]{1,0:T(8,128)(2,1)}, bf16[256,4096]{1,0:T(8,128)(2,1)}, u32[]{:S(2)}, u32[]{:S(2)}) collective-permute-start(bf16[256,4096]{1,0:T(8,128)(2,1)} %get-tuple-element.18.refs_1_), channel_id=1, source_target_pairs={{0,1},{1,2},{2,3},{3,0},{4,5},{5,6},{6,7},{7,4},{8,9},{9,10},{10,1... | collective-permute-start | bytes 6291464 | tf_op jit(solution)/shard_map/ppermute | solution.py:232
  17.4 18.5 %copy-start.5 = (s32[64]{0:T(128)}, s32[64]{0:T(128)S(1)}, u32[]{:S(2)}) copy-start(s32[64]{0:T(128)S(1)} %get-tuple-element.38.slot) | copy-start | bytes 772
  61.3 89.9 %collective-permute-start.4 = (bf16[256,4096]{1,0:T(8,128)(2,1)S(1)}, bf16[256,4096]{1,0:T(8,128)(2,1)}, u32[]{:S(2)}, u32[]{:S(2)}) collective-permute-start(bf16[256,4096]{1,0:T(8,128)(2,1)S(1)} %collective-permute-done.refs_4_), channel_id=1, source_target_pairs={{0,1},{1,2},{2,3},{3,0},{4,5},{5,6},{6,7},{7,4},{8,9},{9,10},{10,1... | collective-permute-start | bytes 6291464 | tf_op jit(solution)/shard_map/ppermute | solution.py:232
  62.1 89.0 %collective-permute-start.5 = (bf16[256,4096]{1,0:T(8,128)(2,1)}, bf16[256,4096]{1,0:T(8,128)(2,1)}, u32[]{:S(2)}, u32[]{:S(2)}) collective-permute-start(bf16[256,4096]{1,0:T(8,128)(2,1)} %collective-permute-done.1.refs_3_), channel_id=1, source_target_pairs={{0,3},{1,0},{2,1},{3,2},{4,7},{5,4},{6,5},{7,6},{8,11},{9,8},{10,9... | collective-permute-start | bytes 6291464 | tf_op jit(solution)/shard_map/ppermute | solution.py:232
  106.7 23.3 %copy-start.2 = (s32[337]{0:T(512)S(1)}, s32[337]{0:T(512)}, u32[]{:S(2)}) copy-start(s32[337]{0:T(512)} %shard_map.51.lists) | copy-start | bytes 4048
  128.1 2.2 %copy-start = (bf16[256,4096]{1,0:T(8,128)(2,1)S(1)}, bf16[256,4096]{1,0:T(8,128)(2,1)}, u32[]{:S(2)}) copy-start(bf16[256,4096]{1,0:T(8,128)(2,1)} %get-tuple-element.17.refs_0_) | copy-start | bytes 6291460
  128.1 2.9 %copy-start.1 = (bf16[256,4096]{1,0:T(8,128)(2,1)S(1)}, bf16[256,4096]{1,0:T(8,128)(2,1)}, u32[]{:S(2)}) copy-start(bf16[256,4096]{1,0:T(8,128)(2,1)} %get-tuple-element.18.refs_1_) | copy-start | bytes 6291460
  157.9 14.7 %collective-permute-start.6 = (f32[4,4096]{1,0:T(4,128)S(1)}, f32[4,4096]{1,0:T(4,128)S(1)}, u32[]{:S(2)}, u32[]{:S(2)}) collective-permute-start(f32[4,4096]{1,0:T(4,128)S(1)} %get-tuple-element.36), channel_id=1, source_target_pairs={{0,1},{1,2},{2,3},{3,0},{4,5},{5,6},{6,7},{7,4},{8,9},{9,10},{10,1... | collective-permute-start | bytes 196616 | tf_op jit(solution)/shard_map/ppermute | solution.py:232
  158.5 14.2 %collective-permute-start.7 = (f32[4,4096]{1,0:T(4,128)S(1)}, f32[4,4096]{1,0:T(4,128)S(1)}, u32[]{:S(2)}, u32[]{:S(2)}) collective-permute-start(f32[4,4096]{1,0:T(4,128)S(1)} %get-tuple-element.29), channel_id=1, source_target_pairs={{0,2},{1,3},{2,0},{3,1},{4,6},{5,7},{6,4},{7,5},{8,10},{9,11},{10,... | collective-permute-start | bytes 196616 | tf_op jit(solution)/shard_map/ppermute | solution.py:232
  159.9 12.8 %collective-permute-start.8 = (f32[4,4096]{1,0:T(4,128)S(1)}, f32[4,4096]{1,0:T(4,128)S(1)}, u32[]{:S(2)}, u32[]{:S(2)}) collective-permute-start(f32[4,4096]{1,0:T(4,128)S(1)} %bitcast.42), channel_id=1, source_target_pairs={{0,3},{1,0},{2,1},{3,2},{4,7},{5,4},{6,5},{7,6},{8,11},{9,8},{10,9... | collective-permute-start | bytes 196616 | tf_op jit(solution)/shard_map/ppermute | solution.py:232
  161.9 22.3 %all-to-all-start.1 = ((bf16[32,64,128]{2,1,0:T(8,128)(2,1)}), bf16[32,64,128]{2,1,0:T(8,128)(2,1)S(1)}, u32[]{:S(2)}, u32[]{:S(2)}) async-start(bf16[32,64,128]{2,1,0:T(8,128)(2,1)} %bitcast.9), calls=%async_computation.1 | async-start | bytes 1048576 | tf_op jit(solution)/shard_map/all_to_all | solution.py:235
  184.2 0.8 copy-start.3
Sparse Core Ops, SparseCore 0:
  10.3 117.7 all-gather.1
